TPU v7x, 128 devices: a whole 4x4x4 slice. The times are simulated.
128 devices in a mesh: gx: 8 (over z, core), gy: 16 (over x, y).
Axes of the slice: x: 4, y: 4, z: 4, core: 2. Of those that a mesh axis runs over, the one named last changes fastest.
Arguments:
- prior_draws: bfloat16 [8, 16, 512, 256], P('gx', 'gy'), may hold values from -8 to 8
- cond_factors: bfloat16 [4, 8, 16, 8, 512, 512], P(None, 'gx', 'gy'), may hold values from -0.0625 to 0.0625
- chol_factors: bfloat16 [4, 8, 16, 512, 512], P(None, 'gx', 'gy'), may hold values from -0.25 to 0.25
- noise: bfloat16 [4, 8, 16, 512, 256], P(None, 'gx', 'gy'), may hold values from -6 to 6
- neighbours: int32 [4, 8, 16, 8], P(None, 'gx', 'gy'), may hold values from 0 to 639
- block_slot: int32 [640], replicated, may hold values from 0 to 639, as said below
Outputs:
- samples: bfloat16 [4, 8, 16, 512, 256], P(None, 'gx', 'gy')
Inputs may be any that keep to these rules, and one draw needn't show every extreme that they name: `block_slot`: A permutation of 0 to 639.
All inputs are finite; a program needn't handle non-finite values.
Results may differ from a plain program's by a relative error of at most 0.0045.
Values may be sent and summed in bfloat16 or wider, within the bound.
No kernel may reach another device: no remote copies, remote signals or barrier semaphores. Data moves between devices by JAX's collectives and lax.ppermute only.
A program may use at most 128 MiB of HBM per device.

v0:
```python
import jax
import jax.numpy as jnp
from jax import lax
from jax.sharding import PartitionSpec as P


def body(prior_draws, cond_factors, chol_factors, noise, neighbours, block_slot):
    count_x = lax.axis_size("gx")
    count_y = lax.axis_size("gy")
    devices = count_x * count_y
    my_row = lax.axis_index("gx")
    levels = cond_factors.shape[0]
    sources = block_slot[neighbours[:, 0, 0, :]] % devices
    source_row = sources // count_y
    source_col = sources % count_y
    previous = prior_draws[0, 0]
    results = []
    for level in range(levels):
        in_row = source_row[level] == my_row
        select_row = (
            (source_col[level][:, None] == jnp.arange(count_y, dtype=jnp.int32)[None, :])
            & in_row[:, None]
        ).astype(jnp.bfloat16)
        select_col = (
            (source_row[level][:, None] == jnp.arange(count_x, dtype=jnp.int32)[None, :])
            & jnp.logical_not(in_row)[:, None]
        ).astype(jnp.bfloat16)
        own = jnp.dot(
            chol_factors[level, 0, 0], noise[level, 0, 0], preferred_element_type=jnp.float32
        )
        row_draws = lax.all_gather(previous[None], "gy", axis=0, tiled=True)
        col_draws = lax.all_gather(previous[None], "gx", axis=0, tiled=True)
        picked = jnp.einsum(
            "kj,jbr->kbr", select_row, row_draws, preferred_element_type=jnp.float32
        )
        picked = picked + jnp.einsum(
            "kj,jbr->kbr", select_col, col_draws, preferred_element_type=jnp.float32
        )
        picked = picked.astype(jnp.bfloat16)
        mean = jnp.einsum(
            "kbc,kcr->br", cond_factors[level, 0, 0], picked, preferred_element_type=jnp.float32
        )
        previous = (mean + own).astype(jnp.bfloat16)
        results.append(previous)
    return jnp.stack(results)[:, None, None]


def solution(mesh):
    in_specs = (
        P("gx", "gy", None, None),
        P(None, "gx", "gy", None, None, None),
        P(None, "gx", "gy", None, None),
        P(None, "gx", "gy", None, None),
        P(None, "gx", "gy", None),
        P(),
    )
    out_specs = P(None, "gx", "gy", None, None)
    return jax.shard_map(body, mesh=mesh, in_specs=in_specs, out_specs=out_specs, check_vma=False)
```

profile of v0, /device:TPU:1, one launch (start us, length us, event | category | flops | bytes accessed | tf_op | source)
XLA Modules:
  0.0 448.1 jit_solution(6572422167671523875)
XLA Ops:
  6.5 0.7 all-gather.19.cloned.1.call-update
  7.3 0.7 all-gather.17.cloned.1.call-update
  8.1 12.2 %slice_bitcast_fusion.3 = (bf16[8,512,512]{2,1,0:T(8,128)(2,1)}, bf16[8,512,512]{2,1,0:T(8,128)(2,1)}, bf16[8,512,512]{2,1,0:T(8,128)(2,1)}, bf16[8,512,512]{2,1,0:T(8,128)(2,1)}) fusion(bf16[4,1,1,8,512,512]{5,4,3,2,1,0:T(8,128)(2,1)} %param.7), kind=kLoop, calls=%fused_computation.10 | loop fusion | bytes 33554432 | tf_op jit(solution)/shard_map/squeeze | solution.py:41
  20.3 8.1 %copy.35 = bf16[8,512,512]{1,0,2:T(8,128)(2,1)} copy(bf16[8,512,512]{2,1,0:T(8,128)(2,1)} %get-tuple-element.13) | data formatting | bytes 8388608 | tf_op jit(solution)/shard_map/squeeze | solution.py:41
  28.5 0.7 gather_fusion
  29.3 8.8 %all-gather.19.cloned.1.call-done = bf16[8,1,512,256]{3,2,1,0:T(8,128)(2,1)} async-done(((bf16[1,1,512,256]{3,2,1,0:T(8,128)(2,1)}), bf16[8,1,512,256]{3,2,1,0:T(8,128)(2,1)}) %all-gather.19.cloned.1.call-update) | async-done | bytes 2097168 | tf_op jit(solution)/shard_map/all_gather | solution.py:32
  38.1 4.9 %fusion.5 = f32[8,512,256]{2,0,1:T(8,128)} fusion(bf16[8,1,512,256]{3,2,1,0:T(8,128)(2,1)} %all-gather.19.cloned.1.call-done, s32[8]{0:T(128)S(1)} %get-tuple-element.20, pred[8]{0:T(512)(128)(4,1)S(1)} %get-tuple-element.25), kind=kOutput, calls=%fused_computation.12 | convolution fusion | flops 16777344 | bytes 6291496 | tf_op jit(solution)/shard_map/kj,jbr->kbr/dot_general | solution.py:36
  43.0 48.6 %all-gather.17.cloned.1.call-done = bf16[16,1,512,256]{3,2,1,0:T(8,128)(2,1)} async-done(((bf16[1,1,512,256]{3,2,1,0:T(8,128)(2,1)}), bf16[16,1,512,256]{3,2,1,0:T(8,128)(2,1)}) %all-gather.17.cloned.1.call-update) | async-done | bytes 4194320 | tf_op jit(solution)/shard_map/all_gather | solution.py:31
  91.6 8.4 %fusion.17 = f32[512,256]{0,1:T(8,128)S(1)} fusion(bf16[8,512,512]{1,0,2:T(8,128)(2,1)} %copy.35, f32[8,512,256]{2,0,1:T(8,128)} %fusion.5, bf16[16,1,512,256]{3,2,1,0:T(8,128)(2,1)} %all-gather.17.cloned.1.call-done, s32[8]{0:T(128)S(1)} %get-tuple-element.30, pred[8]{0:T(512)(128)(4,1)S(1)} %get-tuple-element.26), kind=kOutput, calls=%fused_computation.22 | convolution fusion | flops 1109393664 | bytes 13107240 | tf_op jit(solution)/shard_map/kbc,kcr->br/dot_general | solution.py:40
  100.1 2.1 fusion.20
  102.2 0.5 all-gather.21.cloned.1.call-update
  102.8 0.2 all-gather.27.cloned.1.call-start
  103.0 8.0 %copy.38 = bf16[8,512,512]{1,0,2:T(8,128)(2,1)} copy(bf16[8,512,512]{2,1,0:T(8,128)(2,1)} %get-tuple-element.14) | data formatting | bytes 8388608 | tf_op jit(solution)/shard_map/squeeze | solution.py:41
  111.0 16.8 %all-gather.23.cloned.1.call-done = bf16[4096,256]{0,1:T(8,128)(2,1)} async-done(((bf16[512,256]{0,1:T(8,128)(2,1)}), bf16[4096,256]{0,1:T(8,128)(2,1)}) %all-gather.23.cloned.1.call-update) | async-done | bytes 2097168 | tf_op jit(solution)/shard_map/all_gather | solution.py:32
  127.9 2.5 copy.47
  130.3 3.5 copy.22
  133.8 52.5 %all-gather.21.cloned.1.call-done = bf16[8192,256]{0,1:T(8,128)(2,1)} async-done(((bf16[512,256]{0,1:T(8,128)(2,1)}), bf16[8192,256]{0,1:T(8,128)(2,1)}) %all-gather.21.cloned.1.call-update) | async-done | bytes 4194320 | tf_op jit(solution)/shard_map/all_gather | solution.py:31
  186.4 6.0 %copy.46 = bf16[32,8,16,512]{3,2,1,0:T(8,128)(2,1)} copy(bf16[32,8,16,512]{3,1,2,0:T(8,128)(2,1)} %bitcast.166) | data formatting | bytes 8388608
  192.4 8.5 %copy.21 = bf16[16,512,256]{2,0,1:T(8,128)(2,1)} copy(bf16[16,512,256]{1,0,2:T(8,128)(2,1)} %bitcast.160) | data formatting | bytes 8388608 | tf_op jit(solution)/shard_map/all_gather | solution.py:31
  200.9 5.1 %fusion.50 = f32[8,512,256]{2,0,1:T(8,128)} fusion(bf16[16,512,256]{2,0,1:T(8,128)(2,1)} %copy.21, s32[8]{0:T(128)S(1)} %get-tuple-element.29, pred[8]{0:T(512)(128)(4,1)S(1)} %get-tuple-element.22), kind=kOutput, calls=%fused_computation.65 | convolution fusion | flops 33554688 | bytes 8388648 | tf_op jit(solution)/shard_map/kj,jbr->kbr/dot_general | solution.py:33
  206.0 6.3 %fusion.16 = f32[512,256]{0,1:T(8,128)} fusion(bf16[8,512,512]{1,0,2:T(8,128)(2,1)} %copy.38, f32[8,512,256]{2,0,1:T(8,128)} %fusion.50, bf16[8,512,256]{2,0,1:T(8,128)(2,1)S(1)} %copy-done.5, s32[8]{0:T(128)S(1)} %get-tuple-element.19, pred[8]{0:T(512)(128)(4,1)S(1)} %get-tuple-element.21), kind=kOutput, calls=%fused_computation.21 | convolution fusion | flops 1092616320 | bytes 11010088 | tf_op jit(solution)/shard_map/kbc,kcr->br/dot_general | solution.py:40
  212.4 2.3 fusion.21
  214.7 0.5 all-gather.25.cloned.1.call-update
  215.2 0.3 all-gather.31.cloned.1.call-start
  215.5 8.1 %copy.41 = bf16[8,512,512]{1,0,2:T(8,128)(2,1)} copy(bf16[8,512,512]{2,1,0:T(8,128)(2,1)} %get-tuple-element.16) | data formatting | bytes 8388608 | tf_op jit(solution)/shard_map/squeeze | solution.py:41
  223.6 17.3 %all-gather.27.cloned.1.call-done = bf16[4096,256]{0,1:T(8,128)(2,1)} async-done(((bf16[512,256]{0,1:T(8,128)(2,1)}), bf16[4096,256]{0,1:T(8,128)(2,1)}) %all-gather.27.cloned.1.call-update) | async-done | bytes 2097168 | tf_op jit(solution)/shard_map/all_gather | solution.py:32
  240.9 2.5 copy.49
  243.4 3.5 copy.26
  246.9 52.6 %all-gather.25.cloned.1.call-done = bf16[8192,256]{0,1:T(8,128)(2,1)} async-done(((bf16[512,256]{0,1:T(8,128)(2,1)}), bf16[8192,256]{0,1:T(8,128)(2,1)}) %all-gather.25.cloned.1.call-update) | async-done | bytes 4194320 | tf_op jit(solution)/shard_map/all_gather | solution.py:31
  299.4 6.1 %copy.48 = bf16[32,8,16,512]{3,2,1,0:T(8,128)(2,1)} copy(bf16[32,8,16,512]{3,1,2,0:T(8,128)(2,1)} %bitcast.167) | data formatting | bytes 8388608
  305.5 8.6 %copy.25 = bf16[16,512,256]{2,0,1:T(8,128)(2,1)} copy(bf16[16,512,256]{1,0,2:T(8,128)(2,1)} %bitcast.161) | data formatting | bytes 8388608 | tf_op jit(solution)/shard_map/all_gather | solution.py:31
  314.0 5.1 %fusion.58 = f32[8,512,256]{2,0,1:T(8,128)} fusion(bf16[16,512,256]{2,0,1:T(8,128)(2,1)} %copy.25, s32[8]{0:T(128)S(1)} %get-tuple-element.28, pred[8]{0:T(512)(128)(4,1)S(1)} %get-tuple-element.24), kind=kOutput, calls=%fused_computation.70 | convolution fusion | flops 33554688 | bytes 8388648 | tf_op jit(solution)/shard_map/kj,jbr->kbr/dot_general | solution.py:33
  319.2 6.3 %fusion.15 = f32[512,256]{0,1:T(8,128)} fusion(bf16[8,512,512]{1,0,2:T(8,128)(2,1)} %copy.41, f32[8,512,256]{2,0,1:T(8,128)} %fusion.58, bf16[8,512,256]{2,0,1:T(8,128)(2,1)S(1)} %copy-done.6, s32[8]{0:T(128)S(1)} %get-tuple-element.18, pred[8]{0:T(512)(128)(4,1)S(1)} %get-tuple-element.23), kind=kOutput, calls=%fused_computation.20 | convolution fusion | flops 1092616320 | bytes 11010088 | tf_op jit(solution)/shard_map/kbc,kcr->br/dot_general | solution.py:40
  325.5 2.3 fusion.22
  327.8 0.3 all-gather.29.cloned.1.call-start
  328.1 0.4 all-gather.29.cloned.1.call-update
  328.5 8.0 %copy.44 = bf16[8,512,512]{1,0,2:T(8,128)(2,1)} copy(bf16[8,512,512]{2,1,0:T(8,128)(2,1)} %get-tuple-element.15) | data formatting | bytes 8388608 | tf_op jit(solution)/shard_map/squeeze | solution.py:41
  336.6 17.5 %all-gather.31.cloned.1.call-done = bf16[4096,256]{0,1:T(8,128)(2,1)} async-done(((bf16[512,256]{0,1:T(8,128)(2,1)}), bf16[4096,256]{0,1:T(8,128)(2,1)}) %all-gather.31.cloned.1.call-update) | async-done | bytes 2097168 | tf_op jit(solution)/shard_map/all_gather | solution.py:32
  354.0 2.5 copy.51
  356.5 3.5 copy.30
  360.0 52.7 %all-gather.29.cloned.1.call-done = bf16[8192,256]{0,1:T(8,128)(2,1)} async-done(((bf16[512,256]{0,1:T(8,128)(2,1)}), bf16[8192,256]{0,1:T(8,128)(2,1)}) %all-gather.29.cloned.1.call-update) | async-done | bytes 4194320 | tf_op jit(solution)/shard_map/all_gather | solution.py:31
  412.7 6.0 %copy.50 = bf16[32,8,16,512]{3,2,1,0:T(8,128)(2,1)} copy(bf16[32,8,16,512]{3,1,2,0:T(8,128)(2,1)} %bitcast.168) | data formatting | bytes 8388608
  418.7 8.6 %copy.29 = bf16[16,512,256]{2,0,1:T(8,128)(2,1)} copy(bf16[16,512,256]{1,0,2:T(8,128)(2,1)} %bitcast.162) | data formatting | bytes 8388608 | tf_op jit(solution)/shard_map/all_gather | solution.py:31
  427.3 4.9 %fusion.66 = f32[8,512,256]{2,0,1:T(8,128)} fusion(bf16[16,512,256]{2,0,1:T(8,128)(2,1)} %copy.29, s32[8]{0:T(128)S(1)} %get-tuple-element.27, pred[8]{0:T(512)(128)(4,1)S(1)} %get-tuple-element.6), kind=kOutput, calls=%fused_computation.75 | convolution fusion | flops 33554688 | bytes 8388648 | tf_op jit(solution)/shard_map/kj,jbr->kbr/dot_general | solution.py:33
  432.2 6.1 %fusion.14 = f32[512,256]{0,1:T(8,128)S(1)} fusion(bf16[8,512,512]{1,0,2:T(8,128)(2,1)} %copy.44, f32[8,512,256]{2,0,1:T(8,128)} %fusion.66, bf16[8,512,256]{2,0,1:T(8,128)(2,1)} %copy.30, s32[8]{0:T(128)S(1)} %get-tuple-element.17, pred[8]{0:T(512)(128)(4,1)S(1)} %get-tuple-element.5), kind=kOutput, calls=%fused_computation.19 | convolution fusion | flops 1092616320 | bytes 11010088 | tf_op jit(solution)/shard_map/kbc,kcr->br/dot_general | solution.py:40
  438.4 1.4 fusion.24
  439.8 0.1 maximum_bitcast_fusion
  439.9 1.3 copy.33
  (34 shorter events, 0.5 us)
Async XLA Ops:
  6.5 22.0 %copy-start = (s32[640]{0:T(1024)S(1)}, s32[640]{0:T(1024)}, u32[]{:S(2)}) copy-start(s32[640]{0:T(1024)} %param.11) | copy-start | bytes 7684
  6.5 31.6 %all-gather.19.cloned.1.call-start = ((), (), s32[]{:S(2)}) async-start(), calls=%async_computation.1 | async-start | bytes 2359296 | tf_op jit(solution)/shard_map/all_gather | solution.py:32
  7.3 84.4 %all-gather.17.cloned.1.call-start = ((), (), s32[]{:S(2)}) async-start(), calls=%async_computation | async-start | bytes 4456448 | tf_op jit(solution)/shard_map/all_gather | solution.py:31
  8.0 119.8 %all-gather.23.cloned.1.call-start = ((), (), s32[]{:S(2)}) async-start(), calls=%async_computation.3 | async-start | bytes 2359296 | tf_op jit(solution)/shard_map/all_gather | solution.py:32
  20.3 8.1 %copy-start.8 = (s32[4,1,1,8]{3,2,1,0:T(1,128)S(1)}, s32[4,1,1,8]{3,2,1,0:T(1,128)}, u32[]{:S(2)}) copy-start(s32[4,1,1,8]{3,2,1,0:T(1,128)} %param.10) | copy-start | bytes 388
  91.6 8.4 %copy-start.7 = (bf16[4,1,1,512,256]{4,3,2,1,0:T(8,128)(2,1)S(1)}, bf16[4,1,1,512,256]{4,3,2,1,0:T(8,128)(2,1)}, u32[]{:S(2)}) copy-start(bf16[4,1,1,512,256]{4,3,2,1,0:T(8,128)(2,1)} %param.9) | copy-start | bytes 3145732
  102.2 84.2 %all-gather.21.cloned.1.call-start = ((), (), s32[]{:S(2)}) async-start(), calls=%async_computation.2 | async-start | bytes 4456448 | tf_op jit(solution)/shard_map/all_gather | solution.py:31
  102.8 138.2 %all-gather.27.cloned.1.call-start = ((), (), s32[]{:S(2)}) async-start(), calls=%async_computation.5 | async-start | bytes 2359296 | tf_op jit(solution)/shard_map/all_gather | solution.py:32
  200.9 5.1 %copy-start.5 = (bf16[8,512,256]{2,0,1:T(8,128)(2,1)S(1)}, bf16[8,512,256]{2,0,1:T(8,128)(2,1)}, u32[]{:S(2)}) copy-start(bf16[8,512,256]{2,0,1:T(8,128)(2,1)} %copy.22) | copy-start | bytes 6291460
  214.7 84.8 %all-gather.25.cloned.1.call-start = ((), (), s32[]{:S(2)}) async-start(), calls=%async_computation.4 | async-start | bytes 4456448 | tf_op jit(solution)/shard_map/all_gather | solution.py:31
  215.2 138.8 %all-gather.31.cloned.1.call-start = ((), (), s32[]{:S(2)}) async-start(), calls=%async_computation.7 | async-start | bytes 2359296 | tf_op jit(solution)/shard_map/all_gather | solution.py:32
  314.0 5.1 %copy-start.6 = (bf16[8,512,256]{2,0,1:T(8,128)(2,1)S(1)}, bf16[8,512,256]{2,0,1:T(8,128)(2,1)}, u32[]{:S(2)}) copy-start(bf16[8,512,256]{2,0,1:T(8,128)(2,1)} %copy.26) | copy-start | bytes 6291460
  327.8 84.9 %all-gather.29.cloned.1.call-start = ((), (), s32[]{:S(2)}) async-start(), calls=%async_computation.6 | async-start | bytes 4456448 | tf_op jit(solution)/shard_map/all_gather | solution.py:31
  432.2 7.6 %copy-start.2 = (bf16[512,256]{0,1:T(8,128)(2,1)S(1)}, bf16[512,256]{0,1:T(8,128)(2,1)}, u32[]{:S(2)}) copy-start(bf16[512,256]{0,1:T(8,128)(2,1)} %fusion.20) | copy-start | bytes 786436
  432.2 7.6 %copy-start.3 = (bf16[512,256]{0,1:T(8,128)(2,1)S(1)}, bf16[512,256]{0,1:T(8,128)(2,1)}, u32[]{:S(2)}) copy-start(bf16[512,256]{0,1:T(8,128)(2,1)} %fusion.21) | copy-start | bytes 786436
  432.2 7.6 %copy-start.4 = (bf16[512,256]{0,1:T(8,128)(2,1)S(1)}, bf16[512,256]{0,1:T(8,128)(2,1)}, u32[]{:S(2)}) copy-start(bf16[512,256]{0,1:T(8,128)(2,1)} %fusion.22) | copy-start | bytes 786436
  432.2 9.0 %copy-start.1 = (s32[640]{0:T(1024)S(1)}, s32[640]{0:T(1024)}, u32[]{:S(2)}) copy-start(s32[640]{0:T(1024)} %param.11) | copy-start | bytes 7684
Sparse Core Ops, SparseCore 0:
  9.1 28.9 all-gather.18
  40.2 51.3 all-gather.16
  102.3 25.5 all-gather.22
  129.8 56.4 all-gather.20
  214.8 26.0 all-gather.26
  242.9 56.4 all-gather.24
  327.9 26.0 all-gather.30
  356.1 56.4 all-gather.28
where the time goes:
time: 450 us; the launch traced here: 448 us
  waiting for transfers between devices  270 us (60%)
  local copies, waits for them, and re-layouts  108 us (24%)
  matrix products  55.2 us (12%)
  between operations  13.6 us (3%)
    all_gather x4, waiting for transfers between devices, body(): row_draws = lax.all_gather(previous[None], 'gy', axis=0, tiled=True)  206 us
    all_gather x4, waiting for transfers between devices, body(): col_draws = lax.all_gather(previous[None], 'gx', axis=0, tiled=True)  60.4 us
    squeeze x5, local copies, waits for them, and re-layouts, body(): cond_factors[level, 0, 0]  44.5 us
    dot_general x4, matrix products, body(): jnp.einsum('kbc,kcr->br', cond_factors[level, 0, 0], picked, preferred_el...  27.2 us
    all_gather x3, local copies, waits for them, and re-layouts, body(): row_draws = lax.all_gather(previous[None], 'gy', axis=0, tiled=True)  25.7 us
    unnamed x24, local copies, waits for them, and re-layouts  25.6 us
    dot_general x3, matrix products, body(): jnp.einsum('kj,jbr->kbr', select_row, row_draws, preferred_element_type=j...  15.1 us
    all_gather x3, local copies, waits for them, and re-layouts, body(): col_draws = lax.all_gather(previous[None], 'gx', axis=0, tiled=True)  10.4 us
  transfers between devices with their start and end apart: 8, of which 8 were waited for; matrix products, arithmetic and copies ran while one was open for 15% of the time, Pallas kernels for 0%

commit v1 on v0

v1 whole, which is shorter than its diff:
```python
import functools

import jax
import jax.numpy as jnp
from jax import lax
from jax.experimental import pallas as pl
from jax.experimental.pallas import tpu as pltpu
from jax.sharding import PartitionSpec as P

AXES = ("gx", "gy")
SIDE = 4


def pairs(move):
    out = []
    for z in range(SIDE):
        for c in range(2):
            for x in range(SIDE):
                for y in range(SIDE):
                    x2, y2, z2, c2 = move(x, y, z, c)
                    target = ((z2 % SIDE) * 2 + c2) * SIDE * SIDE + (x2 % SIDE) * SIDE + y2 % SIDE
                    out.append(((z * 2 + c) * SIDE * SIDE + x * SIDE + y, target))
    return out


def first(step):
    return pairs(lambda x, y, z, c: (x + step, y, z, c) if c == 0 else (x, y + step, z, c))


def second(step):
    return pairs(lambda x, y, z, c: (x, y + step, z, c) if c == 0 else (x + step, y, z, c))


def along_z(step):
    return pairs(lambda x, y, z, c: (x, y, z + step, c))


OTHER = pairs(lambda x, y, z, c: (x, y, z, 1 - c))


def send(value, route):
    return lax.ppermute(value, AXES, route)


def level_kernel(level, where_ref, *refs):
    sources = refs[:10]
    own_f, other_f, own_c, other_c, noise_ref, out_ref, factor, chol, picked, total, sem_f, sem_c = refs[10:]
    copies = []
    for k in range(8):
        for j, ref in enumerate((own_f, other_f)):
            copies.append(pltpu.make_async_copy(ref.at[level, k], factor.at[j, k], sem_f.at[j, k]))
    for j, ref in enumerate((own_c, other_c)):
        copies.append(pltpu.make_async_copy(ref.at[level], chol.at[j], sem_c.at[j]))
    for copy in copies[16:] + copies[:16]:
        copy.start()

    for j in range(2):
        copies[16 + j].wait()
        total[j] = jnp.dot(chol[j], noise_ref[j], preferred_element_type=jnp.float32)

    def step(k, carry):
        for j, ref in enumerate((own_f, other_f)):
            code = where_ref[level, j, k]
            which = code // 8
            part = code % 8
            for r, source in enumerate(sources):
                @pl.when(which == r)
                def _():
                    picked[j] = source[part]
            pltpu.make_async_copy(ref.at[level, k], factor.at[j, k], sem_f.at[j, k]).wait()
            total[j] += jnp.dot(factor[j, k], picked[j], preferred_element_type=jnp.float32)
        return carry

    lax.fori_loop(0, 8, step, 0)
    out_ref[...] = total[...].astype(out_ref.dtype)


def level_call(level, where, sources, own_f, other_f, own_c, other_c, noise):
    vmem = pl.BlockSpec(memory_space=pltpu.VMEM)
    anywhere = pl.BlockSpec(memory_space=pl.ANY)
    rows = own_f.shape[-1]
    columns = noise.shape[-1]
    return pl.pallas_call(
        functools.partial(level_kernel, level),
        out_shape=jax.ShapeDtypeStruct((2, rows, columns), jnp.bfloat16),
        in_specs=[pl.BlockSpec(memory_space=pltpu.SMEM)] + [vmem] * 10 + [anywhere] * 4 + [vmem],
        out_specs=vmem,
        scratch_shapes=[
            pltpu.VMEM((2, 8, rows, rows), jnp.bfloat16),
            pltpu.VMEM((2, rows, rows), jnp.bfloat16),
            pltpu.VMEM((2, rows, columns), jnp.bfloat16),
            pltpu.VMEM((2, rows, columns), jnp.float32),
            pltpu.SemaphoreType.DMA((2, 8)),
            pltpu.SemaphoreType.DMA((2,)),
        ],
        compiler_params=pltpu.CompilerParams(vmem_limit_bytes=28 * 1024 * 1024),
        cost_estimate=pl.CostEstimate(
            flops=2 * 18 * rows * rows * columns, bytes_accessed=18 * rows * rows * 2, transcendentals=0
        ),
    )(where, *sources, own_f, other_f, own_c, other_c, noise)


def body(prior_draws, cond_factors, chol_factors, noise, neighbours, block_slot):
    my_gx = lax.axis_index("gx")
    my_gy = lax.axis_index("gy")
    z, core = my_gx // 2, my_gx % 2
    x, y = my_gy // SIDE, my_gy % SIDE
    half = prior_draws.shape[-1] // 2
    low = core == 0

    def mine(block):
        return jnp.where(low, block[..., :half], block[..., half:])

    def others(block):
        return jnp.where(low, block[..., half:], block[..., :half])

    prior = prior_draws[0, 0]
    draws = jnp.stack([mine(prior), send(others(prior), OTHER)])
    own_f = cond_factors[:, 0, 0]
    other_f = send(own_f, OTHER)
    own_c = chol_factors[:, 0, 0]
    other_c = send(own_c, OTHER)
    own_noise = noise[:, 0, 0]
    noises = jnp.stack([mine(own_noise), send(others(own_noise), OTHER)], axis=1)
    own_n = neighbours[:, 0, 0]
    both_n = jnp.stack([own_n, send(own_n, OTHER)], axis=1)

    device = block_slot[both_n] % (2 * SIDE**3)
    row, col = device // (SIDE * SIDE), device % (SIDE * SIDE)
    same_core = row % 2 == core
    j = jnp.arange(2, dtype=jnp.int32)[None, :, None]
    my_row = z * 2 + jnp.where(j == 0, core, 1 - core)
    dx, dy = (col // SIDE - x) % SIDE, (col % SIDE - y) % SIDE
    dz = (row // 2 - z) % SIDE
    d1, d2 = jnp.where(low, dx, dy), jnp.where(low, dy, dx)
    place = lambda d: jnp.where(d == 0, 0, jnp.where(d == 3, 1, jnp.where(d == 1, 2, 3)))
    p1, p2, p3 = place(d1), place(d2), place(dz)
    in_row = jnp.where(p2 == 0, p1 * 8 + j, (3 + p2) * 8 + p1 * 2 + j)
    other_j = jnp.where(same_core, 0, 1)
    in_col = jnp.where(p3 == 0, 0, 6 + p3) * 8 + other_j
    where = jnp.where(row == my_row, in_row, in_col).astype(jnp.int32)

    results = []
    for level in range(cond_factors.shape[0]):
        near = [send(draws, first(s)) for s in (1, -1, 2)]
        column = [send(draws, along_z(s)) for s in (1, -1, 2)]
        line = jnp.concatenate([draws] + near)
        far = [send(line, second(s)) for s in (1, -1, 2)]
        draws = level_call(
            level, where, [draws] + near + far + column, own_f, other_f, own_c, other_c, noises[level]
        )
        got = send(draws[1], OTHER)
        results.append(
            jnp.where(
                low,
                jnp.concatenate([draws[0], got], axis=-1),
                jnp.concatenate([got, draws[0]], axis=-1),
            )
        )
    return jnp.stack(results)[:, None, None]


def solution(mesh):
    in_specs = (
        P("gx", "gy", None, None),
        P(None, "gx", "gy", None, None, None),
        P(None, "gx", "gy", None, None),
        P(None, "gx", "gy", None, None),
        P(None, "gx", "gy", None),
        P(),
    )
    out_specs = P(None, "gx", "gy", None, None)
    return jax.shard_map(body, mesh=mesh, in_specs=in_specs, out_specs=out_specs, check_vma=False)
```

time: 450 us -> 250 us (0.56)
  waiting for transfers between devices: 270 us -> 112 us
  local copies, waits for them, and re-layouts: 108 us -> 21.1 us
  starting transfers between devices: 0.94 us -> 74.9 us
  matrix products: 55.2 us -> 0 us
  Pallas kernels: 0 us -> 32.1 us
  between operations: 13.6 us -> 0.21 us
  other arithmetic: 0.18 us -> 8.78 us
    all_gather x8 -> x0, waiting for transfers between devices: 267 us -> none  [the longest x4 206 us: body(): row_draws = lax.all_gather(previous[None], 'gy', axis=0, tiled=True)]
    ppermute x0 -> x45, waiting for transfers between devices: none -> 112 us  [send(): return lax.ppermute(value, AXES, route)]
    ppermute x0 -> x45, starting transfers between devices: none -> 74.9 us  [send(): return lax.ppermute(value, AXES, route)]
    dot_general x12 -> x0, matrix products: 55.2 us -> none  [the longest x4 27.2 us: body(): jnp.einsum('kbc,kcr->br', cond_factors[level, 0, 0], picked, preferred_el...]
    squeeze x6 -> x0, local copies, waits for them, and re-layouts: 44.5 us -> none  [the longest x5 44.5 us: body(): cond_factors[level, 0, 0]]
    all_gather x6 -> x0, local copies, waits for them, and re-layouts: 36.1 us -> none  [the longest x3 25.7 us: body(): row_draws = lax.all_gather(previous[None], 'gy', axis=0, tiled=True)]
    pallas_call x0 -> x4, Pallas kernels: none -> 32.1 us  [level_call(): pl.pallas_call(functools.partial(level_kernel, level), out_shape=jax.Shap...]
    unnamed x24 -> x25, local copies, waits for them, and re-layouts: 25.6 us -> 19.4 us
  transfers between devices with their start and end apart: 8 -> 45, of which waited for: 8 -> 26; matrix products, arithmetic and copies ran while one was open for 15% -> 4% of each run, Pallas kernels for 0% -> 3%
where the time goes in v1:
time: 250 us; the launch traced here: 249 us
  waiting for transfers between devices  112 us (45%)
  starting transfers between devices  74.9 us (30%)
  Pallas kernels  32.1 us (13%)
  local copies, waits for them, and re-layouts  21.1 us (8%)
  other arithmetic  8.78 us (4%)
    ppermute x45, waiting for transfers between devices, send(): return lax.ppermute(value, AXES, route)  112 us
    ppermute x45, starting transfers between devices, send(): return lax.ppermute(value, AXES, route)  74.9 us
    pallas_call x4, Pallas kernels, level_call(): pl.pallas_call(functools.partial(level_kernel, level), out_shape=jax.Shap...  32.1 us
    unnamed x25, local copies, waits for them, and re-layouts  19.4 us
  transfers between devices with their start and end apart: 45, of which 26 were waited for; matrix products, arithmetic and copies ran while one was open for 4% of the time, Pallas kernels for 3%

profile of v1, /device:TPU:1, one launch (start us, length us, event | category | flops | bytes accessed | tf_op | source)
XLA Modules:
  0.0 249.2 jit_solution(9374441630717798985)
XLA Ops:
  0.0 1.4 collective-permute-start.11
  2.5 1.7 constant_dynamic-update-slice_fusion.4
  4.2 14.0 %collective-permute-done.1 = bf16[512,128]{1,0:T(8,128)(2,1)S(1)} collective-permute-done((bf16[512,128]{1,0:T(8,128)(2,1)S(1)}, bf16[512,128]{1,0:T(8,128)(2,1)S(1)}, u32[]{:S(2)}, u32[]{:S(2)}) %collective-permute-start.1) | collective-permute-done | bytes 131104 | tf_op jit(solution)/shard_map/ppermute | solution.py:42
  18.2 1.4 collective-permute-start.2
  20.0 2.7 %collective-permute-start.3 = (bf16[2,512,128]{2,1,0:T(8,128)(2,1)S(1)}, bf16[2,512,128]{2,1,0:T(8,128)(2,1)S(1)}, u32[]{:S(2)}, u32[]{:S(2)}) collective-permute-start(bf16[2,512,128]{2,1,0:T(8,128)(2,1)S(1)} %pad_maximum_fusion.4.refs_0_), channel_id=1, source_target_pairs={{0,12},{1,13},{2,14},{3,15},{4,0},{5,1},{6,2},{7,3},{8,4},{9,5},{1... | collective-permute-start | bytes 786440 | tf_op jit(solution)/shard_map/ppermute | solution.py:42
  22.9 6.7 %collective-permute-done = s32[4,8]{1,0:T(4,128)S(1)} collective-permute-done((s32[4,8]{1,0:T(4,128)}, s32[4,8]{1,0:T(4,128)S(1)}, u32[]{:S(2)}, u32[]{:S(2)}) %collective-permute-start) | collective-permute-done | bytes 160 | tf_op jit(solution)/shard_map/ppermute | solution.py:42
  29.6 3.0 %collective-permute-start.4 = (bf16[2,512,128]{2,1,0:T(8,128)(2,1)S(1)}, bf16[2,512,128]{2,1,0:T(8,128)(2,1)S(1)}, u32[]{:S(2)}, u32[]{:S(2)}) collective-permute-start(bf16[2,512,128]{2,1,0:T(8,128)(2,1)S(1)} %pad_maximum_fusion.4.refs_0_), channel_id=1, source_target_pairs={{0,8},{1,9},{2,10},{3,11},{4,12},{5,13},{6,14},{7,15},{8,0},{9,1},... | collective-permute-start | bytes 786440 | tf_op jit(solution)/shard_map/ppermute | solution.py:42
  32.6 3.6 %collective-permute-start.10 = (bf16[2,512,128]{2,1,0:T(8,128)(2,1)S(1)}, bf16[2,512,128]{2,1,0:T(8,128)(2,1)S(1)}, u32[]{:S(2)}, u32[]{:S(2)}) collective-permute-start(bf16[2,512,128]{2,1,0:T(8,128)(2,1)S(1)} %pad_maximum_fusion.4.refs_0_), channel_id=1, source_target_pairs={{0,64},{1,65},{2,66},{3,67},{4,68},{5,69},{6,70},{7,71},{8,72},{9,... | collective-permute-start | bytes 786440 | tf_op jit(solution)/shard_map/ppermute | solution.py:42
  36.2 2.1 broadcast_select_fusion
  40.4 2.0 collective-permute-done.10.refs_9_
  42.5 2.8 %collective-permute-start.9 = (bf16[2,512,128]{2,1,0:T(8,128)(2,1)S(1)}, bf16[2,512,128]{2,1,0:T(8,128)(2,1)S(1)}, u32[]{:S(2)}, u32[]{:S(2)}) collective-permute-start(bf16[2,512,128]{2,1,0:T(8,128)(2,1)S(1)} %pad_maximum_fusion.4.refs_0_), channel_id=1, source_target_pairs={{0,96},{1,97},{2,98},{3,99},{4,100},{5,101},{6,102},{7,103},{8,104... | collective-permute-start | bytes 786440 | tf_op jit(solution)/shard_map/ppermute | solution.py:42
  47.4 1.4 collective-permute-done.8.refs_7_
  51.0 3.1 %collective-permute-start.6 = (bf16[8,512,128]{2,1,0:T(8,128)(2,1)}, bf16[8,512,128]{2,1,0:T(8,128)(2,1)}, u32[]{:S(2)}, u32[]{:S(2)}) collective-permute-start(bf16[8,512,128]{2,1,0:T(8,128)(2,1)} %constant_dynamic-update-slice_fusion), channel_id=1, source_target_pairs={{0,3},{1,0},{2,1},{3,2},{4,7},{5,4},{6,5},{7,6},{8,11},{9,8},{10,9... | collective-permute-start | bytes 3145736 | tf_op jit(solution)/shard_map/ppermute | solution.py:42
  57.7 1.4 fusion.6
  59.1 17.2 %collective-permute-done.5.refs_4_ = bf16[8,512,128]{2,1,0:T(8,128)(2,1)} collective-permute-done((bf16[8,512,128]{2,1,0:T(8,128)(2,1)}, bf16[8,512,128]{2,1,0:T(8,128)(2,1)}, u32[]{:S(2)}, u32[]{:S(2)}) %collective-permute-start.5) | collective-permute-done | bytes 1048608 | tf_op jit(solution)/shard_map/ppermute | solution.py:42
  77.5 5.8 %copy-done.2 = bf16[4,1,1,8,512,512]{5,4,3,2,1,0:T(8,128)(2,1)S(1)} copy-done((bf16[4,1,1,8,512,512]{5,4,3,2,1,0:T(8,128)(2,1)S(1)}, bf16[4,1,1,8,512,512]{5,4,3,2,1,0:T(8,128)(2,1)}, u32[]{:S(2)}) %copy-start.2) | copy-done | bytes 16777240
  83.2 1.6 copy-done.4
  86.7 9.1 %shard_map.64.refs_0_ = bf16[2,512,128]{2,1,0:T(8,128)(2,1)S(1)} custom-call(s32[4,2,8]{2,1,0:T(2,128)S(1)} %compare_select_fusion.21.where_ref, bf16[2,512,128]{2,1,0:T(8,128)(2,1)S(1)} %pad_maximum_fusion.4.refs_0_, bf16[2,512,128]{2,1,0:T(8,128)(2,1)S(1)} %collective-permute-done.2.refs_1_, bf16[2,512,128]{2,1,0:T(8,128)(2,1)S(1)} %collective-permute-done.3.refs_2_, ...), custom_call_target="tpu_custom_call" | custom-call | flops 1207959552 | bytes 9437184 | tf_op jit(solution)/shard_map/pallas_call | solution.py:83
  96.4 2.2 collective-permute-start.16
  99.2 3.5 %collective-permute-done.15.refs_1_ = bf16[2,512,128]{2,1,0:T(8,128)(2,1)S(1)} collective-permute-done((bf16[2,512,128]{2,1,0:T(8,128)(2,1)S(1)}, bf16[2,512,128]{2,1,0:T(8,128)(2,1)S(1)}, u32[]{:S(2)}, u32[]{:S(2)}) %collective-permute-start.15) | collective-permute-done | bytes 262176 | tf_op jit(solution)/shard_map/ppermute | solution.py:42
  102.6 2.1 collective-permute-done.16.refs_2_
  106.9 2.3 collective-permute-start.19
  111.0 2.5 %collective-permute-start.22 = (bf16[2,512,128]{2,1,0:T(8,128)(2,1)S(1)}, bf16[2,512,128]{2,1,0:T(8,128)(2,1)S(1)}, u32[]{:S(2)}, u32[]{:S(2)}) collective-permute-start(bf16[2,512,128]{2,1,0:T(8,128)(2,1)S(1)} %shard_map.64.refs_0_), channel_id=1, source_target_pairs={{0,96},{1,97},{2,98},{3,99},{4,100},{5,101},{6,102},{7,103},{8,104... | collective-permute-start | bytes 786440 | tf_op jit(solution)/shard_map/ppermute | solution.py:42
  113.5 4.1 %collective-permute-done.21.refs_7_ = bf16[2,512,128]{2,1,0:T(8,128)(2,1)S(1)} collective-permute-done((bf16[2,512,128]{2,1,0:T(8,128)(2,1)S(1)}, bf16[2,512,128]{2,1,0:T(8,128)(2,1)S(1)}, u32[]{:S(2)}, u32[]{:S(2)}) %collective-permute-start.21) | collective-permute-done | bytes 262176 | tf_op jit(solution)/shard_map/ppermute | solution.py:42
  118.4 6.2 %collective-permute-done.23.refs_9_ = bf16[2,512,128]{2,1,0:T(8,128)(2,1)S(1)} collective-permute-done((bf16[2,512,128]{2,1,0:T(8,128)(2,1)S(1)}, bf16[2,512,128]{2,1,0:T(8,128)(2,1)S(1)}, u32[]{:S(2)}, u32[]{:S(2)}) %collective-permute-start.23) | collective-permute-done | bytes 262176 | tf_op jit(solution)/shard_map/ppermute | solution.py:42
  124.6 7.6 %collective-permute-done.19.refs_5_ = bf16[8,512,128]{2,1,0:T(8,128)(2,1)S(1)} collective-permute-done((bf16[8,512,128]{2,1,0:T(8,128)(2,1)S(1)}, bf16[8,512,128]{2,1,0:T(8,128)(2,1)S(1)}, u32[]{:S(2)}, u32[]{:S(2)}) %collective-permute-start.19) | collective-permute-done | bytes 1048608 | tf_op jit(solution)/shard_map/ppermute | solution.py:42
  132.2 1.8 collective-permute-done.20.refs_6_
  134.0 5.8 %copy-done.3 = bf16[4,1,1,8,512,512]{5,4,3,2,1,0:T(8,128)(2,1)S(1)} copy-done((bf16[4,1,1,8,512,512]{5,4,3,2,1,0:T(8,128)(2,1)S(1)}, bf16[4,1,1,8,512,512]{5,4,3,2,1,0:T(8,128)(2,1)}, u32[]{:S(2)}) %copy-start.3) | copy-done | bytes 16777240
  139.8 7.7 %shard_map.65.refs_0_ = bf16[2,512,128]{2,1,0:T(8,128)(2,1)S(1)} custom-call(s32[4,2,8]{2,1,0:T(2,128)S(1)} %compare_select_fusion.21.where_ref, bf16[2,512,128]{2,1,0:T(8,128)(2,1)S(1)} %shard_map.64.refs_0_, bf16[2,512,128]{2,1,0:T(8,128)(2,1)S(1)} %collective-permute-done.15.refs_1_, bf16[2,512,128]{2,1,0:T(8,128)(2,1)S(1)} %collective-permute-done.16.refs_2_, ...), custom_call_target="tpu_custom_call" | custom-call | flops 1207959552 | bytes 9437184 | tf_op jit(solution)/shard_map/pallas_call | solution.py:83
  148.1 2.1 collective-permute-start.26
  151.0 2.9 %collective-permute-done.25.refs_1_ = bf16[2,512,128]{2,1,0:T(8,128)(2,1)S(1)} collective-permute-done((bf16[2,512,128]{2,1,0:T(8,128)(2,1)S(1)}, bf16[2,512,128]{2,1,0:T(8,128)(2,1)S(1)}, u32[]{:S(2)}, u32[]{:S(2)}) %collective-permute-start.25) | collective-permute-done | bytes 262176 | tf_op jit(solution)/shard_map/ppermute | solution.py:42
  154.0 2.4 collective-permute-done.26.refs_2_
  158.6 1.8 collective-permute-start.29
  161.5 2.5 %collective-permute-start.32 = (bf16[2,512,128]{2,1,0:T(8,128)(2,1)S(1)}, bf16[2,512,128]{2,1,0:T(8,128)(2,1)S(1)}, u32[]{:S(2)}, u32[]{:S(2)}) collective-permute-start(bf16[2,512,128]{2,1,0:T(8,128)(2,1)S(1)} %shard_map.65.refs_0_), channel_id=1, source_target_pairs={{0,96},{1,97},{2,98},{3,99},{4,100},{5,101},{6,102},{7,103},{8,104... | collective-permute-start | bytes 786440 | tf_op jit(solution)/shard_map/ppermute | solution.py:42
  164.0 4.1 %collective-permute-done.31.refs_7_ = bf16[2,512,128]{2,1,0:T(8,128)(2,1)S(1)} collective-permute-done((bf16[2,512,128]{2,1,0:T(8,128)(2,1)S(1)}, bf16[2,512,128]{2,1,0:T(8,128)(2,1)S(1)}, u32[]{:S(2)}, u32[]{:S(2)}) %collective-permute-start.31) | collective-permute-done | bytes 262176 | tf_op jit(solution)/shard_map/ppermute | solution.py:42
  169.0 8.5 %collective-permute-done.33.refs_9_ = bf16[2,512,128]{2,1,0:T(8,128)(2,1)S(1)} collective-permute-done((bf16[2,512,128]{2,1,0:T(8,128)(2,1)S(1)}, bf16[2,512,128]{2,1,0:T(8,128)(2,1)S(1)}, u32[]{:S(2)}, u32[]{:S(2)}) %collective-permute-start.33) | collective-permute-done | bytes 262176 | tf_op jit(solution)/shard_map/ppermute | solution.py:42
  177.5 6.0 %collective-permute-done.29.refs_5_ = bf16[8,512,128]{2,1,0:T(8,128)(2,1)S(1)} collective-permute-done((bf16[8,512,128]{2,1,0:T(8,128)(2,1)S(1)}, bf16[8,512,128]{2,1,0:T(8,128)(2,1)S(1)}, u32[]{:S(2)}, u32[]{:S(2)}) %collective-permute-start.29) | collective-permute-done | bytes 1048608 | tf_op jit(solution)/shard_map/ppermute | solution.py:42
  184.3 7.7 %shard_map.66.refs_0_ = bf16[2,512,128]{2,1,0:T(8,128)(2,1)S(1)} custom-call(s32[4,2,8]{2,1,0:T(2,128)S(1)} %compare_select_fusion.21.where_ref, bf16[2,512,128]{2,1,0:T(8,128)(2,1)S(1)} %shard_map.65.refs_0_, bf16[2,512,128]{2,1,0:T(8,128)(2,1)S(1)} %collective-permute-done.25.refs_1_, bf16[2,512,128]{2,1,0:T(8,128)(2,1)S(1)} %collective-permute-done.26.refs_2_, ...), custom_call_target="tpu_custom_call" | custom-call | flops 1207959552 | bytes 9437184 | tf_op jit(solution)/shard_map/pallas_call | solution.py:83
  192.9 1.8 collective-permute-start.36
  195.4 3.0 %collective-permute-done.35.refs_1_ = bf16[2,512,128]{2,1,0:T(8,128)(2,1)S(1)} collective-permute-done((bf16[2,512,128]{2,1,0:T(8,128)(2,1)S(1)}, bf16[2,512,128]{2,1,0:T(8,128)(2,1)S(1)}, u32[]{:S(2)}, u32[]{:S(2)}) %collective-permute-start.35) | collective-permute-done | bytes 262176 | tf_op jit(solution)/shard_map/ppermute | solution.py:42
  198.5 2.4 collective-permute-done.36.refs_2_
  203.1 1.7 collective-permute-start.39
  206.5 9.3 %collective-permute-start.14 = (bf16[512,128]{1,0:T(8,128)(2,1)S(1)}, bf16[512,128]{1,0:T(8,128)(2,1)S(1)}, u32[]{:S(2)}, u32[]{:S(2)}) collective-permute-start(bf16[512,128]{1,0:T(8,128)(2,1)S(1)} %get-tuple-element.14), channel_id=1, source_target_pairs={{0,16},{1,17},{2,18},{3,19},{4,20},{5,21},{6,22},{7,23},{8,24},{9,... | collective-permute-start | bytes 393224 | tf_op jit(solution)/shard_map/ppermute | solution.py:42
  216.9 2.9 %collective-permute-start.42 = (bf16[2,512,128]{2,1,0:T(8,128)(2,1)S(1)}, bf16[2,512,128]{2,1,0:T(8,128)(2,1)S(1)}, u32[]{:S(2)}, u32[]{:S(2)}) collective-permute-start(bf16[2,512,128]{2,1,0:T(8,128)(2,1)S(1)} %shard_map.66.refs_0_), channel_id=1, source_target_pairs={{0,96},{1,97},{2,98},{3,99},{4,100},{5,101},{6,102},{7,103},{8,104... | collective-permute-start | bytes 786440 | tf_op jit(solution)/shard_map/ppermute | solution.py:42
  219.8 1.6 collective-permute-start.43
  221.4 9.2 %collective-permute-done.42.refs_8_ = bf16[2,512,128]{2,1,0:T(8,128)(2,1)S(1)} collective-permute-done((bf16[2,512,128]{2,1,0:T(8,128)(2,1)S(1)}, bf16[2,512,128]{2,1,0:T(8,128)(2,1)S(1)}, u32[]{:S(2)}, u32[]{:S(2)}) %collective-permute-start.42) | collective-permute-done | bytes 262176 | tf_op jit(solution)/shard_map/ppermute | solution.py:42
  232.0 7.7 %shard_map.67 = bf16[2,512,128]{2,1,0:T(8,128)(2,1)S(1)} custom-call(s32[4,2,8]{2,1,0:T(2,128)S(1)} %compare_select_fusion.21.where_ref, bf16[2,512,128]{2,1,0:T(8,128)(2,1)S(1)} %shard_map.66.refs_0_, bf16[2,512,128]{2,1,0:T(8,128)(2,1)S(1)} %collective-permute-done.35.refs_1_, bf16[2,512,128]{2,1,0:T(8,128)(2,1)S(1)} %collective-permute-done.36.refs_2_, ...), custom_call_target="tpu_custom_call" | custom-call | flops 1207959552 | bytes 9437184 | tf_op jit(solution)/shard_map/pallas_call | solution.py:83
  239.7 7.3 %collective-permute-start.44 = (bf16[512,128]{1,0:T(8,128)(2,1)S(1)}, bf16[512,128]{1,0:T(8,128)(2,1)S(1)}, u32[]{:S(2)}, u32[]{:S(2)}) collective-permute-start(bf16[512,128]{1,0:T(8,128)(2,1)S(1)} %get-tuple-element.20), channel_id=1, source_target_pairs={{0,16},{1,17},{2,18},{3,19},{4,20},{5,21},{6,22},{7,23},{8,24},{9,... | collective-permute-start | bytes 393224 | tf_op jit(solution)/shard_map/ppermute | solution.py:42
  (97 shorter events, 37.5 us)
Async XLA Ops:
  0.0 56.7 %copy-start = (s32[640]{0:T(1024)S(1)}, s32[640]{0:T(1024)}, u32[]{:S(2)}) copy-start(s32[640]{0:T(1024)} %param.11) | copy-start | bytes 7684
  0.0 77.4 %collective-permute-start.11 = (bf16[4,8,512,512]{3,2,1,0:T(8,128)(2,1)}, bf16[4,8,512,512]{3,2,1,0:T(8,128)(2,1)}, u32[]{:S(2)}, u32[]{:S(2)}) collective-permute-start(bf16[4,8,512,512]{3,2,1,0:T(8,128)(2,1)} %bitcast.43), channel_id=1, source_target_pairs={{0,16},{1,17},{2,18},{3,19},{4,20},{5,21},{6,22},{7,23},{8,24},{9,... | collective-permute-start | bytes 50331656 | tf_op jit(solution)/shard_map/ppermute | solution.py:42
  2.4 15.8 %collective-permute-start.1 = (bf16[512,128]{1,0:T(8,128)(2,1)S(1)}, bf16[512,128]{1,0:T(8,128)(2,1)S(1)}, u32[]{:S(2)}, u32[]{:S(2)}) collective-permute-start(bf16[512,128]{1,0:T(8,128)(2,1)S(1)} %broadcast_select_fusion.1), channel_id=1, source_target_pairs={{0,16},{1,17},{2,18},{3,19},{4,20},{5,21},{6,22},{7,23},{8,24},{9,... | collective-permute-start | bytes 393224 | tf_op jit(solution)/shard_map/ppermute | solution.py:42
  18.2 14.4 %collective-permute-start.2 = (bf16[2,512,128]{2,1,0:T(8,128)(2,1)S(1)}, bf16[2,512,128]{2,1,0:T(8,128)(2,1)S(1)}, u32[]{:S(2)}, u32[]{:S(2)}) collective-permute-start(bf16[2,512,128]{2,1,0:T(8,128)(2,1)S(1)} %pad_maximum_fusion.4.refs_0_), channel_id=1, source_target_pairs={{0,4},{1,5},{2,6},{3,7},{4,8},{5,9},{6,10},{7,11},{8,12},{9,13},{1... | collective-permute-start | bytes 786440 | tf_op jit(solution)/shard_map/ppermute | solution.py:42
  19.7 57.8 %collective-permute-start.12 = (bf16[4,512,512]{2,1,0:T(8,128)(2,1)}, bf16[4,512,512]{2,1,0:T(8,128)(2,1)S(1)}, u32[]{:S(2)}, u32[]{:S(2)}) collective-permute-start(bf16[4,512,512]{2,1,0:T(8,128)(2,1)} %bitcast.48), channel_id=1, source_target_pairs={{0,16},{1,17},{2,18},{3,19},{4,20},{5,21},{6,22},{7,23},{8,24},{9,... | collective-permute-start | bytes 6291464 | tf_op jit(solution)/shard_map/ppermute | solution.py:42
  20.0 18.3 %collective-permute-start.3 = (bf16[2,512,128]{2,1,0:T(8,128)(2,1)S(1)}, bf16[2,512,128]{2,1,0:T(8,128)(2,1)S(1)}, u32[]{:S(2)}, u32[]{:S(2)}) collective-permute-start(bf16[2,512,128]{2,1,0:T(8,128)(2,1)S(1)} %pad_maximum_fusion.4.refs_0_), channel_id=1, source_target_pairs={{0,12},{1,13},{2,14},{3,15},{4,0},{5,1},{6,2},{7,3},{8,4},{9,5},{1... | collective-permute-start | bytes 786440 | tf_op jit(solution)/shard_map/ppermute | solution.py:42
  22.7 6.9 %collective-permute-start = (s32[4,8]{1,0:T(4,128)}, s32[4,8]{1,0:T(4,128)S(1)}, u32[]{:S(2)}, u32[]{:S(2)}) collective-permute-start(s32[4,8]{1,0:T(4,128)} %bitcast.62), channel_id=1, source_target_pairs={{0,16},{1,17},{2,18},{3,19},{4,20},{5,21},{6,22},{7,23},{8,24},{9,... | collective-permute-start | bytes 392 | tf_op jit(solution)/shard_map/ppermute | solution.py:42
  29.6 10.1 %collective-permute-start.4 = (bf16[2,512,128]{2,1,0:T(8,128)(2,1)S(1)}, bf16[2,512,128]{2,1,0:T(8,128)(2,1)S(1)}, u32[]{:S(2)}, u32[]{:S(2)}) collective-permute-start(bf16[2,512,128]{2,1,0:T(8,128)(2,1)S(1)} %pad_maximum_fusion.4.refs_0_), channel_id=1, source_target_pairs={{0,8},{1,9},{2,10},{3,11},{4,12},{5,13},{6,14},{7,15},{8,0},{9,1},... | collective-permute-start | bytes 786440 | tf_op jit(solution)/shard_map/ppermute | solution.py:42
  32.6 9.8 %collective-permute-start.10 = (bf16[2,512,128]{2,1,0:T(8,128)(2,1)S(1)}, bf16[2,512,128]{2,1,0:T(8,128)(2,1)S(1)}, u32[]{:S(2)}, u32[]{:S(2)}) collective-permute-start(bf16[2,512,128]{2,1,0:T(8,128)(2,1)S(1)} %pad_maximum_fusion.4.refs_0_), channel_id=1, source_target_pairs={{0,64},{1,65},{2,66},{3,67},{4,68},{5,69},{6,70},{7,71},{8,72},{9,... | collective-permute-start | bytes 786440 | tf_op jit(solution)/shard_map/ppermute | solution.py:42
  38.3 15.8 %collective-permute-start.13 = (bf16[4,512,128]{2,1,0:T(8,128)(2,1)S(1)}, bf16[4,512,128]{2,1,0:T(8,128)(2,1)S(1)}, u32[]{:S(2)}, u32[]{:S(2)}) collective-permute-start(bf16[4,512,128]{2,1,0:T(8,128)(2,1)S(1)} %get-tuple-element.11), channel_id=1, source_target_pairs={{0,16},{1,17},{2,18},{3,19},{4,20},{5,21},{6,22},{7,23},{8,24},{9,... | collective-permute-start | bytes 1572872 | tf_op jit(solution)/shard_map/ppermute | solution.py:42
  39.7 9.1 %collective-permute-start.8 = (bf16[2,512,128]{2,1,0:T(8,128)(2,1)S(1)}, bf16[2,512,128]{2,1,0:T(8,128)(2,1)S(1)}, u32[]{:S(2)}, u32[]{:S(2)}) collective-permute-start(bf16[2,512,128]{2,1,0:T(8,128)(2,1)S(1)} %pad_maximum_fusion.4.refs_0_), channel_id=1, source_target_pairs={{0,32},{1,33},{2,34},{3,35},{4,36},{5,37},{6,38},{7,39},{8,40},{9,... | collective-permute-start | bytes 786440 | tf_op jit(solution)/shard_map/ppermute | solution.py:42
  42.5 7.8 %collective-permute-start.9 = (bf16[2,512,128]{2,1,0:T(8,128)(2,1)S(1)}, bf16[2,512,128]{2,1,0:T(8,128)(2,1)S(1)}, u32[]{:S(2)}, u32[]{:S(2)}) collective-permute-start(bf16[2,512,128]{2,1,0:T(8,128)(2,1)S(1)} %pad_maximum_fusion.4.refs_0_), channel_id=1, source_target_pairs={{0,96},{1,97},{2,98},{3,99},{4,100},{5,101},{6,102},{7,103},{8,104... | collective-permute-start | bytes 786440 | tf_op jit(solution)/shard_map/ppermute | solution.py:42
  49.6 26.7 %collective-permute-start.5 = (bf16[8,512,128]{2,1,0:T(8,128)(2,1)}, bf16[8,512,128]{2,1,0:T(8,128)(2,1)}, u32[]{:S(2)}, u32[]{:S(2)}) collective-permute-start(bf16[8,512,128]{2,1,0:T(8,128)(2,1)} %constant_dynamic-update-slice_fusion), channel_id=1, source_target_pairs={{0,1},{1,2},{2,3},{3,0},{4,5},{5,6},{6,7},{7,4},{8,9},{9,10},{10,1... | collective-permute-start | bytes 3145736 | tf_op jit(solution)/shard_map/ppermute | solution.py:42
  51.0 26.5 %collective-permute-start.6 = (bf16[8,512,128]{2,1,0:T(8,128)(2,1)}, bf16[8,512,128]{2,1,0:T(8,128)(2,1)}, u32[]{:S(2)}, u32[]{:S(2)}) collective-permute-start(bf16[8,512,128]{2,1,0:T(8,128)(2,1)} %constant_dynamic-update-slice_fusion), channel_id=1, source_target_pairs={{0,3},{1,0},{2,1},{3,2},{4,7},{5,4},{6,5},{7,6},{8,11},{9,8},{10,9... | collective-permute-start | bytes 3145736 | tf_op jit(solution)/shard_map/ppermute | solution.py:42
  54.9 22.5 %collective-permute-start.7 = (bf16[8,512,128]{2,1,0:T(8,128)(2,1)}, bf16[8,512,128]{2,1,0:T(8,128)(2,1)}, u32[]{:S(2)}, u32[]{:S(2)}) collective-permute-start(bf16[8,512,128]{2,1,0:T(8,128)(2,1)} %constant_dynamic-update-slice_fusion), channel_id=1, source_target_pairs={{0,2},{1,3},{2,0},{3,1},{4,6},{5,7},{6,4},{7,5},{8,10},{9,11},{10,... | collective-permute-start | bytes 3145736 | tf_op jit(solution)/shard_map/ppermute | solution.py:42
  86.7 47.3 %copy-start.5 = (bf16[4,1,1,512,512]{4,3,2,1,0:T(8,128)(2,1)S(1)}, bf16[4,1,1,512,512]{4,3,2,1,0:T(8,128)(2,1)}, u32[]{:S(2)}) copy-start(bf16[4,1,1,512,512]{4,3,2,1,0:T(8,128)(2,1)} %param.8) | copy-start | bytes 6291460
  95.8 6.8 %collective-permute-start.15 = (bf16[2,512,128]{2,1,0:T(8,128)(2,1)S(1)}, bf16[2,512,128]{2,1,0:T(8,128)(2,1)S(1)}, u32[]{:S(2)}, u32[]{:S(2)}) collective-permute-start(bf16[2,512,128]{2,1,0:T(8,128)(2,1)S(1)} %shard_map.64.refs_0_), channel_id=1, source_target_pairs={{0,4},{1,5},{2,6},{3,7},{4,8},{5,9},{6,10},{7,11},{8,12},{9,13},{1... | collective-permute-start | bytes 786440 | tf_op jit(solution)/shard_map/ppermute | solution.py:42
  96.4 8.3 %collective-permute-start.16 = (bf16[2,512,128]{2,1,0:T(8,128)(2,1)S(1)}, bf16[2,512,128]{2,1,0:T(8,128)(2,1)S(1)}, u32[]{:S(2)}, u32[]{:S(2)}) collective-permute-start(bf16[2,512,128]{2,1,0:T(8,128)(2,1)S(1)} %shard_map.64.refs_0_), channel_id=1, source_target_pairs={{0,12},{1,13},{2,14},{3,15},{4,0},{5,1},{6,2},{7,3},{8,4},{9,5},{1... | collective-permute-start | bytes 786440 | tf_op jit(solution)/shard_map/ppermute | solution.py:42
  98.6 7.0 %collective-permute-start.17 = (bf16[2,512,128]{2,1,0:T(8,128)(2,1)S(1)}, bf16[2,512,128]{2,1,0:T(8,128)(2,1)S(1)}, u32[]{:S(2)}, u32[]{:S(2)}) collective-permute-start(bf16[2,512,128]{2,1,0:T(8,128)(2,1)S(1)} %shard_map.64.refs_0_), channel_id=1, source_target_pairs={{0,8},{1,9},{2,10},{3,11},{4,12},{5,13},{6,14},{7,15},{8,0},{9,1},... | collective-permute-start | bytes 786440 | tf_op jit(solution)/shard_map/ppermute | solution.py:42
  105.7 18.9 %collective-permute-start.18 = (bf16[8,512,128]{2,1,0:T(8,128)(2,1)S(1)}, bf16[8,512,128]{2,1,0:T(8,128)(2,1)S(1)}, u32[]{:S(2)}, u32[]{:S(2)}) collective-permute-start(bf16[8,512,128]{2,1,0:T(8,128)(2,1)S(1)} %pad_maximum_fusion), channel_id=1, source_target_pairs={{0,1},{1,2},{2,3},{3,0},{4,5},{5,6},{6,7},{7,4},{8,9},{9,10},{10,1... | collective-permute-start | bytes 3145736 | tf_op jit(solution)/shard_map/ppermute | solution.py:42
  106.9 25.3 %collective-permute-start.19 = (bf16[8,512,128]{2,1,0:T(8,128)(2,1)S(1)}, bf16[8,512,128]{2,1,0:T(8,128)(2,1)S(1)}, u32[]{:S(2)}, u32[]{:S(2)}) collective-permute-start(bf16[8,512,128]{2,1,0:T(8,128)(2,1)S(1)} %pad_maximum_fusion), channel_id=1, source_target_pairs={{0,3},{1,0},{2,1},{3,2},{4,7},{5,4},{6,5},{7,6},{8,11},{9,8},{10,9... | collective-permute-start | bytes 3145736 | tf_op jit(solution)/shard_map/ppermute | solution.py:42
  109.2 24.8 %collective-permute-start.20 = (bf16[8,512,128]{2,1,0:T(8,128)(2,1)S(1)}, bf16[8,512,128]{2,1,0:T(8,128)(2,1)S(1)}, u32[]{:S(2)}, u32[]{:S(2)}) collective-permute-start(bf16[8,512,128]{2,1,0:T(8,128)(2,1)S(1)} %pad_maximum_fusion), channel_id=1, source_target_pairs={{0,2},{1,3},{2,0},{3,1},{4,6},{5,7},{6,4},{7,5},{8,10},{9,11},{10,... | collective-permute-start | bytes 3145736 | tf_op jit(solution)/shard_map/ppermute | solution.py:42
  110.3 7.2 %collective-permute-start.21 = (bf16[2,512,128]{2,1,0:T(8,128)(2,1)S(1)}, bf16[2,512,128]{2,1,0:T(8,128)(2,1)S(1)}, u32[]{:S(2)}, u32[]{:S(2)}) collective-permute-start(bf16[2,512,128]{2,1,0:T(8,128)(2,1)S(1)} %shard_map.64.refs_0_), channel_id=1, source_target_pairs={{0,32},{1,33},{2,34},{3,35},{4,36},{5,37},{6,38},{7,39},{8,40},{9,... | collective-permute-start | bytes 786440 | tf_op jit(solution)/shard_map/ppermute | solution.py:42
  111.0 7.5 %collective-permute-start.22 = (bf16[2,512,128]{2,1,0:T(8,128)(2,1)S(1)}, bf16[2,512,128]{2,1,0:T(8,128)(2,1)S(1)}, u32[]{:S(2)}, u32[]{:S(2)}) collective-permute-start(bf16[2,512,128]{2,1,0:T(8,128)(2,1)S(1)} %shard_map.64.refs_0_), channel_id=1, source_target_pairs={{0,96},{1,97},{2,98},{3,99},{4,100},{5,101},{6,102},{7,103},{8,104... | collective-permute-start | bytes 786440 | tf_op jit(solution)/shard_map/ppermute | solution.py:42
  117.5 7.1 %collective-permute-start.23 = (bf16[2,512,128]{2,1,0:T(8,128)(2,1)S(1)}, bf16[2,512,128]{2,1,0:T(8,128)(2,1)S(1)}, u32[]{:S(2)}, u32[]{:S(2)}) collective-permute-start(bf16[2,512,128]{2,1,0:T(8,128)(2,1)S(1)} %shard_map.64.refs_0_), channel_id=1, source_target_pairs={{0,64},{1,65},{2,66},{3,67},{4,68},{5,69},{6,70},{7,71},{8,72},{9,... | collective-permute-start | bytes 786440 | tf_op jit(solution)/shard_map/ppermute | solution.py:42
  147.5 6.5 %collective-permute-start.25 = (bf16[2,512,128]{2,1,0:T(8,128)(2,1)S(1)}, bf16[2,512,128]{2,1,0:T(8,128)(2,1)S(1)}, u32[]{:S(2)}, u32[]{:S(2)}) collective-permute-start(bf16[2,512,128]{2,1,0:T(8,128)(2,1)S(1)} %shard_map.65.refs_0_), channel_id=1, source_target_pairs={{0,4},{1,5},{2,6},{3,7},{4,8},{5,9},{6,10},{7,11},{8,12},{9,13},{1... | collective-permute-start | bytes 786440 | tf_op jit(solution)/shard_map/ppermute | solution.py:42
  148.1 8.2 %collective-permute-start.26 = (bf16[2,512,128]{2,1,0:T(8,128)(2,1)S(1)}, bf16[2,512,128]{2,1,0:T(8,128)(2,1)S(1)}, u32[]{:S(2)}, u32[]{:S(2)}) collective-permute-start(bf16[2,512,128]{2,1,0:T(8,128)(2,1)S(1)} %shard_map.65.refs_0_), channel_id=1, source_target_pairs={{0,12},{1,13},{2,14},{3,15},{4,0},{5,1},{6,2},{7,3},{8,4},{9,5},{1... | collective-permute-start | bytes 786440 | tf_op jit(solution)/shard_map/ppermute | solution.py:42
  150.2 7.4 %collective-permute-start.27 = (bf16[2,512,128]{2,1,0:T(8,128)(2,1)S(1)}, bf16[2,512,128]{2,1,0:T(8,128)(2,1)S(1)}, u32[]{:S(2)}, u32[]{:S(2)}) collective-permute-start(bf16[2,512,128]{2,1,0:T(8,128)(2,1)S(1)} %shard_map.65.refs_0_), channel_id=1, source_target_pairs={{0,8},{1,9},{2,10},{3,11},{4,12},{5,13},{6,14},{7,15},{8,0},{9,1},... | collective-permute-start | bytes 786440 | tf_op jit(solution)/shard_map/ppermute | solution.py:42
  157.7 19.7 %collective-permute-start.28 = (bf16[8,512,128]{2,1,0:T(8,128)(2,1)S(1)}, bf16[8,512,128]{2,1,0:T(8,128)(2,1)S(1)}, u32[]{:S(2)}, u32[]{:S(2)}) collective-permute-start(bf16[8,512,128]{2,1,0:T(8,128)(2,1)S(1)} %pad_maximum_fusion.1), channel_id=1, source_target_pairs={{0,1},{1,2},{2,3},{3,0},{4,5},{5,6},{6,7},{7,4},{8,9},{9,10},{10,1... | collective-permute-start | bytes 3145736 | tf_op jit(solution)/shard_map/ppermute | solution.py:42
  158.6 24.8 %collective-permute-start.29 = (bf16[8,512,128]{2,1,0:T(8,128)(2,1)S(1)}, bf16[8,512,128]{2,1,0:T(8,128)(2,1)S(1)}, u32[]{:S(2)}, u32[]{:S(2)}) collective-permute-start(bf16[8,512,128]{2,1,0:T(8,128)(2,1)S(1)} %pad_maximum_fusion.1), channel_id=1, source_target_pairs={{0,3},{1,0},{2,1},{3,2},{4,7},{5,4},{6,5},{7,6},{8,11},{9,8},{10,9... | collective-permute-start | bytes 3145736 | tf_op jit(solution)/shard_map/ppermute | solution.py:42
  160.5 23.8 %collective-permute-start.30 = (bf16[8,512,128]{2,1,0:T(8,128)(2,1)S(1)}, bf16[8,512,128]{2,1,0:T(8,128)(2,1)S(1)}, u32[]{:S(2)}, u32[]{:S(2)}) collective-permute-start(bf16[8,512,128]{2,1,0:T(8,128)(2,1)S(1)} %pad_maximum_fusion.1), channel_id=1, source_target_pairs={{0,2},{1,3},{2,0},{3,1},{4,6},{5,7},{6,4},{7,5},{8,10},{9,11},{10,... | collective-permute-start | bytes 3145736 | tf_op jit(solution)/shard_map/ppermute | solution.py:42
  160.6 7.5 %collective-permute-start.31 = (bf16[2,512,128]{2,1,0:T(8,128)(2,1)S(1)}, bf16[2,512,128]{2,1,0:T(8,128)(2,1)S(1)}, u32[]{:S(2)}, u32[]{:S(2)}) collective-permute-start(bf16[2,512,128]{2,1,0:T(8,128)(2,1)S(1)} %shard_map.65.refs_0_), channel_id=1, source_target_pairs={{0,32},{1,33},{2,34},{3,35},{4,36},{5,37},{6,38},{7,39},{8,40},{9,... | collective-permute-start | bytes 786440 | tf_op jit(solution)/shard_map/ppermute | solution.py:42
  161.5 7.5 %collective-permute-start.32 = (bf16[2,512,128]{2,1,0:T(8,128)(2,1)S(1)}, bf16[2,512,128]{2,1,0:T(8,128)(2,1)S(1)}, u32[]{:S(2)}, u32[]{:S(2)}) collective-permute-start(bf16[2,512,128]{2,1,0:T(8,128)(2,1)S(1)} %shard_map.65.refs_0_), channel_id=1, source_target_pairs={{0,96},{1,97},{2,98},{3,99},{4,100},{5,101},{6,102},{7,103},{8,104... | collective-permute-start | bytes 786440 | tf_op jit(solution)/shard_map/ppermute | solution.py:42
  168.0 9.5 %collective-permute-start.33 = (bf16[2,512,128]{2,1,0:T(8,128)(2,1)S(1)}, bf16[2,512,128]{2,1,0:T(8,128)(2,1)S(1)}, u32[]{:S(2)}, u32[]{:S(2)}) collective-permute-start(bf16[2,512,128]{2,1,0:T(8,128)(2,1)S(1)} %shard_map.65.refs_0_), channel_id=1, source_target_pairs={{0,64},{1,65},{2,66},{3,67},{4,68},{5,69},{6,70},{7,71},{8,72},{9,... | collective-permute-start | bytes 786440 | tf_op jit(solution)/shard_map/ppermute | solution.py:42
  192.0 6.5 %collective-permute-start.35 = (bf16[2,512,128]{2,1,0:T(8,128)(2,1)S(1)}, bf16[2,512,128]{2,1,0:T(8,128)(2,1)S(1)}, u32[]{:S(2)}, u32[]{:S(2)}) collective-permute-start(bf16[2,512,128]{2,1,0:T(8,128)(2,1)S(1)} %shard_map.66.refs_0_), channel_id=1, source_target_pairs={{0,4},{1,5},{2,6},{3,7},{4,8},{5,9},{6,10},{7,11},{8,12},{9,13},{1... | collective-permute-start | bytes 786440 | tf_op jit(solution)/shard_map/ppermute | solution.py:42
  192.9 7.9 %collective-permute-start.36 = (bf16[2,512,128]{2,1,0:T(8,128)(2,1)S(1)}, bf16[2,512,128]{2,1,0:T(8,128)(2,1)S(1)}, u32[]{:S(2)}, u32[]{:S(2)}) collective-permute-start(bf16[2,512,128]{2,1,0:T(8,128)(2,1)S(1)} %shard_map.66.refs_0_), channel_id=1, source_target_pairs={{0,12},{1,13},{2,14},{3,15},{4,0},{5,1},{6,2},{7,3},{8,4},{9,5},{1... | collective-permute-start | bytes 786440 | tf_op jit(solution)/shard_map/ppermute | solution.py:42
  194.7 7.3 %collective-permute-start.37 = (bf16[2,512,128]{2,1,0:T(8,128)(2,1)S(1)}, bf16[2,512,128]{2,1,0:T(8,128)(2,1)S(1)}, u32[]{:S(2)}, u32[]{:S(2)}) collective-permute-start(bf16[2,512,128]{2,1,0:T(8,128)(2,1)S(1)} %shard_map.66.refs_0_), channel_id=1, source_target_pairs={{0,8},{1,9},{2,10},{3,11},{4,12},{5,13},{6,14},{7,15},{8,0},{9,1},... | collective-permute-start | bytes 786440 | tf_op jit(solution)/shard_map/ppermute | solution.py:42
  202.1 29.9 %collective-permute-start.38 = (bf16[8,512,128]{2,1,0:T(8,128)(2,1)S(1)}, bf16[8,512,128]{2,1,0:T(8,128)(2,1)S(1)}, u32[]{:S(2)}, u32[]{:S(2)}) collective-permute-start(bf16[8,512,128]{2,1,0:T(8,128)(2,1)S(1)} %pad_maximum_fusion.2), channel_id=1, source_target_pairs={{0,1},{1,2},{2,3},{3,0},{4,5},{5,6},{6,7},{7,4},{8,9},{9,10},{10,1... | collective-permute-start | bytes 3145736 | tf_op jit(solution)/shard_map/ppermute | solution.py:42
  203.1 28.9 %collective-permute-start.39 = (bf16[8,512,128]{2,1,0:T(8,128)(2,1)S(1)}, bf16[8,512,128]{2,1,0:T(8,128)(2,1)S(1)}, u32[]{:S(2)}, u32[]{:S(2)}) collective-permute-start(bf16[8,512,128]{2,1,0:T(8,128)(2,1)S(1)} %pad_maximum_fusion.2), channel_id=1, source_target_pairs={{0,3},{1,0},{2,1},{3,2},{4,7},{5,4},{6,5},{7,6},{8,11},{9,8},{10,9... | collective-permute-start | bytes 3145736 | tf_op jit(solution)/shard_map/ppermute | solution.py:42
  204.9 27.1 %collective-permute-start.40 = (bf16[8,512,128]{2,1,0:T(8,128)(2,1)S(1)}, bf16[8,512,128]{2,1,0:T(8,128)(2,1)S(1)}, u32[]{:S(2)}, u32[]{:S(2)}) collective-permute-start(bf16[8,512,128]{2,1,0:T(8,128)(2,1)S(1)} %pad_maximum_fusion.2), channel_id=1, source_target_pairs={{0,2},{1,3},{2,0},{3,1},{4,6},{5,7},{6,4},{7,5},{8,10},{9,11},{10,... | collective-permute-start | bytes 3145736 | tf_op jit(solution)/shard_map/ppermute | solution.py:42
  205.9 13.9 %collective-permute-start.41 = (bf16[2,512,128]{2,1,0:T(8,128)(2,1)S(1)}, bf16[2,512,128]{2,1,0:T(8,128)(2,1)S(1)}, u32[]{:S(2)}, u32[]{:S(2)}) collective-permute-start(bf16[2,512,128]{2,1,0:T(8,128)(2,1)S(1)} %shard_map.66.refs_0_), channel_id=1, source_target_pairs={{0,32},{1,33},{2,34},{3,35},{4,36},{5,37},{6,38},{7,39},{8,40},{9,... | collective-permute-start | bytes 786440 | tf_op jit(solution)/shard_map/ppermute | solution.py:42
  206.5 10.3 %collective-permute-start.14 = (bf16[512,128]{1,0:T(8,128)(2,1)S(1)}, bf16[512,128]{1,0:T(8,128)(2,1)S(1)}, u32[]{:S(2)}, u32[]{:S(2)}) collective-permute-start(bf16[512,128]{1,0:T(8,128)(2,1)S(1)} %get-tuple-element.14), channel_id=1, source_target_pairs={{0,16},{1,17},{2,18},{3,19},{4,20},{5,21},{6,22},{7,23},{8,24},{9,... | collective-permute-start | bytes 393224 | tf_op jit(solution)/shard_map/ppermute | solution.py:42
  216.9 13.7 %collective-permute-start.42 = (bf16[2,512,128]{2,1,0:T(8,128)(2,1)S(1)}, bf16[2,512,128]{2,1,0:T(8,128)(2,1)S(1)}, u32[]{:S(2)}, u32[]{:S(2)}) collective-permute-start(bf16[2,512,128]{2,1,0:T(8,128)(2,1)S(1)} %shard_map.66.refs_0_), channel_id=1, source_target_pairs={{0,96},{1,97},{2,98},{3,99},{4,100},{5,101},{6,102},{7,103},{8,104... | collective-permute-start | bytes 786440 | tf_op jit(solution)/shard_map/ppermute | solution.py:42
  219.8 12.1 %collective-permute-start.43 = (bf16[2,512,128]{2,1,0:T(8,128)(2,1)S(1)}, bf16[2,512,128]{2,1,0:T(8,128)(2,1)S(1)}, u32[]{:S(2)}, u32[]{:S(2)}) collective-permute-start(bf16[2,512,128]{2,1,0:T(8,128)(2,1)S(1)} %shard_map.66.refs_0_), channel_id=1, source_target_pairs={{0,64},{1,65},{2,66},{3,67},{4,68},{5,69},{6,70},{7,71},{8,72},{9,... | collective-permute-start | bytes 786440 | tf_op jit(solution)/shard_map/ppermute | solution.py:42
  230.6 16.4 %collective-permute-start.24 = (bf16[512,128]{1,0:T(8,128)(2,1)S(1)}, bf16[512,128]{1,0:T(8,128)(2,1)S(1)}, u32[]{:S(2)}, u32[]{:S(2)}) collective-permute-start(bf16[512,128]{1,0:T(8,128)(2,1)S(1)} %get-tuple-element.16), channel_id=1, source_target_pairs={{0,16},{1,17},{2,18},{3,19},{4,20},{5,21},{6,22},{7,23},{8,24},{9,... | collective-permute-start | bytes 393224 | tf_op jit(solution)/shard_map/ppermute | solution.py:42
  232.0 15.1 %collective-permute-start.34 = (bf16[512,128]{1,0:T(8,128)(2,1)S(1)}, bf16[512,128]{1,0:T(8,128)(2,1)S(1)}, u32[]{:S(2)}, u32[]{:S(2)}) collective-permute-start(bf16[512,128]{1,0:T(8,128)(2,1)S(1)} %get-tuple-element.18), channel_id=1, source_target_pairs={{0,16},{1,17},{2,18},{3,19},{4,20},{5,21},{6,22},{7,23},{8,24},{9,... | collective-permute-start | bytes 393224 | tf_op jit(solution)/shard_map/ppermute | solution.py:42
  232.0 17.2 %copy-start.1 = (s32[640]{0:T(1024)S(1)}, s32[640]{0:T(1024)}, u32[]{:S(2)}) copy-start(s32[640]{0:T(1024)} %param.11) | copy-start | bytes 7684
  239.7 8.3 %collective-permute-start.44 = (bf16[512,128]{1,0:T(8,128)(2,1)S(1)}, bf16[512,128]{1,0:T(8,128)(2,1)S(1)}, u32[]{:S(2)}, u32[]{:S(2)}) collective-permute-start(bf16[512,128]{1,0:T(8,128)(2,1)S(1)} %get-tuple-element.20), channel_id=1, source_target_pairs={{0,16},{1,17},{2,18},{3,19},{4,20},{5,21},{6,22},{7,23},{8,24},{9,... | collective-permute-start | bytes 393224 | tf_op jit(solution)/shard_map/ppermute | solution.py:42
  (8 other events, 17.3 us)

commit v2 on v1

v2 whole, which is shorter than its diff:
```python
import functools

import jax
import jax.numpy as jnp
from jax import lax
from jax.experimental import pallas as pl
from jax.experimental.pallas import tpu as pltpu
from jax.sharding import PartitionSpec as P

AXES = ("gx", "gy")
SIDE = 4
SOON = 9


def pairs(move):
    out = []
    for z in range(SIDE):
        for c in range(2):
            for x in range(SIDE):
                for y in range(SIDE):
                    x2, y2, z2, c2 = move(x, y, z, c)
                    target = ((z2 % SIDE) * 2 + c2) * SIDE * SIDE + (x2 % SIDE) * SIDE + y2 % SIDE
                    out.append(((z * 2 + c) * SIDE * SIDE + x * SIDE + y, target))
    return out


def first(step):
    return pairs(lambda x, y, z, c: (x + step, y, z, c) if c == 0 else (x, y + step, z, c))


def second(step):
    return pairs(lambda x, y, z, c: (x, y + step, z, c) if c == 0 else (x + step, y, z, c))


def along_z(step):
    return pairs(lambda x, y, z, c: (x, y, z + step, c))


OTHER = pairs(lambda x, y, z, c: (x, y, z, 1 - c))


def send(value, route):
    return lax.ppermute(value, AXES, route)


VMEM = pl.BlockSpec(memory_space=pltpu.VMEM)
SMEM = pl.BlockSpec(memory_space=pltpu.SMEM)
ANYWHERE = pl.BlockSpec(memory_space=pl.ANY)
HBM = pl.BlockSpec(memory_space=pltpu.HBM)


def noise_kernel(core_ref, chol_ref, noise_ref, mine_ref, others_ref):
    half = mine_ref.shape[-1]
    product = jnp.dot(chol_ref[0], noise_ref[0], preferred_element_type=jnp.float32)

    @pl.when(core_ref[0] == 0)
    def _():
        mine_ref[0] = product[:, :half]
        others_ref[0] = product[:, half:]

    @pl.when(core_ref[0] != 0)
    def _():
        mine_ref[0] = product[:, half:]
        others_ref[0] = product[:, :half]


def noise_call(core, chol, noise):
    levels, rows, columns = noise.shape
    half = columns // 2
    part = pl.BlockSpec((1, rows, half), lambda l: (l, 0, 0))
    shape = jax.ShapeDtypeStruct((levels, rows, half), jnp.float32)
    return pl.pallas_call(
        noise_kernel,
        grid=(levels,),
        out_shape=(shape, shape),
        in_specs=[
            SMEM,
            pl.BlockSpec((1, rows, rows), lambda l: (l, 0, 0)),
            pl.BlockSpec((1, rows, columns), lambda l: (l, 0, 0)),
        ],
        out_specs=(part, part),
        cost_estimate=pl.CostEstimate(
            flops=2 * levels * rows * rows * columns, bytes_accessed=levels * rows * rows * 4, transcendentals=0
        ),
    )(core, chol, noise)


def pick(which, part, sources, target):
    def tree(low, high):
        if high - low == 1:
            target[...] = sources[low][part]
            return
        middle = (low + high) // 2

        @pl.when(which < middle)
        def _():
            tree(low, middle)

        @pl.when(which >= middle)
        def _():
            tree(middle, high)

    tree(0, len(sources))


def stage_kernel(level, token_ref, own_f, other_f, factor, sems):
    copies = [
        pltpu.make_async_copy(ref.at[level], factor.at[j], sems.at[j]) for j, ref in enumerate((own_f, other_f))
    ]
    for copy in copies:
        copy.start()
    for copy in copies:
        copy.wait()


def stage_call(level, token, own_f, other_f):
    return pl.pallas_call(
        functools.partial(stage_kernel, level),
        out_shape=jax.ShapeDtypeStruct((2,) + own_f.shape[1:], own_f.dtype),
        in_specs=[ANYWHERE, HBM, HBM],
        out_specs=VMEM,
        scratch_shapes=[pltpu.SemaphoreType.DMA((2,))],
        compiler_params=pltpu.CompilerParams(vmem_limit_bytes=24 * 1024 * 1024),
        cost_estimate=pl.CostEstimate(
            flops=0, bytes_accessed=2 * own_f.size // own_f.shape[0] * 2, transcendentals=0
        ),
    )(token, own_f, other_f)


def level_kernel(level, count, where_ref, *refs):
    sources = refs[:count]
    mine_ref, theirs_ref, factor, out_ref, give_ref, picked = refs[count:]

    def step(t, carry):
        code = where_ref[level, t // 8, t % 8]
        pick(code // 8, code % 8, sources, picked.at[t // 8, t % 8])
        return carry

    lax.fori_loop(0, 16, step, 0)
    for j, terms in enumerate((mine_ref, theirs_ref)):
        total = terms[level]
        for k in range(8):
            total += jnp.dot(factor[j, k], picked[j, k], preferred_element_type=jnp.float32)
        out_ref[j] = total.astype(out_ref.dtype)
    give_ref[...] = out_ref[1]


def level_call(level, where, sources, mine, theirs, factor):
    rows, columns = mine.shape[-2:]
    return pl.pallas_call(
        functools.partial(level_kernel, level, len(sources)),
        out_shape=(
            jax.ShapeDtypeStruct((2, rows, columns), jnp.bfloat16),
            jax.ShapeDtypeStruct((rows, columns), jnp.bfloat16),
        ),
        in_specs=[SMEM] + [VMEM] * (len(sources) + 3),
        out_specs=(VMEM, VMEM),
        scratch_shapes=[pltpu.VMEM((2, 8, rows, columns), jnp.bfloat16)],
        compiler_params=pltpu.CompilerParams(vmem_limit_bytes=24 * 1024 * 1024),
        cost_estimate=pl.CostEstimate(
            flops=2 * 16 * rows * rows * columns, bytes_accessed=16 * rows * columns * 2, transcendentals=0
        ),
    )(where, *sources, mine, theirs, factor)


def body(prior_draws, cond_factors, chol_factors, noise, neighbours, block_slot):
    my_gx = lax.axis_index("gx")
    my_gy = lax.axis_index("gy")
    z, core = my_gx // 2, my_gx % 2
    x, y = my_gy // SIDE, my_gy % SIDE
    half = prior_draws.shape[-1] // 2
    low = core == 0

    prior = prior_draws[0, 0]
    mine = jnp.where(low, prior[:, :half], prior[:, half:])
    others = jnp.where(low, prior[:, half:], prior[:, :half])
    draws = jnp.stack([mine, send(others, OTHER)])

    own_n = neighbours[:, 0, 0]
    both_n = jnp.stack([own_n, send(own_n, OTHER)], axis=1)

    device = block_slot[both_n] % (2 * SIDE**3)
    row, col = device // (SIDE * SIDE), device % (SIDE * SIDE)
    j = jnp.arange(2, dtype=jnp.int32)[None, :, None]
    my_row = z * 2 + jnp.where(j == 0, core, 1 - core)
    dx, dy = (col // SIDE - x) % SIDE, (col % SIDE - y) % SIDE
    dz = (row // 2 - z) % SIDE
    d1, d2 = jnp.where(low, dx, dy), jnp.where(low, dy, dx)

    def place(d):
        return jnp.where(d == 0, 0, jnp.where(d == 3, 1, jnp.where(d == 1, 2, 3)))

    p1, p2, p3 = place(d1), place(d2), place(dz)
    in_row = jnp.where(
        p2 == 0,
        p1 * 8 + j,
        jnp.where(
            p1 > 0,
            (SOON - 1 + p2) * 8 + (p1 - 1) * 2 + j,
            jnp.where(p2 < 3, (3 + p2) * 8 + j, (SOON + j) * 8 + 6),
        ),
    )
    in_col = jnp.where(p3 == 0, 0, 5 + p3) * 8 + jnp.where(row % 2 == core, 0, 1)
    where = jnp.where(row == my_row, in_row, in_col).astype(jnp.int32)

    own_f = cond_factors[:, 0, 0]
    chol, innovations = chol_factors[:, 0, 0], noise[:, 0, 0]

    kept, given, got = [], [], []
    for level in range(cond_factors.shape[0]):
        near = [send(draws, first(s)) for s in (2, 1, -1)]
        if level == 0:
            held, held_f, where = lax.optimization_barrier((draws, own_f, where))
            other_f = send(held_f, OTHER)
        else:
            swapped = send(given[-1], OTHER)
            held, swapped = lax.optimization_barrier((draws, swapped))
            got.append(swapped)
        along = [send(held, second(s)) for s in (1, -1)]
        line = jnp.concatenate([near[1], near[2], near[0]])
        if level == 0:
            line, chol, innovations = lax.optimization_barrier((line, chol, innovations))
            own_terms, sent_terms = noise_call(core.reshape(1), chol, innovations)
            other_terms = send(sent_terms, OTHER)
        held, line = lax.optimization_barrier((held, line))
        far = [
            send(line, second(2)),
            send(jnp.concatenate([line, along[0][:1]]), second(1)),
            send(jnp.concatenate([line, along[1][1:]]), second(-1)),
        ]
        column = [send(held, along_z(s)) for s in (2, 1, -1)]
        factor = stage_call(level, line, own_f, other_f)
        sources = [draws, near[1], near[2], near[0]] + along + [column[1], column[2], column[0]]
        sources += [far[1], far[2], far[0]]
        draws, give = level_call(level, where, sources, own_terms, other_terms, factor)
        kept.append(draws[0])
        given.append(give)
    got.append(send(given[-1], OTHER))
    left = jnp.stack(kept)
    right = jnp.stack(got)
    whole = jnp.where(low, jnp.concatenate([left, right], axis=-1), jnp.concatenate([right, left], axis=-1))
    return whole[:, None, None]


def solution(mesh):
    in_specs = (
        P("gx", "gy", None, None),
        P(None, "gx", "gy", None, None, None),
        P(None, "gx", "gy", None, None),
        P(None, "gx", "gy", None, None),
        P(None, "gx", "gy", None),
        P(),
    )
    out_specs = P(None, "gx", "gy", None, None)
    return jax.shard_map(body, mesh=mesh, in_specs=in_specs, out_specs=out_specs, check_vma=False)
```

time: 250 us -> 186 us (0.74)
  waiting for transfers between devices: 112 us -> 57.4 us
  starting transfers between devices: 74.9 us -> 69.1 us
  other arithmetic: 8.78 us -> 4.14 us
  local copies, waits for them, and re-layouts: 21.1 us -> 24.1 us
    ppermute x45 -> x52, waiting for transfers between devices: 112 us -> 57.4 us  [send(): return lax.ppermute(value, AXES, route)]
    ppermute x45 -> x52, starting transfers between devices: 74.9 us -> 69.1 us  [send(): return lax.ppermute(value, AXES, route)]
    unnamed x25 -> x14, local copies, waits for them, and re-layouts: 19.4 us -> 23.1 us
    pallas_call x4 -> x9, Pallas kernels: 32.1 us -> 30.2 us  [the longest x4 15.7 us: level_call(): pl.pallas_call(functools.partial(level_kernel, level, len(sources)), out_...]
  transfers between devices with their start and end apart: 45 -> 52, of which waited for: 26 -> 20; matrix products, arithmetic and copies ran while one was open for 4% -> 1% of each run, Pallas kernels for 3% -> 8%
where the time goes in v2:
time: 186 us; the launch traced here: 185 us
  starting transfers between devices  69.1 us (37%)
  waiting for transfers between devices  57.4 us (31%)
  Pallas kernels  30.2 us (16%)
  local copies, waits for them, and re-layouts  24.1 us (13%)
  other arithmetic  4.14 us (2%)
    ppermute x52, starting transfers between devices, send(): return lax.ppermute(value, AXES, route)  69.1 us
    ppermute x52, waiting for transfers between devices, send(): return lax.ppermute(value, AXES, route)  57.4 us
    unnamed x14, local copies, waits for them, and re-layouts  23.1 us
    pallas_call x4, Pallas kernels, level_call(): pl.pallas_call(functools.partial(level_kernel, level, len(sources)), out_...  15.7 us
    pallas_call x4, Pallas kernels, stage_call(): pl.pallas_call(functools.partial(stage_kernel, level), out_shape=jax.Shap...  9.97 us
    pallas_call x1, Pallas kernels, noise_call(): pl.pallas_call(noise_kernel, grid=(levels,), out_shape=(shape, shape), in...  4.5 us
  transfers between devices with their start and end apart: 52, of which 20 were waited for; matrix products, arithmetic and copies ran while one was open for 1% of the time, Pallas kernels for 8%

profile of v2, /device:TPU:1, one launch (start us, length us, event | category | flops | bytes accessed | tf_op | source)
XLA Modules:
  0.0 185.2 jit_solution(1035956752197966465)
XLA Ops:
  1.0 1.5 collective-permute-start
  8.7 1.6 collective-permute-start.4
  12.8 2.5 %collective-permute-start.6 = (bf16[2,512,128]{2,1,0:T(8,128)(2,1)S(1)}, bf16[2,512,128]{2,1,0:T(8,128)(2,1)S(1)}, u32[]{:S(2)}, u32[]{:S(2)}) collective-permute-start(bf16[2,512,128]{2,1,0:T(8,128)(2,1)S(1)} %pad_maximum_fusion.12.refs_0_), channel_id=1, source_target_pairs={{0,3},{1,0},{2,1},{3,2},{4,7},{5,4},{6,5},{7,6},{8,11},{9,8},{10,9... | collective-permute-start | bytes 786440 | tf_op jit(solution)/shard_map/ppermute | solution.py:43
  15.3 1.5 collective-permute-done.4.refs_3_
  16.9 1.7 collective-permute-start.7
  18.6 2.2 %collective-permute-start.8 = (bf16[2,512,128]{2,1,0:T(8,128)(2,1)S(1)}, bf16[2,512,128]{2,1,0:T(8,128)(2,1)S(1)}, u32[]{:S(2)}, u32[]{:S(2)}) collective-permute-start(bf16[2,512,128]{2,1,0:T(8,128)(2,1)S(1)} %pad_maximum_fusion.12.refs_0_), channel_id=1, source_target_pairs={{0,96},{1,97},{2,98},{3,99},{4,100},{5,101},{6,102},{7,103},{8,104... | collective-permute-start | bytes 786440 | tf_op jit(solution)/shard_map/ppermute | solution.py:43
  20.8 4.5 %shard_map.64 = (f32[4,512,128]{2,1,0:T(8,128)}, f32[4,512,128]{2,1,0:T(8,128)}) custom-call(s32[1]{0:T(128)} %bitcast.9.core_ref, bf16[4,512,512]{2,1,0:T(8,128)(2,1)} %bitcast.28, bf16[4,512,256]{2,1,0:T(8,128)(2,1)} %bitcast.29), custom_call_target="tpu_custom_call" | custom-call | flops 536870912 | bytes 4194304 | tf_op jit(solution)/shard_map/pallas_call | solution.py:72
  25.3 3.2 %collective-permute-start.13 = (f32[4,512,128]{2,1,0:T(8,128)}, f32[4,512,128]{2,1,0:T(8,128)S(1)}, u32[]{:S(2)}, u32[]{:S(2)}) collective-permute-start(f32[4,512,128]{2,1,0:T(8,128)} %get-tuple-element.43), channel_id=1, source_target_pairs={{0,16},{1,17},{2,18},{3,19},{4,20},{5,21},{6,22},{7,23},{8,24},{9,... | collective-permute-start | bytes 3145736 | tf_op jit(solution)/shard_map/ppermute | solution.py:43
  28.9 2.5 %collective-permute-start.11 = (bf16[7,512,128]{2,1,0:T(8,128)(2,1)S(1)}, bf16[7,512,128]{2,1,0:T(8,128)(2,1)S(1)}, u32[]{:S(2)}, u32[]{:S(2)}) collective-permute-start(bf16[7,512,128]{2,1,0:T(8,128)(2,1)S(1)} %get-tuple-element.71), channel_id=1, source_target_pairs={{0,3},{1,0},{2,1},{3,2},{4,7},{5,4},{6,5},{7,6},{8,11},{9,8},{10,9... | collective-permute-start | bytes 2752520 | tf_op jit(solution)/shard_map/ppermute | solution.py:43
  32.3 2.7 %collective-permute-start.9 = (bf16[2,512,128]{2,1,0:T(8,128)(2,1)S(1)}, bf16[2,512,128]{2,1,0:T(8,128)(2,1)S(1)}, u32[]{:S(2)}, u32[]{:S(2)}) collective-permute-start(bf16[2,512,128]{2,1,0:T(8,128)(2,1)S(1)} %pad_maximum_fusion.12.refs_0_), channel_id=1, source_target_pairs={{0,64},{1,65},{2,66},{3,67},{4,68},{5,69},{6,70},{7,71},{8,72},{9,... | collective-permute-start | bytes 786440 | tf_op jit(solution)/shard_map/ppermute | solution.py:43
  34.9 5.8 %copy-done.2 = bf16[4,1,1,8,512,512]{5,4,3,2,1,0:T(8,128)(2,1)S(1)} copy-done((bf16[4,1,1,8,512,512]{5,4,3,2,1,0:T(8,128)(2,1)S(1)}, bf16[4,1,1,8,512,512]{5,4,3,2,1,0:T(8,128)(2,1)}, u32[]{:S(2)}) %copy-start.2) | copy-done | bytes 16777240
  40.7 2.5 %shard_map.65.refs_14_ = bf16[2,8,512,512]{3,2,1,0:T(8,128)(2,1)S(1)} custom-call(bf16[6,512,128]{2,1,0:T(8,128)(2,1)S(1)} %pad_maximum_fusion.8.token_ref, bf16[4,8,512,512]{3,2,1,0:T(8,128)(2,1)S(1)} %bitcast.24, bf16[4,8,512,512]{3,2,1,0:T(8,128)(2,1)} %collective-permute-done.14.other_f), custom_call_target="tpu_custom_call" | custom-call | bytes 8388608 | tf_op jit(solution)/shard_map/pallas_call | solution.py:117
  43.2 7.1 %collective-permute-done.12.refs_11_ = bf16[6,512,128]{2,1,0:T(8,128)(2,1)S(1)} collective-permute-done((bf16[6,512,128]{2,1,0:T(8,128)(2,1)S(1)}, bf16[6,512,128]{2,1,0:T(8,128)(2,1)S(1)}, u32[]{:S(2)}, u32[]{:S(2)}) %collective-permute-start.12) | collective-permute-done | bytes 786464 | tf_op jit(solution)/shard_map/ppermute | solution.py:43
  50.9 3.9 %shard_map.66 = (bf16[2,512,128]{2,1,0:T(8,128)(2,1)S(1)}, bf16[512,128]{1,0:T(8,128)(2,1)S(1)}) custom-call(s32[4,2,8]{2,1,0:T(2,128)S(1)} %compare_select_fusion.23.where_ref, bf16[2,512,128]{2,1,0:T(8,128)(2,1)S(1)} %pad_maximum_fusion.12.refs_0_, bf16[2,512,128]{2,1,0:T(8,128)(2,1)S(1)} %collective-permute-done.2.refs_1_, ...), custom_call_target="tpu_custom_call" | custom-call | flops 1073741824 | bytes 2097152 | tf_op jit(solution)/shard_map/pallas_call | solution.py:150
  54.8 2.1 %collective-permute-start.15 = (bf16[2,512,128]{2,1,0:T(8,128)(2,1)S(1)}, bf16[2,512,128]{2,1,0:T(8,128)(2,1)S(1)}, u32[]{:S(2)}, u32[]{:S(2)}) collective-permute-start(bf16[2,512,128]{2,1,0:T(8,128)(2,1)S(1)} %get-tuple-element.48.refs_0_), channel_id=1, source_target_pairs={{0,4},{1,5},{2,6},{3,7},{4,8},{5,9},{6,10},{7,11},{8,12},{9,13},{1... | collective-permute-start | bytes 786440 | tf_op jit(solution)/shard_map/ppermute | solution.py:43
  56.9 1.7 collective-permute-start.16
  62.9 1.9 %collective-permute-start.20 = (bf16[2,512,128]{2,1,0:T(8,128)(2,1)S(1)}, bf16[2,512,128]{2,1,0:T(8,128)(2,1)S(1)}, u32[]{:S(2)}, u32[]{:S(2)}) collective-permute-start(bf16[2,512,128]{2,1,0:T(8,128)(2,1)S(1)} %get-tuple-element.48.refs_0_), channel_id=1, source_target_pairs={{0,3},{1,0},{2,1},{3,2},{4,7},{5,4},{6,5},{7,6},{8,11},{9,8},{10,9... | collective-permute-start | bytes 786440 | tf_op jit(solution)/shard_map/ppermute | solution.py:43
  64.8 1.7 collective-permute-done.17.refs_3_
  66.6 4.5 %collective-permute-done.19.refs_4_ = bf16[2,512,128]{2,1,0:T(8,128)(2,1)S(1)} collective-permute-done((bf16[2,512,128]{2,1,0:T(8,128)(2,1)S(1)}, bf16[2,512,128]{2,1,0:T(8,128)(2,1)S(1)}, u32[]{:S(2)}, u32[]{:S(2)}) %collective-permute-start.19) | collective-permute-done | bytes 262176 | tf_op jit(solution)/shard_map/ppermute | solution.py:43
  71.5 2.5 %collective-permute-start.25 = (bf16[7,512,128]{2,1,0:T(8,128)(2,1)S(1)}, bf16[7,512,128]{2,1,0:T(8,128)(2,1)S(1)}, u32[]{:S(2)}, u32[]{:S(2)}) collective-permute-start(bf16[7,512,128]{2,1,0:T(8,128)(2,1)S(1)} %get-tuple-element.69), channel_id=1, source_target_pairs={{0,3},{1,0},{2,1},{3,2},{4,7},{5,4},{6,5},{7,6},{8,11},{9,8},{10,9... | collective-permute-start | bytes 2752520 | tf_op jit(solution)/shard_map/ppermute | solution.py:43
  74.7 2.7 %collective-permute-start.22 = (bf16[2,512,128]{2,1,0:T(8,128)(2,1)S(1)}, bf16[2,512,128]{2,1,0:T(8,128)(2,1)S(1)}, u32[]{:S(2)}, u32[]{:S(2)}) collective-permute-start(bf16[2,512,128]{2,1,0:T(8,128)(2,1)S(1)} %get-tuple-element.48.refs_0_), channel_id=1, source_target_pairs={{0,96},{1,97},{2,98},{3,99},{4,100},{5,101},{6,102},{7,103},{8,104... | collective-permute-start | bytes 786440 | tf_op jit(solution)/shard_map/ppermute | solution.py:43
  77.4 6.2 %collective-permute-done.21.refs_6_ = bf16[2,512,128]{2,1,0:T(8,128)(2,1)S(1)} collective-permute-done((bf16[2,512,128]{2,1,0:T(8,128)(2,1)S(1)}, bf16[2,512,128]{2,1,0:T(8,128)(2,1)S(1)}, u32[]{:S(2)}, u32[]{:S(2)}) %collective-permute-start.21) | collective-permute-done | bytes 262176 | tf_op jit(solution)/shard_map/ppermute | solution.py:43
  83.9 5.8 %copy-done.3 = bf16[4,1,1,8,512,512]{5,4,3,2,1,0:T(8,128)(2,1)S(1)} copy-done((bf16[4,1,1,8,512,512]{5,4,3,2,1,0:T(8,128)(2,1)S(1)}, bf16[4,1,1,8,512,512]{5,4,3,2,1,0:T(8,128)(2,1)}, u32[]{:S(2)}) %copy-start.3) | copy-done | bytes 16777240
  89.7 2.5 %shard_map.67.refs_14_ = bf16[2,8,512,512]{3,2,1,0:T(8,128)(2,1)S(1)} custom-call(bf16[6,512,128]{2,1,0:T(8,128)(2,1)S(1)} %pad_maximum_fusion.9.token_ref, bf16[4,8,512,512]{3,2,1,0:T(8,128)(2,1)S(1)} %bitcast.25, bf16[4,8,512,512]{3,2,1,0:T(8,128)(2,1)} %collective-permute-done.14.other_f), custom_call_target="tpu_custom_call" | custom-call | bytes 8388608 | tf_op jit(solution)/shard_map/pallas_call | solution.py:117
  92.2 2.0 %collective-permute-done.26.refs_11_ = bf16[6,512,128]{2,1,0:T(8,128)(2,1)S(1)} collective-permute-done((bf16[6,512,128]{2,1,0:T(8,128)(2,1)S(1)}, bf16[6,512,128]{2,1,0:T(8,128)(2,1)S(1)}, u32[]{:S(2)}, u32[]{:S(2)}) %collective-permute-start.26) | collective-permute-done | bytes 786464 | tf_op jit(solution)/shard_map/ppermute | solution.py:43
  94.2 3.9 %shard_map.68 = (bf16[2,512,128]{2,1,0:T(8,128)(2,1)S(1)}, bf16[512,128]{1,0:T(8,128)(2,1)S(1)}) custom-call(s32[4,2,8]{2,1,0:T(2,128)S(1)} %compare_select_fusion.23.where_ref, bf16[2,512,128]{2,1,0:T(8,128)(2,1)S(1)} %get-tuple-element.48.refs_0_, bf16[2,512,128]{2,1,0:T(8,128)(2,1)S(1)} %collective-permute-done.15.refs_1_, ...), custom_call_target="tpu_custom_call" | custom-call | flops 1073741824 | bytes 2097152 | tf_op jit(solution)/shard_map/pallas_call | solution.py:150
  99.1 1.8 collective-permute-start.28
  101.0 3.3 %collective-permute-start.30 = (bf16[512,128]{1,0:T(8,128)(2,1)S(1)}, bf16[512,128]{1,0:T(8,128)(2,1)S(1)}, u32[]{:S(2)}, u32[]{:S(2)}) collective-permute-start(bf16[512,128]{1,0:T(8,128)(2,1)S(1)} %get-tuple-element.51), channel_id=1, source_target_pairs={{0,16},{1,17},{2,18},{3,19},{4,20},{5,21},{6,22},{7,23},{8,24},{9,... | collective-permute-start | bytes 393224 | tf_op jit(solution)/shard_map/ppermute | solution.py:43
  105.3 2.7 %collective-permute-start.32 = (bf16[2,512,128]{2,1,0:T(8,128)(2,1)S(1)}, bf16[2,512,128]{2,1,0:T(8,128)(2,1)S(1)}, u32[]{:S(2)}, u32[]{:S(2)}) collective-permute-start(bf16[2,512,128]{2,1,0:T(8,128)(2,1)S(1)} %get-tuple-element.53.refs_0_), channel_id=1, source_target_pairs={{0,3},{1,0},{2,1},{3,2},{4,7},{5,4},{6,5},{7,6},{8,11},{9,8},{10,9... | collective-permute-start | bytes 786440 | tf_op jit(solution)/shard_map/ppermute | solution.py:43
  108.1 4.8 %collective-permute-done.31.refs_4_ = bf16[2,512,128]{2,1,0:T(8,128)(2,1)S(1)} collective-permute-done((bf16[2,512,128]{2,1,0:T(8,128)(2,1)S(1)}, bf16[2,512,128]{2,1,0:T(8,128)(2,1)S(1)}, u32[]{:S(2)}, u32[]{:S(2)}) %collective-permute-start.31) | collective-permute-done | bytes 262176 | tf_op jit(solution)/shard_map/ppermute | solution.py:43
  113.5 2.3 %collective-permute-start.37 = (bf16[7,512,128]{2,1,0:T(8,128)(2,1)S(1)}, bf16[7,512,128]{2,1,0:T(8,128)(2,1)S(1)}, u32[]{:S(2)}, u32[]{:S(2)}) collective-permute-start(bf16[7,512,128]{2,1,0:T(8,128)(2,1)S(1)} %get-tuple-element.67), channel_id=1, source_target_pairs={{0,3},{1,0},{2,1},{3,2},{4,7},{5,4},{6,5},{7,6},{8,11},{9,8},{10,9... | collective-permute-start | bytes 2752520 | tf_op jit(solution)/shard_map/ppermute | solution.py:43
  116.1 2.7 %collective-permute-start.34 = (bf16[2,512,128]{2,1,0:T(8,128)(2,1)S(1)}, bf16[2,512,128]{2,1,0:T(8,128)(2,1)S(1)}, u32[]{:S(2)}, u32[]{:S(2)}) collective-permute-start(bf16[2,512,128]{2,1,0:T(8,128)(2,1)S(1)} %get-tuple-element.53.refs_0_), channel_id=1, source_target_pairs={{0,96},{1,97},{2,98},{3,99},{4,100},{5,101},{6,102},{7,103},{8,104... | collective-permute-start | bytes 786440 | tf_op jit(solution)/shard_map/ppermute | solution.py:43
  118.7 4.2 %collective-permute-done.33.refs_6_ = bf16[2,512,128]{2,1,0:T(8,128)(2,1)S(1)} collective-permute-done((bf16[2,512,128]{2,1,0:T(8,128)(2,1)S(1)}, bf16[2,512,128]{2,1,0:T(8,128)(2,1)S(1)}, u32[]{:S(2)}, u32[]{:S(2)}) %collective-permute-start.33) | collective-permute-done | bytes 262176 | tf_op jit(solution)/shard_map/ppermute | solution.py:43
  123.3 5.8 %copy-done.4 = bf16[4,1,1,8,512,512]{5,4,3,2,1,0:T(8,128)(2,1)S(1)} copy-done((bf16[4,1,1,8,512,512]{5,4,3,2,1,0:T(8,128)(2,1)S(1)}, bf16[4,1,1,8,512,512]{5,4,3,2,1,0:T(8,128)(2,1)}, u32[]{:S(2)}) %copy-start.4) | copy-done | bytes 16777240
  129.0 2.5 %shard_map.69.refs_14_ = bf16[2,8,512,512]{3,2,1,0:T(8,128)(2,1)S(1)} custom-call(bf16[6,512,128]{2,1,0:T(8,128)(2,1)S(1)} %pad_maximum_fusion.10.token_ref, bf16[4,8,512,512]{3,2,1,0:T(8,128)(2,1)S(1)} %bitcast.26, bf16[4,8,512,512]{3,2,1,0:T(8,128)(2,1)} %collective-permute-done.14.other_f), custom_call_target="tpu_custom_call" | custom-call | bytes 8388608 | tf_op jit(solution)/shard_map/pallas_call | solution.py:117
  131.6 4.0 %collective-permute-done.38.refs_11_ = bf16[6,512,128]{2,1,0:T(8,128)(2,1)S(1)} collective-permute-done((bf16[6,512,128]{2,1,0:T(8,128)(2,1)S(1)}, bf16[6,512,128]{2,1,0:T(8,128)(2,1)S(1)}, u32[]{:S(2)}, u32[]{:S(2)}) %collective-permute-start.38) | collective-permute-done | bytes 786464 | tf_op jit(solution)/shard_map/ppermute | solution.py:43
  135.6 3.9 %shard_map.70 = (bf16[2,512,128]{2,1,0:T(8,128)(2,1)S(1)}, bf16[512,128]{1,0:T(8,128)(2,1)S(1)}) custom-call(s32[4,2,8]{2,1,0:T(2,128)S(1)} %compare_select_fusion.23.where_ref, bf16[2,512,128]{2,1,0:T(8,128)(2,1)S(1)} %get-tuple-element.53.refs_0_, bf16[2,512,128]{2,1,0:T(8,128)(2,1)S(1)} %collective-permute-done.27.refs_1_, ...), custom_call_target="tpu_custom_call" | custom-call | flops 1073741824 | bytes 2097152 | tf_op jit(solution)/shard_map/pallas_call | solution.py:150
  140.4 1.8 collective-permute-start.40
  142.8 2.4 %collective-permute-start.42 = (bf16[512,128]{1,0:T(8,128)(2,1)S(1)}, bf16[512,128]{1,0:T(8,128)(2,1)S(1)}, u32[]{:S(2)}, u32[]{:S(2)}) collective-permute-start(bf16[512,128]{1,0:T(8,128)(2,1)S(1)} %get-tuple-element.56), channel_id=1, source_target_pairs={{0,16},{1,17},{2,18},{3,19},{4,20},{5,21},{6,22},{7,23},{8,24},{9,... | collective-permute-start | bytes 393224 | tf_op jit(solution)/shard_map/ppermute | solution.py:43
  146.7 2.1 %collective-permute-start.44 = (bf16[2,512,128]{2,1,0:T(8,128)(2,1)S(1)}, bf16[2,512,128]{2,1,0:T(8,128)(2,1)S(1)}, u32[]{:S(2)}, u32[]{:S(2)}) collective-permute-start(bf16[2,512,128]{2,1,0:T(8,128)(2,1)S(1)} %get-tuple-element.58.refs_0_), channel_id=1, source_target_pairs={{0,3},{1,0},{2,1},{3,2},{4,7},{5,4},{6,5},{7,6},{8,11},{9,8},{10,9... | collective-permute-start | bytes 786440 | tf_op jit(solution)/shard_map/ppermute | solution.py:43
  149.5 5.7 %collective-permute-done.43.refs_4_ = bf16[2,512,128]{2,1,0:T(8,128)(2,1)S(1)} collective-permute-done((bf16[2,512,128]{2,1,0:T(8,128)(2,1)S(1)}, bf16[2,512,128]{2,1,0:T(8,128)(2,1)S(1)}, u32[]{:S(2)}, u32[]{:S(2)}) %collective-permute-start.43) | collective-permute-done | bytes 262176 | tf_op jit(solution)/shard_map/ppermute | solution.py:43
  155.4 2.7 %collective-permute-start.49 = (bf16[7,512,128]{2,1,0:T(8,128)(2,1)S(1)}, bf16[7,512,128]{2,1,0:T(8,128)(2,1)S(1)}, u32[]{:S(2)}, u32[]{:S(2)}) collective-permute-start(bf16[7,512,128]{2,1,0:T(8,128)(2,1)S(1)} %get-tuple-element.65), channel_id=1, source_target_pairs={{0,3},{1,0},{2,1},{3,2},{4,7},{5,4},{6,5},{7,6},{8,11},{9,8},{10,9... | collective-permute-start | bytes 2752520 | tf_op jit(solution)/shard_map/ppermute | solution.py:43
  158.8 2.7 %collective-permute-start.46 = (bf16[2,512,128]{2,1,0:T(8,128)(2,1)S(1)}, bf16[2,512,128]{2,1,0:T(8,128)(2,1)S(1)}, u32[]{:S(2)}, u32[]{:S(2)}) collective-permute-start(bf16[2,512,128]{2,1,0:T(8,128)(2,1)S(1)} %get-tuple-element.58.refs_0_), channel_id=1, source_target_pairs={{0,96},{1,97},{2,98},{3,99},{4,100},{5,101},{6,102},{7,103},{8,104... | collective-permute-start | bytes 786440 | tf_op jit(solution)/shard_map/ppermute | solution.py:43
  161.5 6.2 %collective-permute-done.45.refs_6_ = bf16[2,512,128]{2,1,0:T(8,128)(2,1)S(1)} collective-permute-done((bf16[2,512,128]{2,1,0:T(8,128)(2,1)S(1)}, bf16[2,512,128]{2,1,0:T(8,128)(2,1)S(1)}, u32[]{:S(2)}, u32[]{:S(2)}) %collective-permute-start.45) | collective-permute-done | bytes 262176 | tf_op jit(solution)/shard_map/ppermute | solution.py:43
  168.0 5.8 %copy-done.5 = bf16[4,1,1,8,512,512]{5,4,3,2,1,0:T(8,128)(2,1)S(1)} copy-done((bf16[4,1,1,8,512,512]{5,4,3,2,1,0:T(8,128)(2,1)S(1)}, bf16[4,1,1,8,512,512]{5,4,3,2,1,0:T(8,128)(2,1)}, u32[]{:S(2)}) %copy-start.5) | copy-done | bytes 16777240
  173.8 2.5 %shard_map.71.refs_14_ = bf16[2,8,512,512]{3,2,1,0:T(8,128)(2,1)S(1)} custom-call(bf16[6,512,128]{2,1,0:T(8,128)(2,1)S(1)} %pad_maximum_fusion.11.token_ref, bf16[4,8,512,512]{3,2,1,0:T(8,128)(2,1)S(1)} %bitcast.27, bf16[4,8,512,512]{3,2,1,0:T(8,128)(2,1)} %collective-permute-done.14.other_f), custom_call_target="tpu_custom_call" | custom-call | bytes 8388608 | tf_op jit(solution)/shard_map/pallas_call | solution.py:117
  176.3 2.0 %collective-permute-done.50.refs_11_ = bf16[6,512,128]{2,1,0:T(8,128)(2,1)S(1)} collective-permute-done((bf16[6,512,128]{2,1,0:T(8,128)(2,1)S(1)}, bf16[6,512,128]{2,1,0:T(8,128)(2,1)S(1)}, u32[]{:S(2)}, u32[]{:S(2)}) %collective-permute-start.50) | collective-permute-done | bytes 786464 | tf_op jit(solution)/shard_map/ppermute | solution.py:43
  178.3 3.9 %shard_map.72 = (bf16[2,512,128]{2,1,0:T(8,128)(2,1)S(1)}, bf16[512,128]{1,0:T(8,128)(2,1)S(1)}) custom-call(s32[4,2,8]{2,1,0:T(2,128)S(1)} %compare_select_fusion.23.where_ref, bf16[2,512,128]{2,1,0:T(8,128)(2,1)S(1)} %get-tuple-element.58.refs_0_, bf16[2,512,128]{2,1,0:T(8,128)(2,1)S(1)} %collective-permute-done.39.refs_1_, ...), custom_call_target="tpu_custom_call" | custom-call | flops 1073741824 | bytes 2097152 | tf_op jit(solution)/shard_map/pallas_call | solution.py:150
  (112 shorter events, 28.6 us)
Async XLA Ops:
  1.0 4.6 %collective-permute-start = (bf16[512,128]{1,0:T(8,128)(2,1)S(1)}, bf16[512,128]{1,0:T(8,128)(2,1)S(1)}, u32[]{:S(2)}, u32[]{:S(2)}) collective-permute-start(bf16[512,128]{1,0:T(8,128)(2,1)S(1)} %get-tuple-element.74), channel_id=1, source_target_pairs={{0,16},{1,17},{2,18},{3,19},{4,20},{5,21},{6,22},{7,23},{8,24},{9,... | collective-permute-start | bytes 393224 | tf_op jit(solution)/shard_map/ppermute | solution.py:43
  5.7 26.6 %collective-permute-start.14 = (bf16[4,8,512,512]{3,2,1,0:T(8,128)(2,1)}, bf16[4,8,512,512]{3,2,1,0:T(8,128)(2,1)}, u32[]{:S(2)}, u32[]{:S(2)}) collective-permute-start(bf16[4,8,512,512]{3,2,1,0:T(8,128)(2,1)} %bitcast.23), channel_id=1, source_target_pairs={{0,16},{1,17},{2,18},{3,19},{4,20},{5,21},{6,22},{7,23},{8,24},{9,... | collective-permute-start | bytes 50331656 | tf_op jit(solution)/shard_map/ppermute | solution.py:43
  5.9 6.9 %collective-permute-start.2 = (bf16[2,512,128]{2,1,0:T(8,128)(2,1)S(1)}, bf16[2,512,128]{2,1,0:T(8,128)(2,1)S(1)}, u32[]{:S(2)}, u32[]{:S(2)}) collective-permute-start(bf16[2,512,128]{2,1,0:T(8,128)(2,1)S(1)} %pad_maximum_fusion.12.refs_0_), channel_id=1, source_target_pairs={{0,4},{1,5},{2,6},{3,7},{4,8},{5,9},{6,10},{7,11},{8,12},{9,13},{1... | collective-permute-start | bytes 786440 | tf_op jit(solution)/shard_map/ppermute | solution.py:43
  7.3 8.0 %collective-permute-start.3 = (bf16[2,512,128]{2,1,0:T(8,128)(2,1)S(1)}, bf16[2,512,128]{2,1,0:T(8,128)(2,1)S(1)}, u32[]{:S(2)}, u32[]{:S(2)}) collective-permute-start(bf16[2,512,128]{2,1,0:T(8,128)(2,1)S(1)} %pad_maximum_fusion.12.refs_0_), channel_id=1, source_target_pairs={{0,12},{1,13},{2,14},{3,15},{4,0},{5,1},{6,2},{7,3},{8,4},{9,5},{1... | collective-permute-start | bytes 786440 | tf_op jit(solution)/shard_map/ppermute | solution.py:43
  8.7 8.0 %collective-permute-start.4 = (bf16[2,512,128]{2,1,0:T(8,128)(2,1)S(1)}, bf16[2,512,128]{2,1,0:T(8,128)(2,1)S(1)}, u32[]{:S(2)}, u32[]{:S(2)}) collective-permute-start(bf16[2,512,128]{2,1,0:T(8,128)(2,1)S(1)} %pad_maximum_fusion.12.refs_0_), channel_id=1, source_target_pairs={{0,8},{1,9},{2,10},{3,11},{4,12},{5,13},{6,14},{7,15},{8,0},{9,1},... | collective-permute-start | bytes 786440 | tf_op jit(solution)/shard_map/ppermute | solution.py:43
  10.4 14.9 %collective-permute-start.5 = (bf16[2,512,128]{2,1,0:T(8,128)(2,1)S(1)}, bf16[2,512,128]{2,1,0:T(8,128)(2,1)S(1)}, u32[]{:S(2)}, u32[]{:S(2)}) collective-permute-start(bf16[2,512,128]{2,1,0:T(8,128)(2,1)S(1)} %pad_maximum_fusion.12.refs_0_), channel_id=1, source_target_pairs={{0,1},{1,2},{2,3},{3,0},{4,5},{5,6},{6,7},{7,4},{8,9},{9,10},{10,1... | collective-permute-start | bytes 786440 | tf_op jit(solution)/shard_map/ppermute | solution.py:43
  12.8 15.7 %collective-permute-start.6 = (bf16[2,512,128]{2,1,0:T(8,128)(2,1)S(1)}, bf16[2,512,128]{2,1,0:T(8,128)(2,1)S(1)}, u32[]{:S(2)}, u32[]{:S(2)}) collective-permute-start(bf16[2,512,128]{2,1,0:T(8,128)(2,1)S(1)} %pad_maximum_fusion.12.refs_0_), channel_id=1, source_target_pairs={{0,3},{1,0},{2,1},{3,2},{4,7},{5,4},{6,5},{7,6},{8,11},{9,8},{10,9... | collective-permute-start | bytes 786440 | tf_op jit(solution)/shard_map/ppermute | solution.py:43
  16.9 12.0 %collective-permute-start.7 = (bf16[2,512,128]{2,1,0:T(8,128)(2,1)S(1)}, bf16[2,512,128]{2,1,0:T(8,128)(2,1)S(1)}, u32[]{:S(2)}, u32[]{:S(2)}) collective-permute-start(bf16[2,512,128]{2,1,0:T(8,128)(2,1)S(1)} %pad_maximum_fusion.12.refs_0_), channel_id=1, source_target_pairs={{0,32},{1,33},{2,34},{3,35},{4,36},{5,37},{6,38},{7,39},{8,40},{9,... | collective-permute-start | bytes 786440 | tf_op jit(solution)/shard_map/ppermute | solution.py:43
  18.6 12.8 %collective-permute-start.8 = (bf16[2,512,128]{2,1,0:T(8,128)(2,1)S(1)}, bf16[2,512,128]{2,1,0:T(8,128)(2,1)S(1)}, u32[]{:S(2)}, u32[]{:S(2)}) collective-permute-start(bf16[2,512,128]{2,1,0:T(8,128)(2,1)S(1)} %pad_maximum_fusion.12.refs_0_), channel_id=1, source_target_pairs={{0,96},{1,97},{2,98},{3,99},{4,100},{5,101},{6,102},{7,103},{8,104... | collective-permute-start | bytes 786440 | tf_op jit(solution)/shard_map/ppermute | solution.py:43
  25.3 25.6 %collective-permute-start.13 = (f32[4,512,128]{2,1,0:T(8,128)}, f32[4,512,128]{2,1,0:T(8,128)S(1)}, u32[]{:S(2)}, u32[]{:S(2)}) collective-permute-start(f32[4,512,128]{2,1,0:T(8,128)} %get-tuple-element.43), channel_id=1, source_target_pairs={{0,16},{1,17},{2,18},{3,19},{4,20},{5,21},{6,22},{7,23},{8,24},{9,... | collective-permute-start | bytes 3145736 | tf_op jit(solution)/shard_map/ppermute | solution.py:43
  28.6 22.2 %collective-permute-start.10 = (bf16[7,512,128]{2,1,0:T(8,128)(2,1)S(1)}, bf16[7,512,128]{2,1,0:T(8,128)(2,1)S(1)}, u32[]{:S(2)}, u32[]{:S(2)}) collective-permute-start(bf16[7,512,128]{2,1,0:T(8,128)(2,1)S(1)} %get-tuple-element.72), channel_id=1, source_target_pairs={{0,1},{1,2},{2,3},{3,0},{4,5},{5,6},{6,7},{7,4},{8,9},{9,10},{10,1... | collective-permute-start | bytes 2752520 | tf_op jit(solution)/shard_map/ppermute | solution.py:43
  28.9 22.0 %collective-permute-start.11 = (bf16[7,512,128]{2,1,0:T(8,128)(2,1)S(1)}, bf16[7,512,128]{2,1,0:T(8,128)(2,1)S(1)}, u32[]{:S(2)}, u32[]{:S(2)}) collective-permute-start(bf16[7,512,128]{2,1,0:T(8,128)(2,1)S(1)} %get-tuple-element.71), channel_id=1, source_target_pairs={{0,3},{1,0},{2,1},{3,2},{4,7},{5,4},{6,5},{7,6},{8,11},{9,8},{10,9... | collective-permute-start | bytes 2752520 | tf_op jit(solution)/shard_map/ppermute | solution.py:43
  31.4 18.9 %collective-permute-start.12 = (bf16[6,512,128]{2,1,0:T(8,128)(2,1)S(1)}, bf16[6,512,128]{2,1,0:T(8,128)(2,1)S(1)}, u32[]{:S(2)}, u32[]{:S(2)}) collective-permute-start(bf16[6,512,128]{2,1,0:T(8,128)(2,1)S(1)} %pad_maximum_fusion.8.token_ref), channel_id=1, source_target_pairs={{0,2},{1,3},{2,0},{3,1},{4,6},{5,7},{6,4},{7,5},{8,10},{9,11},{10,... | collective-permute-start | bytes 2359304 | tf_op jit(solution)/shard_map/ppermute | solution.py:43
  32.3 11.0 %collective-permute-start.9 = (bf16[2,512,128]{2,1,0:T(8,128)(2,1)S(1)}, bf16[2,512,128]{2,1,0:T(8,128)(2,1)S(1)}, u32[]{:S(2)}, u32[]{:S(2)}) collective-permute-start(bf16[2,512,128]{2,1,0:T(8,128)(2,1)S(1)} %pad_maximum_fusion.12.refs_0_), channel_id=1, source_target_pairs={{0,64},{1,65},{2,66},{3,67},{4,68},{5,69},{6,70},{7,71},{8,72},{9,... | collective-permute-start | bytes 786440 | tf_op jit(solution)/shard_map/ppermute | solution.py:43
  54.8 9.9 %collective-permute-start.15 = (bf16[2,512,128]{2,1,0:T(8,128)(2,1)S(1)}, bf16[2,512,128]{2,1,0:T(8,128)(2,1)S(1)}, u32[]{:S(2)}, u32[]{:S(2)}) collective-permute-start(bf16[2,512,128]{2,1,0:T(8,128)(2,1)S(1)} %get-tuple-element.48.refs_0_), channel_id=1, source_target_pairs={{0,4},{1,5},{2,6},{3,7},{4,8},{5,9},{6,10},{7,11},{8,12},{9,13},{1... | collective-permute-start | bytes 786440 | tf_op jit(solution)/shard_map/ppermute | solution.py:43
  56.9 7.9 %collective-permute-start.16 = (bf16[2,512,128]{2,1,0:T(8,128)(2,1)S(1)}, bf16[2,512,128]{2,1,0:T(8,128)(2,1)S(1)}, u32[]{:S(2)}, u32[]{:S(2)}) collective-permute-start(bf16[2,512,128]{2,1,0:T(8,128)(2,1)S(1)} %get-tuple-element.48.refs_0_), channel_id=1, source_target_pairs={{0,12},{1,13},{2,14},{3,15},{4,0},{5,1},{6,2},{7,3},{8,4},{9,5},{1... | collective-permute-start | bytes 786440 | tf_op jit(solution)/shard_map/ppermute | solution.py:43
  58.6 8.0 %collective-permute-start.17 = (bf16[2,512,128]{2,1,0:T(8,128)(2,1)S(1)}, bf16[2,512,128]{2,1,0:T(8,128)(2,1)S(1)}, u32[]{:S(2)}, u32[]{:S(2)}) collective-permute-start(bf16[2,512,128]{2,1,0:T(8,128)(2,1)S(1)} %get-tuple-element.48.refs_0_), channel_id=1, source_target_pairs={{0,8},{1,9},{2,10},{3,11},{4,12},{5,13},{6,14},{7,15},{8,0},{9,1},... | collective-permute-start | bytes 786440 | tf_op jit(solution)/shard_map/ppermute | solution.py:43
  62.1 9.0 %collective-permute-start.19 = (bf16[2,512,128]{2,1,0:T(8,128)(2,1)S(1)}, bf16[2,512,128]{2,1,0:T(8,128)(2,1)S(1)}, u32[]{:S(2)}, u32[]{:S(2)}) collective-permute-start(bf16[2,512,128]{2,1,0:T(8,128)(2,1)S(1)} %get-tuple-element.48.refs_0_), channel_id=1, source_target_pairs={{0,1},{1,2},{2,3},{3,0},{4,5},{5,6},{6,7},{7,4},{8,9},{9,10},{10,1... | collective-permute-start | bytes 786440 | tf_op jit(solution)/shard_map/ppermute | solution.py:43
  62.9 8.2 %collective-permute-start.20 = (bf16[2,512,128]{2,1,0:T(8,128)(2,1)S(1)}, bf16[2,512,128]{2,1,0:T(8,128)(2,1)S(1)}, u32[]{:S(2)}, u32[]{:S(2)}) collective-permute-start(bf16[2,512,128]{2,1,0:T(8,128)(2,1)S(1)} %get-tuple-element.48.refs_0_), channel_id=1, source_target_pairs={{0,3},{1,0},{2,1},{3,2},{4,7},{5,4},{6,5},{7,6},{8,11},{9,8},{10,9... | collective-permute-start | bytes 786440 | tf_op jit(solution)/shard_map/ppermute | solution.py:43
  71.3 23.0 %collective-permute-start.24 = (bf16[7,512,128]{2,1,0:T(8,128)(2,1)S(1)}, bf16[7,512,128]{2,1,0:T(8,128)(2,1)S(1)}, u32[]{:S(2)}, u32[]{:S(2)}) collective-permute-start(bf16[7,512,128]{2,1,0:T(8,128)(2,1)S(1)} %get-tuple-element.70), channel_id=1, source_target_pairs={{0,1},{1,2},{2,3},{3,0},{4,5},{5,6},{6,7},{7,4},{8,9},{9,10},{10,1... | collective-permute-start | bytes 2752520 | tf_op jit(solution)/shard_map/ppermute | solution.py:43
  71.5 22.7 %collective-permute-start.25 = (bf16[7,512,128]{2,1,0:T(8,128)(2,1)S(1)}, bf16[7,512,128]{2,1,0:T(8,128)(2,1)S(1)}, u32[]{:S(2)}, u32[]{:S(2)}) collective-permute-start(bf16[7,512,128]{2,1,0:T(8,128)(2,1)S(1)} %get-tuple-element.69), channel_id=1, source_target_pairs={{0,3},{1,0},{2,1},{3,2},{4,7},{5,4},{6,5},{7,6},{8,11},{9,8},{10,9... | collective-permute-start | bytes 2752520 | tf_op jit(solution)/shard_map/ppermute | solution.py:43
  74.0 20.2 %collective-permute-start.26 = (bf16[6,512,128]{2,1,0:T(8,128)(2,1)S(1)}, bf16[6,512,128]{2,1,0:T(8,128)(2,1)S(1)}, u32[]{:S(2)}, u32[]{:S(2)}) collective-permute-start(bf16[6,512,128]{2,1,0:T(8,128)(2,1)S(1)} %pad_maximum_fusion.9.token_ref), channel_id=1, source_target_pairs={{0,2},{1,3},{2,0},{3,1},{4,6},{5,7},{6,4},{7,5},{8,10},{9,11},{10,... | collective-permute-start | bytes 2359304 | tf_op jit(solution)/shard_map/ppermute | solution.py:43
  74.7 8.9 %collective-permute-start.21 = (bf16[2,512,128]{2,1,0:T(8,128)(2,1)S(1)}, bf16[2,512,128]{2,1,0:T(8,128)(2,1)S(1)}, u32[]{:S(2)}, u32[]{:S(2)}) collective-permute-start(bf16[2,512,128]{2,1,0:T(8,128)(2,1)S(1)} %get-tuple-element.48.refs_0_), channel_id=1, source_target_pairs={{0,32},{1,33},{2,34},{3,35},{4,36},{5,37},{6,38},{7,39},{8,40},{9,... | collective-permute-start | bytes 786440 | tf_op jit(solution)/shard_map/ppermute | solution.py:43
  74.7 17.4 %collective-permute-start.22 = (bf16[2,512,128]{2,1,0:T(8,128)(2,1)S(1)}, bf16[2,512,128]{2,1,0:T(8,128)(2,1)S(1)}, u32[]{:S(2)}, u32[]{:S(2)}) collective-permute-start(bf16[2,512,128]{2,1,0:T(8,128)(2,1)S(1)} %get-tuple-element.48.refs_0_), channel_id=1, source_target_pairs={{0,96},{1,97},{2,98},{3,99},{4,100},{5,101},{6,102},{7,103},{8,104... | collective-permute-start | bytes 786440 | tf_op jit(solution)/shard_map/ppermute | solution.py:43
  83.6 8.6 %collective-permute-start.23 = (bf16[2,512,128]{2,1,0:T(8,128)(2,1)S(1)}, bf16[2,512,128]{2,1,0:T(8,128)(2,1)S(1)}, u32[]{:S(2)}, u32[]{:S(2)}) collective-permute-start(bf16[2,512,128]{2,1,0:T(8,128)(2,1)S(1)} %get-tuple-element.48.refs_0_), channel_id=1, source_target_pairs={{0,64},{1,65},{2,66},{3,67},{4,68},{5,69},{6,70},{7,71},{8,72},{9,... | collective-permute-start | bytes 786440 | tf_op jit(solution)/shard_map/ppermute | solution.py:43
  98.2 9.8 %collective-permute-start.27 = (bf16[2,512,128]{2,1,0:T(8,128)(2,1)S(1)}, bf16[2,512,128]{2,1,0:T(8,128)(2,1)S(1)}, u32[]{:S(2)}, u32[]{:S(2)}) collective-permute-start(bf16[2,512,128]{2,1,0:T(8,128)(2,1)S(1)} %get-tuple-element.53.refs_0_), channel_id=1, source_target_pairs={{0,4},{1,5},{2,6},{3,7},{4,8},{5,9},{6,10},{7,11},{8,12},{9,13},{1... | collective-permute-start | bytes 786440 | tf_op jit(solution)/shard_map/ppermute | solution.py:43
  99.1 8.9 %collective-permute-start.28 = (bf16[2,512,128]{2,1,0:T(8,128)(2,1)S(1)}, bf16[2,512,128]{2,1,0:T(8,128)(2,1)S(1)}, u32[]{:S(2)}, u32[]{:S(2)}) collective-permute-start(bf16[2,512,128]{2,1,0:T(8,128)(2,1)S(1)} %get-tuple-element.53.refs_0_), channel_id=1, source_target_pairs={{0,12},{1,13},{2,14},{3,15},{4,0},{5,1},{6,2},{7,3},{8,4},{9,5},{1... | collective-permute-start | bytes 786440 | tf_op jit(solution)/shard_map/ppermute | solution.py:43
  100.9 7.0 %collective-permute-start.29 = (bf16[2,512,128]{2,1,0:T(8,128)(2,1)S(1)}, bf16[2,512,128]{2,1,0:T(8,128)(2,1)S(1)}, u32[]{:S(2)}, u32[]{:S(2)}) collective-permute-start(bf16[2,512,128]{2,1,0:T(8,128)(2,1)S(1)} %get-tuple-element.53.refs_0_), channel_id=1, source_target_pairs={{0,8},{1,9},{2,10},{3,11},{4,12},{5,13},{6,14},{7,15},{8,0},{9,1},... | collective-permute-start | bytes 786440 | tf_op jit(solution)/shard_map/ppermute | solution.py:43
  101.0 4.3 %collective-permute-start.30 = (bf16[512,128]{1,0:T(8,128)(2,1)S(1)}, bf16[512,128]{1,0:T(8,128)(2,1)S(1)}, u32[]{:S(2)}, u32[]{:S(2)}) collective-permute-start(bf16[512,128]{1,0:T(8,128)(2,1)S(1)} %get-tuple-element.51), channel_id=1, source_target_pairs={{0,16},{1,17},{2,18},{3,19},{4,20},{5,21},{6,22},{7,23},{8,24},{9,... | collective-permute-start | bytes 393224 | tf_op jit(solution)/shard_map/ppermute | solution.py:43
  105.3 7.5 %collective-permute-start.31 = (bf16[2,512,128]{2,1,0:T(8,128)(2,1)S(1)}, bf16[2,512,128]{2,1,0:T(8,128)(2,1)S(1)}, u32[]{:S(2)}, u32[]{:S(2)}) collective-permute-start(bf16[2,512,128]{2,1,0:T(8,128)(2,1)S(1)} %get-tuple-element.53.refs_0_), channel_id=1, source_target_pairs={{0,1},{1,2},{2,3},{3,0},{4,5},{5,6},{6,7},{7,4},{8,9},{9,10},{10,1... | collective-permute-start | bytes 786440 | tf_op jit(solution)/shard_map/ppermute | solution.py:43
  105.3 7.6 %collective-permute-start.32 = (bf16[2,512,128]{2,1,0:T(8,128)(2,1)S(1)}, bf16[2,512,128]{2,1,0:T(8,128)(2,1)S(1)}, u32[]{:S(2)}, u32[]{:S(2)}) collective-permute-start(bf16[2,512,128]{2,1,0:T(8,128)(2,1)S(1)} %get-tuple-element.53.refs_0_), channel_id=1, source_target_pairs={{0,3},{1,0},{2,1},{3,2},{4,7},{5,4},{6,5},{7,6},{8,11},{9,8},{10,9... | collective-permute-start | bytes 786440 | tf_op jit(solution)/shard_map/ppermute | solution.py:43
  113.0 22.6 %collective-permute-start.36 = (bf16[7,512,128]{2,1,0:T(8,128)(2,1)S(1)}, bf16[7,512,128]{2,1,0:T(8,128)(2,1)S(1)}, u32[]{:S(2)}, u32[]{:S(2)}) collective-permute-start(bf16[7,512,128]{2,1,0:T(8,128)(2,1)S(1)} %get-tuple-element.68), channel_id=1, source_target_pairs={{0,1},{1,2},{2,3},{3,0},{4,5},{5,6},{6,7},{7,4},{8,9},{9,10},{10,1... | collective-permute-start | bytes 2752520 | tf_op jit(solution)/shard_map/ppermute | solution.py:43
  113.5 22.1 %collective-permute-start.37 = (bf16[7,512,128]{2,1,0:T(8,128)(2,1)S(1)}, bf16[7,512,128]{2,1,0:T(8,128)(2,1)S(1)}, u32[]{:S(2)}, u32[]{:S(2)}) collective-permute-start(bf16[7,512,128]{2,1,0:T(8,128)(2,1)S(1)} %get-tuple-element.67), channel_id=1, source_target_pairs={{0,3},{1,0},{2,1},{3,2},{4,7},{5,4},{6,5},{7,6},{8,11},{9,8},{10,9... | collective-permute-start | bytes 2752520 | tf_op jit(solution)/shard_map/ppermute | solution.py:43
  115.8 19.8 %collective-permute-start.38 = (bf16[6,512,128]{2,1,0:T(8,128)(2,1)S(1)}, bf16[6,512,128]{2,1,0:T(8,128)(2,1)S(1)}, u32[]{:S(2)}, u32[]{:S(2)}) collective-permute-start(bf16[6,512,128]{2,1,0:T(8,128)(2,1)S(1)} %pad_maximum_fusion.10.token_ref), channel_id=1, source_target_pairs={{0,2},{1,3},{2,0},{3,1},{4,6},{5,7},{6,4},{7,5},{8,10},{9,11},{10,... | collective-permute-start | bytes 2359304 | tf_op jit(solution)/shard_map/ppermute | solution.py:43
  116.1 6.9 %collective-permute-start.33 = (bf16[2,512,128]{2,1,0:T(8,128)(2,1)S(1)}, bf16[2,512,128]{2,1,0:T(8,128)(2,1)S(1)}, u32[]{:S(2)}, u32[]{:S(2)}) collective-permute-start(bf16[2,512,128]{2,1,0:T(8,128)(2,1)S(1)} %get-tuple-element.53.refs_0_), channel_id=1, source_target_pairs={{0,32},{1,33},{2,34},{3,35},{4,36},{5,37},{6,38},{7,39},{8,40},{9,... | collective-permute-start | bytes 786440 | tf_op jit(solution)/shard_map/ppermute | solution.py:43
  116.1 15.5 %collective-permute-start.34 = (bf16[2,512,128]{2,1,0:T(8,128)(2,1)S(1)}, bf16[2,512,128]{2,1,0:T(8,128)(2,1)S(1)}, u32[]{:S(2)}, u32[]{:S(2)}) collective-permute-start(bf16[2,512,128]{2,1,0:T(8,128)(2,1)S(1)} %get-tuple-element.53.refs_0_), channel_id=1, source_target_pairs={{0,96},{1,97},{2,98},{3,99},{4,100},{5,101},{6,102},{7,103},{8,104... | collective-permute-start | bytes 786440 | tf_op jit(solution)/shard_map/ppermute | solution.py:43
  123.0 8.6 %collective-permute-start.35 = (bf16[2,512,128]{2,1,0:T(8,128)(2,1)S(1)}, bf16[2,512,128]{2,1,0:T(8,128)(2,1)S(1)}, u32[]{:S(2)}, u32[]{:S(2)}) collective-permute-start(bf16[2,512,128]{2,1,0:T(8,128)(2,1)S(1)} %get-tuple-element.53.refs_0_), channel_id=1, source_target_pairs={{0,64},{1,65},{2,66},{3,67},{4,68},{5,69},{6,70},{7,71},{8,72},{9,... | collective-permute-start | bytes 786440 | tf_op jit(solution)/shard_map/ppermute | solution.py:43
  139.5 9.4 %collective-permute-start.39 = (bf16[2,512,128]{2,1,0:T(8,128)(2,1)S(1)}, bf16[2,512,128]{2,1,0:T(8,128)(2,1)S(1)}, u32[]{:S(2)}, u32[]{:S(2)}) collective-permute-start(bf16[2,512,128]{2,1,0:T(8,128)(2,1)S(1)} %get-tuple-element.58.refs_0_), channel_id=1, source_target_pairs={{0,4},{1,5},{2,6},{3,7},{4,8},{5,9},{6,10},{7,11},{8,12},{9,13},{1... | collective-permute-start | bytes 786440 | tf_op jit(solution)/shard_map/ppermute | solution.py:43
  140.4 8.5 %collective-permute-start.40 = (bf16[2,512,128]{2,1,0:T(8,128)(2,1)S(1)}, bf16[2,512,128]{2,1,0:T(8,128)(2,1)S(1)}, u32[]{:S(2)}, u32[]{:S(2)}) collective-permute-start(bf16[2,512,128]{2,1,0:T(8,128)(2,1)S(1)} %get-tuple-element.58.refs_0_), channel_id=1, source_target_pairs={{0,12},{1,13},{2,14},{3,15},{4,0},{5,1},{6,2},{7,3},{8,4},{9,5},{1... | collective-permute-start | bytes 786440 | tf_op jit(solution)/shard_map/ppermute | solution.py:43
  142.2 7.1 %collective-permute-start.41 = (bf16[2,512,128]{2,1,0:T(8,128)(2,1)S(1)}, bf16[2,512,128]{2,1,0:T(8,128)(2,1)S(1)}, u32[]{:S(2)}, u32[]{:S(2)}) collective-permute-start(bf16[2,512,128]{2,1,0:T(8,128)(2,1)S(1)} %get-tuple-element.58.refs_0_), channel_id=1, source_target_pairs={{0,8},{1,9},{2,10},{3,11},{4,12},{5,13},{6,14},{7,15},{8,0},{9,1},... | collective-permute-start | bytes 786440 | tf_op jit(solution)/shard_map/ppermute | solution.py:43
  146.2 9.0 %collective-permute-start.43 = (bf16[2,512,128]{2,1,0:T(8,128)(2,1)S(1)}, bf16[2,512,128]{2,1,0:T(8,128)(2,1)S(1)}, u32[]{:S(2)}, u32[]{:S(2)}) collective-permute-start(bf16[2,512,128]{2,1,0:T(8,128)(2,1)S(1)} %get-tuple-element.58.refs_0_), channel_id=1, source_target_pairs={{0,1},{1,2},{2,3},{3,0},{4,5},{5,6},{6,7},{7,4},{8,9},{9,10},{10,1... | collective-permute-start | bytes 786440 | tf_op jit(solution)/shard_map/ppermute | solution.py:43
  146.7 8.4 %collective-permute-start.44 = (bf16[2,512,128]{2,1,0:T(8,128)(2,1)S(1)}, bf16[2,512,128]{2,1,0:T(8,128)(2,1)S(1)}, u32[]{:S(2)}, u32[]{:S(2)}) collective-permute-start(bf16[2,512,128]{2,1,0:T(8,128)(2,1)S(1)} %get-tuple-element.58.refs_0_), channel_id=1, source_target_pairs={{0,3},{1,0},{2,1},{3,2},{4,7},{5,4},{6,5},{7,6},{8,11},{9,8},{10,9... | collective-permute-start | bytes 786440 | tf_op jit(solution)/shard_map/ppermute | solution.py:43
  155.3 23.0 %collective-permute-start.48 = (bf16[7,512,128]{2,1,0:T(8,128)(2,1)S(1)}, bf16[7,512,128]{2,1,0:T(8,128)(2,1)S(1)}, u32[]{:S(2)}, u32[]{:S(2)}) collective-permute-start(bf16[7,512,128]{2,1,0:T(8,128)(2,1)S(1)} %get-tuple-element.66), channel_id=1, source_target_pairs={{0,1},{1,2},{2,3},{3,0},{4,5},{5,6},{6,7},{7,4},{8,9},{9,10},{10,1... | collective-permute-start | bytes 2752520 | tf_op jit(solution)/shard_map/ppermute | solution.py:43
  155.4 22.9 %collective-permute-start.49 = (bf16[7,512,128]{2,1,0:T(8,128)(2,1)S(1)}, bf16[7,512,128]{2,1,0:T(8,128)(2,1)S(1)}, u32[]{:S(2)}, u32[]{:S(2)}) collective-permute-start(bf16[7,512,128]{2,1,0:T(8,128)(2,1)S(1)} %get-tuple-element.65), channel_id=1, source_target_pairs={{0,3},{1,0},{2,1},{3,2},{4,7},{5,4},{6,5},{7,6},{8,11},{9,8},{10,9... | collective-permute-start | bytes 2752520 | tf_op jit(solution)/shard_map/ppermute | solution.py:43
  158.1 20.2 %collective-permute-start.50 = (bf16[6,512,128]{2,1,0:T(8,128)(2,1)S(1)}, bf16[6,512,128]{2,1,0:T(8,128)(2,1)S(1)}, u32[]{:S(2)}, u32[]{:S(2)}) collective-permute-start(bf16[6,512,128]{2,1,0:T(8,128)(2,1)S(1)} %pad_maximum_fusion.11.token_ref), channel_id=1, source_target_pairs={{0,2},{1,3},{2,0},{3,1},{4,6},{5,7},{6,4},{7,5},{8,10},{9,11},{10,... | collective-permute-start | bytes 2359304 | tf_op jit(solution)/shard_map/ppermute | solution.py:43
  158.8 8.9 %collective-permute-start.45 = (bf16[2,512,128]{2,1,0:T(8,128)(2,1)S(1)}, bf16[2,512,128]{2,1,0:T(8,128)(2,1)S(1)}, u32[]{:S(2)}, u32[]{:S(2)}) collective-permute-start(bf16[2,512,128]{2,1,0:T(8,128)(2,1)S(1)} %get-tuple-element.58.refs_0_), channel_id=1, source_target_pairs={{0,32},{1,33},{2,34},{3,35},{4,36},{5,37},{6,38},{7,39},{8,40},{9,... | collective-permute-start | bytes 786440 | tf_op jit(solution)/shard_map/ppermute | solution.py:43
  158.8 17.5 %collective-permute-start.46 = (bf16[2,512,128]{2,1,0:T(8,128)(2,1)S(1)}, bf16[2,512,128]{2,1,0:T(8,128)(2,1)S(1)}, u32[]{:S(2)}, u32[]{:S(2)}) collective-permute-start(bf16[2,512,128]{2,1,0:T(8,128)(2,1)S(1)} %get-tuple-element.58.refs_0_), channel_id=1, source_target_pairs={{0,96},{1,97},{2,98},{3,99},{4,100},{5,101},{6,102},{7,103},{8,104... | collective-permute-start | bytes 786440 | tf_op jit(solution)/shard_map/ppermute | solution.py:43
  167.7 8.6 %collective-permute-start.47 = (bf16[2,512,128]{2,1,0:T(8,128)(2,1)S(1)}, bf16[2,512,128]{2,1,0:T(8,128)(2,1)S(1)}, u32[]{:S(2)}, u32[]{:S(2)}) collective-permute-start(bf16[2,512,128]{2,1,0:T(8,128)(2,1)S(1)} %get-tuple-element.58.refs_0_), channel_id=1, source_target_pairs={{0,64},{1,65},{2,66},{3,67},{4,68},{5,69},{6,70},{7,71},{8,72},{9,... | collective-permute-start | bytes 786440 | tf_op jit(solution)/shard_map/ppermute | solution.py:43
  (11 other events, 48.9 us)

commit v3 on v2

--- a/solution.py
+++ b/solution.py
@@ -49,36 +49,37 @@
 HBM = pl.BlockSpec(memory_space=pltpu.HBM)
 
 
-def noise_kernel(core_ref, chol_ref, noise_ref, mine_ref, others_ref):
-    half = mine_ref.shape[-1]
-    product = jnp.dot(chol_ref[0], noise_ref[0], preferred_element_type=jnp.float32)
-
-    @pl.when(core_ref[0] == 0)
-    def _():
-        mine_ref[0] = product[:, :half]
-        others_ref[0] = product[:, half:]
-
-    @pl.when(core_ref[0] != 0)
-    def _():
-        mine_ref[0] = product[:, half:]
-        others_ref[0] = product[:, :half]
+def noise_kernel(core_ref, chol_ref, noise_ref, mine_ref, others_ref, chol, noise, sems):
+    levels, _, half = mine_ref.shape
+    copies = []
+    for l in range(levels):
+        copies.append(pltpu.make_async_copy(chol_ref.at[l], chol.at[l], sems.at[l, 0]))
+        copies.append(pltpu.make_async_copy(noise_ref.at[l], noise.at[l], sems.at[l, 1]))
+    for copy in copies:
+        copy.start()
+    low = core_ref[0] == 0
+    for l in range(levels):
+        copies[2 * l].wait()
+        copies[2 * l + 1].wait()
+        product = jnp.dot(chol[l], noise[l], preferred_element_type=jnp.float32)
+        mine_ref[l] = jnp.where(low, product[:, :half], product[:, half:])
+        others_ref[l] = jnp.where(low, product[:, half:], product[:, :half])
 
 
 def noise_call(core, chol, noise):
     levels, rows, columns = noise.shape
-    half = columns // 2
-    part = pl.BlockSpec((1, rows, half), lambda l: (l, 0, 0))
-    shape = jax.ShapeDtypeStruct((levels, rows, half), jnp.float32)
+    shape = jax.ShapeDtypeStruct((levels, rows, columns // 2), jnp.float32)
     return pl.pallas_call(
         noise_kernel,
-        grid=(levels,),
         out_shape=(shape, shape),
-        in_specs=[
-            SMEM,
-            pl.BlockSpec((1, rows, rows), lambda l: (l, 0, 0)),
-            pl.BlockSpec((1, rows, columns), lambda l: (l, 0, 0)),
+        in_specs=[SMEM, HBM, HBM],
+        out_specs=(VMEM, VMEM),
+        scratch_shapes=[
+            pltpu.VMEM(chol.shape, jnp.bfloat16),
+            pltpu.VMEM(noise.shape, jnp.bfloat16),
+            pltpu.SemaphoreType.DMA((levels, 2)),
         ],
-        out_specs=(part, part),
+        compiler_params=pltpu.CompilerParams(vmem_limit_bytes=56 * 1024 * 1024),
         cost_estimate=pl.CostEstimate(
             flops=2 * levels * rows * rows * columns, bytes_accessed=levels * rows * rows * 4, transcendentals=0
         ),
@@ -120,7 +121,7 @@
         in_specs=[ANYWHERE, HBM, HBM],
         out_specs=VMEM,
         scratch_shapes=[pltpu.SemaphoreType.DMA((2,))],
-        compiler_params=pltpu.CompilerParams(vmem_limit_bytes=24 * 1024 * 1024),
+        compiler_params=pltpu.CompilerParams(vmem_limit_bytes=30 * 1024 * 1024),
         cost_estimate=pl.CostEstimate(
             flops=0, bytes_accessed=2 * own_f.size // own_f.shape[0] * 2, transcendentals=0
         ),
@@ -132,8 +133,8 @@
     mine_ref, theirs_ref, factor, out_ref, give_ref, picked = refs[count:]
 
     def step(t, carry):
-        code = where_ref[level, t // 8, t % 8]
-        pick(code // 8, code % 8, sources, picked.at[t // 8, t % 8])
+        code = where_ref[level, t >> 3, t & 7]
+        pick(code >> 3, code & 7, sources, picked.at[t >> 3, t & 7])
         return carry
 
     lax.fori_loop(0, 16, step, 0)
@@ -201,33 +202,37 @@
         ),
     )
     in_col = jnp.where(p3 == 0, 0, 5 + p3) * 8 + jnp.where(row % 2 == core, 0, 1)
+    own_far = (SOON - 1 + p2) * 8 + 6 + j
+    in_row = jnp.concatenate([jnp.where((p1 == 0) & (p2 > 0), own_far, in_row)[:1], in_row[1:]])
     where = jnp.where(row == my_row, in_row, in_col).astype(jnp.int32)
 
     own_f = cond_factors[:, 0, 0]
-    chol, innovations = chol_factors[:, 0, 0], noise[:, 0, 0]
+    own_terms, sent_terms = noise_call(core.reshape(1), chol_factors[:, 0, 0], noise[:, 0, 0])
 
     kept, given, got = [], [], []
     for level in range(cond_factors.shape[0]):
         near = [send(draws, first(s)) for s in (2, 1, -1)]
         if level == 0:
-            held, held_f, where = lax.optimization_barrier((draws, own_f, where))
+            held, sent_terms, where = lax.optimization_barrier((draws, sent_terms, where))
+            other_terms = send(sent_terms, OTHER)
+            other_terms, held_f = lax.optimization_barrier((other_terms, own_f))
             other_f = send(held_f, OTHER)
         else:
             swapped = send(given[-1], OTHER)
             held, swapped = lax.optimization_barrier((draws, swapped))
             got.append(swapped)
-        along = [send(held, second(s)) for s in (1, -1)]
+        along = [send(held, second(s)) for s in (1, -1)] if level > 0 else [draws, draws]
         line = jnp.concatenate([near[1], near[2], near[0]])
+        held, line = lax.optimization_barrier((held, line))
         if level == 0:
-            line, chol, innovations = lax.optimization_barrier((line, chol, innovations))
-            own_terms, sent_terms = noise_call(core.reshape(1), chol, innovations)
-            other_terms = send(sent_terms, OTHER)
-        held, line = lax.optimization_barrier((held, line))
-        far = [
-            send(line, second(2)),
-            send(jnp.concatenate([line, along[0][:1]]), second(1)),
-            send(jnp.concatenate([line, along[1][1:]]), second(-1)),
-        ]
+            whole_line = jnp.concatenate([line, held])
+            far = [send(whole_line, second(s)) for s in (2, 1, -1)]
+        else:
+            far = [
+                send(line, second(2)),
+                send(jnp.concatenate([line, along[0][:1]]), second(1)),
+                send(jnp.concatenate([line, along[1][1:]]), second(-1)),
+            ]
         column = [send(held, along_z(s)) for s in (2, 1, -1)]
         factor = stage_call(level, line, own_f, other_f)
         sources = [draws, near[1], near[2], near[0]] + along + [column[1], column[2], column[0]]

time: 186 us -> 182 us (0.978)
  local copies, waits for them, and re-layouts: 24.1 us -> 4.16 us
  waiting for transfers between devices: 57.4 us -> 71.9 us
  Pallas kernels: 30.2 us -> 33.1 us
    unnamed x14 -> x13, local copies, waits for them, and re-layouts: 23.1 us -> 3.11 us
    ppermute x52 -> x50, waiting for transfers between devices: 57.4 us -> 71.9 us  [send(): return lax.ppermute(value, AXES, route)]
    pallas_call x4, Pallas kernels: 9.97 us -> 13.9 us  [stage_call(): pl.pallas_call(functools.partial(stage_kernel, level), out_shape=jax.Shap...]
    ppermute x52 -> x50, starting transfers between devices: 69.1 us -> 69.1 us  [send(): return lax.ppermute(value, AXES, route)]
  transfers between devices with their start and end apart: 52 -> 50, of which waited for: 20 -> 23; matrix products, arithmetic and copies ran while one was open for 1% -> 1% of each run, Pallas kernels for 8% -> 10%
where the time goes in v3:
time: 182 us
  waiting for transfers between devices  71.9 us (40%)
  starting transfers between devices  69.1 us (38%)
  Pallas kernels  33.1 us (18%)
  local copies, waits for them, and re-layouts  4.16 us (2%)
  other arithmetic  3.44 us (2%)
    ppermute x50, waiting for transfers between devices, send(): return lax.ppermute(value, AXES, route)  71.9 us
    ppermute x50, starting transfers between devices, send(): return lax.ppermute(value, AXES, route)  69.1 us
    pallas_call x4, Pallas kernels, level_call(): pl.pallas_call(functools.partial(level_kernel, level, len(sources)), out_...  15 us
    pallas_call x4, Pallas kernels, stage_call(): pl.pallas_call(functools.partial(stage_kernel, level), out_shape=jax.Shap...  13.9 us
    pallas_call x1, Pallas kernels, noise_call(): pl.pallas_call(noise_kernel, out_shape=(shape, shape), in_specs=[SMEM, HB...  4.23 us
  transfers between devices with their start and end apart: 50, of which 23 were waited for; matrix products, arithmetic and copies ran while one was open for 1% of the time, Pallas kernels for 10%

profile of v3, /device:TPU:1, one launch (start us, length us, event | category | flops | bytes accessed | tf_op | source)
XLA Modules:
  0.0 182.2 jit_solution(2180067467322992151)
XLA Ops:
  2.6 4.2 %shard_map.64 = (f32[4,512,128]{2,1,0:T(8,128)}, f32[4,512,128]{2,1,0:T(8,128)}) custom-call(s32[1]{0:T(128)} %bitcast.3.core_ref, bf16[4,512,512]{2,1,0:T(8,128)(2,1)} %bitcast.28, bf16[4,512,256]{2,1,0:T(8,128)(2,1)} %bitcast.29), custom_call_target="tpu_custom_call" | custom-call | flops 536870912 | bytes 4194304 | tf_op jit(solution)/shard_map/pallas_call | solution.py:72
  8.6 2.3 %collective-permute-done.11.refs_13_ = f32[4,512,128]{2,1,0:T(8,128)S(1)} collective-permute-done((f32[4,512,128]{2,1,0:T(8,128)S(1)}, f32[4,512,128]{2,1,0:T(8,128)S(1)}, u32[]{:S(2)}, u32[]{:S(2)}) %collective-permute-start.11) | collective-permute-done | bytes 1048608 | tf_op jit(solution)/shard_map/ppermute | solution.py:43
  14.1 1.6 collective-permute-start.4
  15.8 2.4 %collective-permute-done.2.refs_1_ = bf16[2,512,128]{2,1,0:T(8,128)(2,1)S(1)} collective-permute-done((bf16[2,512,128]{2,1,0:T(8,128)(2,1)S(1)}, bf16[2,512,128]{2,1,0:T(8,128)(2,1)S(1)}, u32[]{:S(2)}, u32[]{:S(2)}) %collective-permute-start.2) | collective-permute-done | bytes 262176 | tf_op jit(solution)/shard_map/ppermute | solution.py:43
  18.2 4.0 %collective-permute-done.4.refs_3_ = bf16[2,512,128]{2,1,0:T(8,128)(2,1)S(1)} collective-permute-done((bf16[2,512,128]{2,1,0:T(8,128)(2,1)S(1)}, bf16[2,512,128]{2,1,0:T(8,128)(2,1)S(1)}, u32[]{:S(2)}, u32[]{:S(2)}) %collective-permute-start.4) | collective-permute-done | bytes 262176 | tf_op jit(solution)/shard_map/ppermute | solution.py:43
  22.4 2.5 %collective-permute-start.10 = (bf16[8,512,128]{2,1,0:T(8,128)(2,1)S(1)}, bf16[8,512,128]{2,1,0:T(8,128)(2,1)S(1)}, u32[]{:S(2)}, u32[]{:S(2)}) collective-permute-start(bf16[8,512,128]{2,1,0:T(8,128)(2,1)S(1)} %constant_dynamic-update-slice_fusion), channel_id=1, source_target_pairs={{0,2},{1,3},{2,0},{3,1},{4,6},{5,7},{6,4},{7,5},{8,10},{9,11},{10,... | collective-permute-start | bytes 3145736 | tf_op jit(solution)/shard_map/ppermute | solution.py:43
  25.2 2.4 %collective-permute-start.9 = (bf16[8,512,128]{2,1,0:T(8,128)(2,1)S(1)}, bf16[8,512,128]{2,1,0:T(8,128)(2,1)S(1)}, u32[]{:S(2)}, u32[]{:S(2)}) collective-permute-start(bf16[8,512,128]{2,1,0:T(8,128)(2,1)S(1)} %constant_dynamic-update-slice_fusion), channel_id=1, source_target_pairs={{0,3},{1,0},{2,1},{3,2},{4,7},{5,4},{6,5},{7,6},{8,11},{9,8},{10,9... | collective-permute-start | bytes 3145736 | tf_op jit(solution)/shard_map/ppermute | solution.py:43
  27.6 1.6 collective-permute-start.5
  29.2 6.7 %collective-permute-done.5.refs_6_ = bf16[2,512,128]{2,1,0:T(8,128)(2,1)S(1)} collective-permute-done((bf16[2,512,128]{2,1,0:T(8,128)(2,1)S(1)}, bf16[2,512,128]{2,1,0:T(8,128)(2,1)S(1)}, u32[]{:S(2)}, u32[]{:S(2)}) %collective-permute-start.5) | collective-permute-done | bytes 262176 | tf_op jit(solution)/shard_map/ppermute | solution.py:43
  37.1 2.9 %collective-permute-start.7 = (bf16[2,512,128]{2,1,0:T(8,128)(2,1)S(1)}, bf16[2,512,128]{2,1,0:T(8,128)(2,1)S(1)}, u32[]{:S(2)}, u32[]{:S(2)}) collective-permute-start(bf16[2,512,128]{2,1,0:T(8,128)(2,1)S(1)} %pad_maximum_fusion.10.refs_0_.refs_4_.refs_5_), channel_id=1, source_target_pairs={{0,64},{1,65},{2,66},{3,67},{4,68},{5,69},{6,70},{7,71},{8,72},{9,... | collective-permute-start | bytes 786440 | tf_op jit(solution)/shard_map/ppermute | solution.py:43
  40.0 2.9 %copy-done.3 = bf16[4,8,512,512]{3,2,1,0:T(8,128)(2,1)} copy-done((bf16[4,8,512,512]{3,2,1,0:T(8,128)(2,1)}, bf16[4,8,512,512]{3,2,1,0:T(8,128)(2,1)S(1)}, u32[]{:S(2)}) %copy-start.3) | copy-done | bytes 16777240
  42.9 3.5 %shard_map.65.refs_14_ = bf16[2,8,512,512]{3,2,1,0:T(8,128)(2,1)S(1)} custom-call(bf16[6,512,128]{2,1,0:T(8,128)(2,1)S(1)} %pad_maximum_fusion.6.token_ref, bf16[4,8,512,512]{3,2,1,0:T(8,128)(2,1)} %bitcast.24, bf16[4,8,512,512]{3,2,1,0:T(8,128)(2,1)} %copy-done.3), custom_call_target="tpu_custom_call" | custom-call | bytes 8388608 | tf_op jit(solution)/shard_map/pallas_call | solution.py:118
  46.4 2.7 %collective-permute-done.8.refs_9_ = bf16[8,512,128]{2,1,0:T(8,128)(2,1)S(1)} collective-permute-done((bf16[8,512,128]{2,1,0:T(8,128)(2,1)S(1)}, bf16[8,512,128]{2,1,0:T(8,128)(2,1)S(1)}, u32[]{:S(2)}, u32[]{:S(2)}) %collective-permute-start.8) | collective-permute-done | bytes 1048608 | tf_op jit(solution)/shard_map/ppermute | solution.py:43
  49.1 3.7 %shard_map.66 = (bf16[2,512,128]{2,1,0:T(8,128)(2,1)S(1)}, bf16[512,128]{1,0:T(8,128)(2,1)S(1)}) custom-call(s32[4,2,8]{2,1,0:T(2,128)S(1)} %compare_select_fusion.23.where_ref, bf16[2,512,128]{2,1,0:T(8,128)(2,1)S(1)} %pad_maximum_fusion.10.refs_0_.refs_4_.refs_5_, bf16[2,512,128]{2,1,0:T(8,128)(2,1)S(1)} %collective-permute-done.2.refs_1_, ...), custom_call_target="tpu_custom_call" | custom-call | flops 1073741824 | bytes 2097152 | tf_op jit(solution)/shard_map/pallas_call | solution.py:151
  53.9 1.7 collective-permute-start.14
  55.8 2.8 %collective-permute-start.16 = (bf16[512,128]{1,0:T(8,128)(2,1)S(1)}, bf16[512,128]{1,0:T(8,128)(2,1)S(1)}, u32[]{:S(2)}, u32[]{:S(2)}) collective-permute-start(bf16[512,128]{1,0:T(8,128)(2,1)S(1)} %get-tuple-element.44), channel_id=1, source_target_pairs={{0,16},{1,17},{2,18},{3,19},{4,20},{5,21},{6,22},{7,23},{8,24},{9,... | collective-permute-start | bytes 393224 | tf_op jit(solution)/shard_map/ppermute | solution.py:43
  62.4 5.7 %collective-permute-done.17.refs_4_ = bf16[2,512,128]{2,1,0:T(8,128)(2,1)S(1)} collective-permute-done((bf16[2,512,128]{2,1,0:T(8,128)(2,1)S(1)}, bf16[2,512,128]{2,1,0:T(8,128)(2,1)S(1)}, u32[]{:S(2)}, u32[]{:S(2)}) %collective-permute-start.17) | collective-permute-done | bytes 262176 | tf_op jit(solution)/shard_map/ppermute | solution.py:43
  69.3 1.8 collective-permute-start.23
  71.8 1.7 collective-permute-start.19
  73.4 2.1 %collective-permute-start.20 = (bf16[2,512,128]{2,1,0:T(8,128)(2,1)S(1)}, bf16[2,512,128]{2,1,0:T(8,128)(2,1)S(1)}, u32[]{:S(2)}, u32[]{:S(2)}) collective-permute-start(bf16[2,512,128]{2,1,0:T(8,128)(2,1)S(1)} %get-tuple-element.46.refs_0_), channel_id=1, source_target_pairs={{0,96},{1,97},{2,98},{3,99},{4,100},{5,101},{6,102},{7,103},{8,104... | collective-permute-start | bytes 786440 | tf_op jit(solution)/shard_map/ppermute | solution.py:43
  75.5 5.8 %collective-permute-done.19.refs_6_ = bf16[2,512,128]{2,1,0:T(8,128)(2,1)S(1)} collective-permute-done((bf16[2,512,128]{2,1,0:T(8,128)(2,1)S(1)}, bf16[2,512,128]{2,1,0:T(8,128)(2,1)S(1)}, u32[]{:S(2)}, u32[]{:S(2)}) %collective-permute-start.19) | collective-permute-done | bytes 262176 | tf_op jit(solution)/shard_map/ppermute | solution.py:43
  82.3 3.5 %shard_map.67.refs_14_ = bf16[2,8,512,512]{3,2,1,0:T(8,128)(2,1)S(1)} custom-call(bf16[6,512,128]{2,1,0:T(8,128)(2,1)S(1)} %pad_maximum_fusion.7.token_ref, bf16[4,8,512,512]{3,2,1,0:T(8,128)(2,1)} %bitcast.25, bf16[4,8,512,512]{3,2,1,0:T(8,128)(2,1)} %copy-done.3), custom_call_target="tpu_custom_call" | custom-call | bytes 8388608 | tf_op jit(solution)/shard_map/pallas_call | solution.py:118
  85.8 3.3 %collective-permute-done.21.refs_8_ = bf16[2,512,128]{2,1,0:T(8,128)(2,1)S(1)} collective-permute-done((bf16[2,512,128]{2,1,0:T(8,128)(2,1)S(1)}, bf16[2,512,128]{2,1,0:T(8,128)(2,1)S(1)}, u32[]{:S(2)}, u32[]{:S(2)}) %collective-permute-start.21) | collective-permute-done | bytes 262176 | tf_op jit(solution)/shard_map/ppermute | solution.py:43
  89.1 2.2 %collective-permute-done.24.refs_11_ = bf16[6,512,128]{2,1,0:T(8,128)(2,1)S(1)} collective-permute-done((bf16[6,512,128]{2,1,0:T(8,128)(2,1)S(1)}, bf16[6,512,128]{2,1,0:T(8,128)(2,1)S(1)}, u32[]{:S(2)}, u32[]{:S(2)}) %collective-permute-start.24) | collective-permute-done | bytes 786464 | tf_op jit(solution)/shard_map/ppermute | solution.py:43
  91.3 3.7 %shard_map.68 = (bf16[2,512,128]{2,1,0:T(8,128)(2,1)S(1)}, bf16[512,128]{1,0:T(8,128)(2,1)S(1)}) custom-call(s32[4,2,8]{2,1,0:T(2,128)S(1)} %compare_select_fusion.23.where_ref, bf16[2,512,128]{2,1,0:T(8,128)(2,1)S(1)} %get-tuple-element.46.refs_0_, bf16[2,512,128]{2,1,0:T(8,128)(2,1)S(1)} %collective-permute-done.13.refs_1_, ...), custom_call_target="tpu_custom_call" | custom-call | flops 1073741824 | bytes 2097152 | tf_op jit(solution)/shard_map/pallas_call | solution.py:151
  98.8 2.3 %collective-permute-start.28 = (bf16[512,128]{1,0:T(8,128)(2,1)S(1)}, bf16[512,128]{1,0:T(8,128)(2,1)S(1)}, u32[]{:S(2)}, u32[]{:S(2)}) collective-permute-start(bf16[512,128]{1,0:T(8,128)(2,1)S(1)} %get-tuple-element.49), channel_id=1, source_target_pairs={{0,16},{1,17},{2,18},{3,19},{4,20},{5,21},{6,22},{7,23},{8,24},{9,... | collective-permute-start | bytes 393224 | tf_op jit(solution)/shard_map/ppermute | solution.py:43
  102.1 2.7 %collective-permute-start.30 = (bf16[2,512,128]{2,1,0:T(8,128)(2,1)S(1)}, bf16[2,512,128]{2,1,0:T(8,128)(2,1)S(1)}, u32[]{:S(2)}, u32[]{:S(2)}) collective-permute-start(bf16[2,512,128]{2,1,0:T(8,128)(2,1)S(1)} %get-tuple-element.51.refs_0_), channel_id=1, source_target_pairs={{0,3},{1,0},{2,1},{3,2},{4,7},{5,4},{6,5},{7,6},{8,11},{9,8},{10,9... | collective-permute-start | bytes 786440 | tf_op jit(solution)/shard_map/ppermute | solution.py:43
  105.8 3.9 %collective-permute-done.29.refs_4_ = bf16[2,512,128]{2,1,0:T(8,128)(2,1)S(1)} collective-permute-done((bf16[2,512,128]{2,1,0:T(8,128)(2,1)S(1)}, bf16[2,512,128]{2,1,0:T(8,128)(2,1)S(1)}, u32[]{:S(2)}, u32[]{:S(2)}) %collective-permute-start.29) | collective-permute-done | bytes 262176 | tf_op jit(solution)/shard_map/ppermute | solution.py:43
  110.6 2.0 %collective-permute-start.35 = (bf16[7,512,128]{2,1,0:T(8,128)(2,1)S(1)}, bf16[7,512,128]{2,1,0:T(8,128)(2,1)S(1)}, u32[]{:S(2)}, u32[]{:S(2)}) collective-permute-start(bf16[7,512,128]{2,1,0:T(8,128)(2,1)S(1)} %get-tuple-element.73), channel_id=1, source_target_pairs={{0,3},{1,0},{2,1},{3,2},{4,7},{5,4},{6,5},{7,6},{8,11},{9,8},{10,9... | collective-permute-start | bytes 2752520 | tf_op jit(solution)/shard_map/ppermute | solution.py:43
  113.4 1.6 collective-permute-start.31
  115.0 2.1 %collective-permute-start.32 = (bf16[2,512,128]{2,1,0:T(8,128)(2,1)S(1)}, bf16[2,512,128]{2,1,0:T(8,128)(2,1)S(1)}, u32[]{:S(2)}, u32[]{:S(2)}) collective-permute-start(bf16[2,512,128]{2,1,0:T(8,128)(2,1)S(1)} %get-tuple-element.51.refs_0_), channel_id=1, source_target_pairs={{0,96},{1,97},{2,98},{3,99},{4,100},{5,101},{6,102},{7,103},{8,104... | collective-permute-start | bytes 786440 | tf_op jit(solution)/shard_map/ppermute | solution.py:43
  117.1 5.0 %collective-permute-done.31.refs_6_ = bf16[2,512,128]{2,1,0:T(8,128)(2,1)S(1)} collective-permute-done((bf16[2,512,128]{2,1,0:T(8,128)(2,1)S(1)}, bf16[2,512,128]{2,1,0:T(8,128)(2,1)S(1)}, u32[]{:S(2)}, u32[]{:S(2)}) %collective-permute-start.31) | collective-permute-done | bytes 262176 | tf_op jit(solution)/shard_map/ppermute | solution.py:43
  123.1 3.5 %shard_map.69.refs_14_ = bf16[2,8,512,512]{3,2,1,0:T(8,128)(2,1)S(1)} custom-call(bf16[6,512,128]{2,1,0:T(8,128)(2,1)S(1)} %pad_maximum_fusion.8.token_ref, bf16[4,8,512,512]{3,2,1,0:T(8,128)(2,1)} %bitcast.26, bf16[4,8,512,512]{3,2,1,0:T(8,128)(2,1)} %copy-done.3), custom_call_target="tpu_custom_call" | custom-call | bytes 8388608 | tf_op jit(solution)/shard_map/pallas_call | solution.py:118
  126.6 2.6 %collective-permute-done.33.refs_8_ = bf16[2,512,128]{2,1,0:T(8,128)(2,1)S(1)} collective-permute-done((bf16[2,512,128]{2,1,0:T(8,128)(2,1)S(1)}, bf16[2,512,128]{2,1,0:T(8,128)(2,1)S(1)}, u32[]{:S(2)}, u32[]{:S(2)}) %collective-permute-start.33) | collective-permute-done | bytes 262176 | tf_op jit(solution)/shard_map/ppermute | solution.py:43
  129.1 3.7 %collective-permute-done.36.refs_11_ = bf16[6,512,128]{2,1,0:T(8,128)(2,1)S(1)} collective-permute-done((bf16[6,512,128]{2,1,0:T(8,128)(2,1)S(1)}, bf16[6,512,128]{2,1,0:T(8,128)(2,1)S(1)}, u32[]{:S(2)}, u32[]{:S(2)}) %collective-permute-start.36) | collective-permute-done | bytes 786464 | tf_op jit(solution)/shard_map/ppermute | solution.py:43
  132.9 3.7 %shard_map.70 = (bf16[2,512,128]{2,1,0:T(8,128)(2,1)S(1)}, bf16[512,128]{1,0:T(8,128)(2,1)S(1)}) custom-call(s32[4,2,8]{2,1,0:T(2,128)S(1)} %compare_select_fusion.23.where_ref, bf16[2,512,128]{2,1,0:T(8,128)(2,1)S(1)} %get-tuple-element.51.refs_0_, bf16[2,512,128]{2,1,0:T(8,128)(2,1)S(1)} %collective-permute-done.25.refs_1_, ...), custom_call_target="tpu_custom_call" | custom-call | flops 1073741824 | bytes 2097152 | tf_op jit(solution)/shard_map/pallas_call | solution.py:151
  137.5 1.8 %collective-permute-start.38 = (bf16[2,512,128]{2,1,0:T(8,128)(2,1)S(1)}, bf16[2,512,128]{2,1,0:T(8,128)(2,1)S(1)}, u32[]{:S(2)}, u32[]{:S(2)}) collective-permute-start(bf16[2,512,128]{2,1,0:T(8,128)(2,1)S(1)} %get-tuple-element.56.refs_0_), channel_id=1, source_target_pairs={{0,12},{1,13},{2,14},{3,15},{4,0},{5,1},{6,2},{7,3},{8,4},{9,5},{1... | collective-permute-start | bytes 786440 | tf_op jit(solution)/shard_map/ppermute | solution.py:43
  139.9 2.4 %collective-permute-start.40 = (bf16[512,128]{1,0:T(8,128)(2,1)S(1)}, bf16[512,128]{1,0:T(8,128)(2,1)S(1)}, u32[]{:S(2)}, u32[]{:S(2)}) collective-permute-start(bf16[512,128]{1,0:T(8,128)(2,1)S(1)} %get-tuple-element.54), channel_id=1, source_target_pairs={{0,16},{1,17},{2,18},{3,19},{4,20},{5,21},{6,22},{7,23},{8,24},{9,... | collective-permute-start | bytes 393224 | tf_op jit(solution)/shard_map/ppermute | solution.py:43
  143.4 2.6 %collective-permute-start.42 = (bf16[2,512,128]{2,1,0:T(8,128)(2,1)S(1)}, bf16[2,512,128]{2,1,0:T(8,128)(2,1)S(1)}, u32[]{:S(2)}, u32[]{:S(2)}) collective-permute-start(bf16[2,512,128]{2,1,0:T(8,128)(2,1)S(1)} %get-tuple-element.56.refs_0_), channel_id=1, source_target_pairs={{0,3},{1,0},{2,1},{3,2},{4,7},{5,4},{6,5},{7,6},{8,11},{9,8},{10,9... | collective-permute-start | bytes 786440 | tf_op jit(solution)/shard_map/ppermute | solution.py:43
  146.9 5.0 %collective-permute-done.41.refs_4_ = bf16[2,512,128]{2,1,0:T(8,128)(2,1)S(1)} collective-permute-done((bf16[2,512,128]{2,1,0:T(8,128)(2,1)S(1)}, bf16[2,512,128]{2,1,0:T(8,128)(2,1)S(1)}, u32[]{:S(2)}, u32[]{:S(2)}) %collective-permute-start.41) | collective-permute-done | bytes 262176 | tf_op jit(solution)/shard_map/ppermute | solution.py:43
  152.1 2.7 %collective-permute-start.47 = (bf16[7,512,128]{2,1,0:T(8,128)(2,1)S(1)}, bf16[7,512,128]{2,1,0:T(8,128)(2,1)S(1)}, u32[]{:S(2)}, u32[]{:S(2)}) collective-permute-start(bf16[7,512,128]{2,1,0:T(8,128)(2,1)S(1)} %get-tuple-element.71), channel_id=1, source_target_pairs={{0,3},{1,0},{2,1},{3,2},{4,7},{5,4},{6,5},{7,6},{8,11},{9,8},{10,9... | collective-permute-start | bytes 2752520 | tf_op jit(solution)/shard_map/ppermute | solution.py:43
  155.5 1.7 collective-permute-start.43
  157.2 2.1 %collective-permute-start.44 = (bf16[2,512,128]{2,1,0:T(8,128)(2,1)S(1)}, bf16[2,512,128]{2,1,0:T(8,128)(2,1)S(1)}, u32[]{:S(2)}, u32[]{:S(2)}) collective-permute-start(bf16[2,512,128]{2,1,0:T(8,128)(2,1)S(1)} %get-tuple-element.56.refs_0_), channel_id=1, source_target_pairs={{0,96},{1,97},{2,98},{3,99},{4,100},{5,101},{6,102},{7,103},{8,104... | collective-permute-start | bytes 786440 | tf_op jit(solution)/shard_map/ppermute | solution.py:43
  159.3 6.0 %collective-permute-done.43.refs_6_ = bf16[2,512,128]{2,1,0:T(8,128)(2,1)S(1)} collective-permute-done((bf16[2,512,128]{2,1,0:T(8,128)(2,1)S(1)}, bf16[2,512,128]{2,1,0:T(8,128)(2,1)S(1)}, u32[]{:S(2)}, u32[]{:S(2)}) %collective-permute-start.43) | collective-permute-done | bytes 262176 | tf_op jit(solution)/shard_map/ppermute | solution.py:43
  166.3 3.5 %shard_map.71.refs_14_ = bf16[2,8,512,512]{3,2,1,0:T(8,128)(2,1)S(1)} custom-call(bf16[6,512,128]{2,1,0:T(8,128)(2,1)S(1)} %pad_maximum_fusion.9.token_ref, bf16[4,8,512,512]{3,2,1,0:T(8,128)(2,1)} %bitcast.27, bf16[4,8,512,512]{3,2,1,0:T(8,128)(2,1)} %copy-done.3), custom_call_target="tpu_custom_call" | custom-call | bytes 8388608 | tf_op jit(solution)/shard_map/pallas_call | solution.py:118
  169.8 3.6 %collective-permute-done.45.refs_8_ = bf16[2,512,128]{2,1,0:T(8,128)(2,1)S(1)} collective-permute-done((bf16[2,512,128]{2,1,0:T(8,128)(2,1)S(1)}, bf16[2,512,128]{2,1,0:T(8,128)(2,1)S(1)}, u32[]{:S(2)}, u32[]{:S(2)}) %collective-permute-start.45) | collective-permute-done | bytes 262176 | tf_op jit(solution)/shard_map/ppermute | solution.py:43
  173.3 1.7 collective-permute-done.48.refs_11_
  175.0 3.7 %shard_map.72 = (bf16[2,512,128]{2,1,0:T(8,128)(2,1)S(1)}, bf16[512,128]{1,0:T(8,128)(2,1)S(1)}) custom-call(s32[4,2,8]{2,1,0:T(2,128)S(1)} %compare_select_fusion.23.where_ref, bf16[2,512,128]{2,1,0:T(8,128)(2,1)S(1)} %get-tuple-element.56.refs_0_, bf16[2,512,128]{2,1,0:T(8,128)(2,1)S(1)} %collective-permute-done.37.refs_1_, ...), custom_call_target="tpu_custom_call" | custom-call | flops 1073741824 | bytes 2097152 | tf_op jit(solution)/shard_map/pallas_call | solution.py:151
  (111 shorter events, 34.1 us)
Async XLA Ops:
  0.0 6.8 %collective-permute-start.1 = (s32[4,8]{1,0:T(4,128)}, s32[4,8]{1,0:T(4,128)S(1)}, u32[]{:S(2)}, u32[]{:S(2)}) collective-permute-start(s32[4,8]{1,0:T(4,128)} %bitcast.36), channel_id=1, source_target_pairs={{0,16},{1,17},{2,18},{3,19},{4,20},{5,21},{6,22},{7,23},{8,24},{9,... | collective-permute-start | bytes 392 | tf_op jit(solution)/shard_map/ppermute | solution.py:43
  2.4 5.6 %collective-permute-start = (bf16[512,128]{1,0:T(8,128)(2,1)S(1)}, bf16[512,128]{1,0:T(8,128)(2,1)S(1)}, u32[]{:S(2)}, u32[]{:S(2)}) collective-permute-start(bf16[512,128]{1,0:T(8,128)(2,1)S(1)} %get-tuple-element.78), channel_id=1, source_target_pairs={{0,16},{1,17},{2,18},{3,19},{4,20},{5,21},{6,22},{7,23},{8,24},{9,... | collective-permute-start | bytes 393224 | tf_op jit(solution)/shard_map/ppermute | solution.py:43
  10.9 26.2 %collective-permute-start.12 = (bf16[4,8,512,512]{3,2,1,0:T(8,128)(2,1)}, bf16[4,8,512,512]{3,2,1,0:T(8,128)(2,1)S(1)}, u32[]{:S(2)}, u32[]{:S(2)}) collective-permute-start(bf16[4,8,512,512]{3,2,1,0:T(8,128)(2,1)} %bitcast.23), channel_id=1, source_target_pairs={{0,16},{1,17},{2,18},{3,19},{4,20},{5,21},{6,22},{7,23},{8,24},{9,... | collective-permute-start | bytes 50331656 | tf_op jit(solution)/shard_map/ppermute | solution.py:43
  11.3 6.9 %collective-permute-start.2 = (bf16[2,512,128]{2,1,0:T(8,128)(2,1)S(1)}, bf16[2,512,128]{2,1,0:T(8,128)(2,1)S(1)}, u32[]{:S(2)}, u32[]{:S(2)}) collective-permute-start(bf16[2,512,128]{2,1,0:T(8,128)(2,1)S(1)} %pad_maximum_fusion.10.refs_0_.refs_4_.refs_5_), channel_id=1, source_target_pairs={{0,4},{1,5},{2,6},{3,7},{4,8},{5,9},{6,10},{7,11},{8,12},{9,13},{1... | collective-permute-start | bytes 786440 | tf_op jit(solution)/shard_map/ppermute | solution.py:43
  12.7 5.5 %collective-permute-start.3 = (bf16[2,512,128]{2,1,0:T(8,128)(2,1)S(1)}, bf16[2,512,128]{2,1,0:T(8,128)(2,1)S(1)}, u32[]{:S(2)}, u32[]{:S(2)}) collective-permute-start(bf16[2,512,128]{2,1,0:T(8,128)(2,1)S(1)} %pad_maximum_fusion.10.refs_0_.refs_4_.refs_5_), channel_id=1, source_target_pairs={{0,12},{1,13},{2,14},{3,15},{4,0},{5,1},{6,2},{7,3},{8,4},{9,5},{1... | collective-permute-start | bytes 786440 | tf_op jit(solution)/shard_map/ppermute | solution.py:43
  14.1 8.0 %collective-permute-start.4 = (bf16[2,512,128]{2,1,0:T(8,128)(2,1)S(1)}, bf16[2,512,128]{2,1,0:T(8,128)(2,1)S(1)}, u32[]{:S(2)}, u32[]{:S(2)}) collective-permute-start(bf16[2,512,128]{2,1,0:T(8,128)(2,1)S(1)} %pad_maximum_fusion.10.refs_0_.refs_4_.refs_5_), channel_id=1, source_target_pairs={{0,8},{1,9},{2,10},{3,11},{4,12},{5,13},{6,14},{7,15},{8,0},{9,1},... | collective-permute-start | bytes 786440 | tf_op jit(solution)/shard_map/ppermute | solution.py:43
  22.4 24.0 %collective-permute-start.10 = (bf16[8,512,128]{2,1,0:T(8,128)(2,1)S(1)}, bf16[8,512,128]{2,1,0:T(8,128)(2,1)S(1)}, u32[]{:S(2)}, u32[]{:S(2)}) collective-permute-start(bf16[8,512,128]{2,1,0:T(8,128)(2,1)S(1)} %constant_dynamic-update-slice_fusion), channel_id=1, source_target_pairs={{0,2},{1,3},{2,0},{3,1},{4,6},{5,7},{6,4},{7,5},{8,10},{9,11},{10,... | collective-permute-start | bytes 3145736 | tf_op jit(solution)/shard_map/ppermute | solution.py:43
  24.9 24.2 %collective-permute-start.8 = (bf16[8,512,128]{2,1,0:T(8,128)(2,1)S(1)}, bf16[8,512,128]{2,1,0:T(8,128)(2,1)S(1)}, u32[]{:S(2)}, u32[]{:S(2)}) collective-permute-start(bf16[8,512,128]{2,1,0:T(8,128)(2,1)S(1)} %constant_dynamic-update-slice_fusion), channel_id=1, source_target_pairs={{0,1},{1,2},{2,3},{3,0},{4,5},{5,6},{6,7},{7,4},{8,9},{9,10},{10,1... | collective-permute-start | bytes 3145736 | tf_op jit(solution)/shard_map/ppermute | solution.py:43
  25.2 23.9 %collective-permute-start.9 = (bf16[8,512,128]{2,1,0:T(8,128)(2,1)S(1)}, bf16[8,512,128]{2,1,0:T(8,128)(2,1)S(1)}, u32[]{:S(2)}, u32[]{:S(2)}) collective-permute-start(bf16[8,512,128]{2,1,0:T(8,128)(2,1)S(1)} %constant_dynamic-update-slice_fusion), channel_id=1, source_target_pairs={{0,3},{1,0},{2,1},{3,2},{4,7},{5,4},{6,5},{7,6},{8,11},{9,8},{10,9... | collective-permute-start | bytes 3145736 | tf_op jit(solution)/shard_map/ppermute | solution.py:43
  27.6 8.3 %collective-permute-start.5 = (bf16[2,512,128]{2,1,0:T(8,128)(2,1)S(1)}, bf16[2,512,128]{2,1,0:T(8,128)(2,1)S(1)}, u32[]{:S(2)}, u32[]{:S(2)}) collective-permute-start(bf16[2,512,128]{2,1,0:T(8,128)(2,1)S(1)} %pad_maximum_fusion.10.refs_0_.refs_4_.refs_5_), channel_id=1, source_target_pairs={{0,32},{1,33},{2,34},{3,35},{4,36},{5,37},{6,38},{7,39},{8,40},{9,... | collective-permute-start | bytes 786440 | tf_op jit(solution)/shard_map/ppermute | solution.py:43
  35.9 10.5 %collective-permute-start.6 = (bf16[2,512,128]{2,1,0:T(8,128)(2,1)S(1)}, bf16[2,512,128]{2,1,0:T(8,128)(2,1)S(1)}, u32[]{:S(2)}, u32[]{:S(2)}) collective-permute-start(bf16[2,512,128]{2,1,0:T(8,128)(2,1)S(1)} %pad_maximum_fusion.10.refs_0_.refs_4_.refs_5_), channel_id=1, source_target_pairs={{0,96},{1,97},{2,98},{3,99},{4,100},{5,101},{6,102},{7,103},{8,104... | collective-permute-start | bytes 786440 | tf_op jit(solution)/shard_map/ppermute | solution.py:43
  37.1 9.3 %collective-permute-start.7 = (bf16[2,512,128]{2,1,0:T(8,128)(2,1)S(1)}, bf16[2,512,128]{2,1,0:T(8,128)(2,1)S(1)}, u32[]{:S(2)}, u32[]{:S(2)}) collective-permute-start(bf16[2,512,128]{2,1,0:T(8,128)(2,1)S(1)} %pad_maximum_fusion.10.refs_0_.refs_4_.refs_5_), channel_id=1, source_target_pairs={{0,64},{1,65},{2,66},{3,67},{4,68},{5,69},{6,70},{7,71},{8,72},{9,... | collective-permute-start | bytes 786440 | tf_op jit(solution)/shard_map/ppermute | solution.py:43
  52.9 9.4 %collective-permute-start.13 = (bf16[2,512,128]{2,1,0:T(8,128)(2,1)S(1)}, bf16[2,512,128]{2,1,0:T(8,128)(2,1)S(1)}, u32[]{:S(2)}, u32[]{:S(2)}) collective-permute-start(bf16[2,512,128]{2,1,0:T(8,128)(2,1)S(1)} %get-tuple-element.46.refs_0_), channel_id=1, source_target_pairs={{0,4},{1,5},{2,6},{3,7},{4,8},{5,9},{6,10},{7,11},{8,12},{9,13},{1... | collective-permute-start | bytes 786440 | tf_op jit(solution)/shard_map/ppermute | solution.py:43
  53.9 8.4 %collective-permute-start.14 = (bf16[2,512,128]{2,1,0:T(8,128)(2,1)S(1)}, bf16[2,512,128]{2,1,0:T(8,128)(2,1)S(1)}, u32[]{:S(2)}, u32[]{:S(2)}) collective-permute-start(bf16[2,512,128]{2,1,0:T(8,128)(2,1)S(1)} %get-tuple-element.46.refs_0_), channel_id=1, source_target_pairs={{0,12},{1,13},{2,14},{3,15},{4,0},{5,1},{6,2},{7,3},{8,4},{9,5},{1... | collective-permute-start | bytes 786440 | tf_op jit(solution)/shard_map/ppermute | solution.py:43
  55.6 6.7 %collective-permute-start.15 = (bf16[2,512,128]{2,1,0:T(8,128)(2,1)S(1)}, bf16[2,512,128]{2,1,0:T(8,128)(2,1)S(1)}, u32[]{:S(2)}, u32[]{:S(2)}) collective-permute-start(bf16[2,512,128]{2,1,0:T(8,128)(2,1)S(1)} %get-tuple-element.46.refs_0_), channel_id=1, source_target_pairs={{0,8},{1,9},{2,10},{3,11},{4,12},{5,13},{6,14},{7,15},{8,0},{9,1},... | collective-permute-start | bytes 786440 | tf_op jit(solution)/shard_map/ppermute | solution.py:43
  55.8 3.8 %collective-permute-start.16 = (bf16[512,128]{1,0:T(8,128)(2,1)S(1)}, bf16[512,128]{1,0:T(8,128)(2,1)S(1)}, u32[]{:S(2)}, u32[]{:S(2)}) collective-permute-start(bf16[512,128]{1,0:T(8,128)(2,1)S(1)} %get-tuple-element.44), channel_id=1, source_target_pairs={{0,16},{1,17},{2,18},{3,19},{4,20},{5,21},{6,22},{7,23},{8,24},{9,... | collective-permute-start | bytes 393224 | tf_op jit(solution)/shard_map/ppermute | solution.py:43
  59.6 8.5 %collective-permute-start.17 = (bf16[2,512,128]{2,1,0:T(8,128)(2,1)S(1)}, bf16[2,512,128]{2,1,0:T(8,128)(2,1)S(1)}, u32[]{:S(2)}, u32[]{:S(2)}) collective-permute-start(bf16[2,512,128]{2,1,0:T(8,128)(2,1)S(1)} %get-tuple-element.46.refs_0_), channel_id=1, source_target_pairs={{0,1},{1,2},{2,3},{3,0},{4,5},{5,6},{6,7},{7,4},{8,9},{9,10},{10,1... | collective-permute-start | bytes 786440 | tf_op jit(solution)/shard_map/ppermute | solution.py:43
  60.8 7.4 %collective-permute-start.18 = (bf16[2,512,128]{2,1,0:T(8,128)(2,1)S(1)}, bf16[2,512,128]{2,1,0:T(8,128)(2,1)S(1)}, u32[]{:S(2)}, u32[]{:S(2)}) collective-permute-start(bf16[2,512,128]{2,1,0:T(8,128)(2,1)S(1)} %get-tuple-element.46.refs_0_), channel_id=1, source_target_pairs={{0,3},{1,0},{2,1},{3,2},{4,7},{5,4},{6,5},{7,6},{8,11},{9,8},{10,9... | collective-permute-start | bytes 786440 | tf_op jit(solution)/shard_map/ppermute | solution.py:43
  68.3 23.0 %collective-permute-start.22 = (bf16[7,512,128]{2,1,0:T(8,128)(2,1)S(1)}, bf16[7,512,128]{2,1,0:T(8,128)(2,1)S(1)}, u32[]{:S(2)}, u32[]{:S(2)}) collective-permute-start(bf16[7,512,128]{2,1,0:T(8,128)(2,1)S(1)} %get-tuple-element.76), channel_id=1, source_target_pairs={{0,1},{1,2},{2,3},{3,0},{4,5},{5,6},{6,7},{7,4},{8,9},{9,10},{10,1... | collective-permute-start | bytes 2752520 | tf_op jit(solution)/shard_map/ppermute | solution.py:43
  69.3 22.0 %collective-permute-start.23 = (bf16[7,512,128]{2,1,0:T(8,128)(2,1)S(1)}, bf16[7,512,128]{2,1,0:T(8,128)(2,1)S(1)}, u32[]{:S(2)}, u32[]{:S(2)}) collective-permute-start(bf16[7,512,128]{2,1,0:T(8,128)(2,1)S(1)} %get-tuple-element.75), channel_id=1, source_target_pairs={{0,3},{1,0},{2,1},{3,2},{4,7},{5,4},{6,5},{7,6},{8,11},{9,8},{10,9... | collective-permute-start | bytes 2752520 | tf_op jit(solution)/shard_map/ppermute | solution.py:43
  71.1 20.2 %collective-permute-start.24 = (bf16[6,512,128]{2,1,0:T(8,128)(2,1)S(1)}, bf16[6,512,128]{2,1,0:T(8,128)(2,1)S(1)}, u32[]{:S(2)}, u32[]{:S(2)}) collective-permute-start(bf16[6,512,128]{2,1,0:T(8,128)(2,1)S(1)} %pad_maximum_fusion.7.token_ref), channel_id=1, source_target_pairs={{0,2},{1,3},{2,0},{3,1},{4,6},{5,7},{6,4},{7,5},{8,10},{9,11},{10,... | collective-permute-start | bytes 2359304 | tf_op jit(solution)/shard_map/ppermute | solution.py:43
  71.8 9.5 %collective-permute-start.19 = (bf16[2,512,128]{2,1,0:T(8,128)(2,1)S(1)}, bf16[2,512,128]{2,1,0:T(8,128)(2,1)S(1)}, u32[]{:S(2)}, u32[]{:S(2)}) collective-permute-start(bf16[2,512,128]{2,1,0:T(8,128)(2,1)S(1)} %get-tuple-element.46.refs_0_), channel_id=1, source_target_pairs={{0,32},{1,33},{2,34},{3,35},{4,36},{5,37},{6,38},{7,39},{8,40},{9,... | collective-permute-start | bytes 786440 | tf_op jit(solution)/shard_map/ppermute | solution.py:43
  73.4 12.3 %collective-permute-start.20 = (bf16[2,512,128]{2,1,0:T(8,128)(2,1)S(1)}, bf16[2,512,128]{2,1,0:T(8,128)(2,1)S(1)}, u32[]{:S(2)}, u32[]{:S(2)}) collective-permute-start(bf16[2,512,128]{2,1,0:T(8,128)(2,1)S(1)} %get-tuple-element.46.refs_0_), channel_id=1, source_target_pairs={{0,96},{1,97},{2,98},{3,99},{4,100},{5,101},{6,102},{7,103},{8,104... | collective-permute-start | bytes 786440 | tf_op jit(solution)/shard_map/ppermute | solution.py:43
  81.3 7.8 %collective-permute-start.21 = (bf16[2,512,128]{2,1,0:T(8,128)(2,1)S(1)}, bf16[2,512,128]{2,1,0:T(8,128)(2,1)S(1)}, u32[]{:S(2)}, u32[]{:S(2)}) collective-permute-start(bf16[2,512,128]{2,1,0:T(8,128)(2,1)S(1)} %get-tuple-element.46.refs_0_), channel_id=1, source_target_pairs={{0,64},{1,65},{2,66},{3,67},{4,68},{5,69},{6,70},{7,71},{8,72},{9,... | collective-permute-start | bytes 786440 | tf_op jit(solution)/shard_map/ppermute | solution.py:43
  95.0 9.8 %collective-permute-start.25 = (bf16[2,512,128]{2,1,0:T(8,128)(2,1)S(1)}, bf16[2,512,128]{2,1,0:T(8,128)(2,1)S(1)}, u32[]{:S(2)}, u32[]{:S(2)}) collective-permute-start(bf16[2,512,128]{2,1,0:T(8,128)(2,1)S(1)} %get-tuple-element.51.refs_0_), channel_id=1, source_target_pairs={{0,4},{1,5},{2,6},{3,7},{4,8},{5,9},{6,10},{7,11},{8,12},{9,13},{1... | collective-permute-start | bytes 786440 | tf_op jit(solution)/shard_map/ppermute | solution.py:43
  96.2 8.6 %collective-permute-start.26 = (bf16[2,512,128]{2,1,0:T(8,128)(2,1)S(1)}, bf16[2,512,128]{2,1,0:T(8,128)(2,1)S(1)}, u32[]{:S(2)}, u32[]{:S(2)}) collective-permute-start(bf16[2,512,128]{2,1,0:T(8,128)(2,1)S(1)} %get-tuple-element.51.refs_0_), channel_id=1, source_target_pairs={{0,12},{1,13},{2,14},{3,15},{4,0},{5,1},{6,2},{7,3},{8,4},{9,5},{1... | collective-permute-start | bytes 786440 | tf_op jit(solution)/shard_map/ppermute | solution.py:43
  97.8 7.9 %collective-permute-start.27 = (bf16[2,512,128]{2,1,0:T(8,128)(2,1)S(1)}, bf16[2,512,128]{2,1,0:T(8,128)(2,1)S(1)}, u32[]{:S(2)}, u32[]{:S(2)}) collective-permute-start(bf16[2,512,128]{2,1,0:T(8,128)(2,1)S(1)} %get-tuple-element.51.refs_0_), channel_id=1, source_target_pairs={{0,8},{1,9},{2,10},{3,11},{4,12},{5,13},{6,14},{7,15},{8,0},{9,1},... | collective-permute-start | bytes 786440 | tf_op jit(solution)/shard_map/ppermute | solution.py:43
  98.8 3.3 %collective-permute-start.28 = (bf16[512,128]{1,0:T(8,128)(2,1)S(1)}, bf16[512,128]{1,0:T(8,128)(2,1)S(1)}, u32[]{:S(2)}, u32[]{:S(2)}) collective-permute-start(bf16[512,128]{1,0:T(8,128)(2,1)S(1)} %get-tuple-element.49), channel_id=1, source_target_pairs={{0,16},{1,17},{2,18},{3,19},{4,20},{5,21},{6,22},{7,23},{8,24},{9,... | collective-permute-start | bytes 393224 | tf_op jit(solution)/shard_map/ppermute | solution.py:43
  102.1 7.5 %collective-permute-start.29 = (bf16[2,512,128]{2,1,0:T(8,128)(2,1)S(1)}, bf16[2,512,128]{2,1,0:T(8,128)(2,1)S(1)}, u32[]{:S(2)}, u32[]{:S(2)}) collective-permute-start(bf16[2,512,128]{2,1,0:T(8,128)(2,1)S(1)} %get-tuple-element.51.refs_0_), channel_id=1, source_target_pairs={{0,1},{1,2},{2,3},{3,0},{4,5},{5,6},{6,7},{7,4},{8,9},{9,10},{10,1... | collective-permute-start | bytes 786440 | tf_op jit(solution)/shard_map/ppermute | solution.py:43
  102.1 7.6 %collective-permute-start.30 = (bf16[2,512,128]{2,1,0:T(8,128)(2,1)S(1)}, bf16[2,512,128]{2,1,0:T(8,128)(2,1)S(1)}, u32[]{:S(2)}, u32[]{:S(2)}) collective-permute-start(bf16[2,512,128]{2,1,0:T(8,128)(2,1)S(1)} %get-tuple-element.51.refs_0_), channel_id=1, source_target_pairs={{0,3},{1,0},{2,1},{3,2},{4,7},{5,4},{6,5},{7,6},{8,11},{9,8},{10,9... | collective-permute-start | bytes 786440 | tf_op jit(solution)/shard_map/ppermute | solution.py:43
  109.9 23.0 %collective-permute-start.34 = (bf16[7,512,128]{2,1,0:T(8,128)(2,1)S(1)}, bf16[7,512,128]{2,1,0:T(8,128)(2,1)S(1)}, u32[]{:S(2)}, u32[]{:S(2)}) collective-permute-start(bf16[7,512,128]{2,1,0:T(8,128)(2,1)S(1)} %get-tuple-element.74), channel_id=1, source_target_pairs={{0,1},{1,2},{2,3},{3,0},{4,5},{5,6},{6,7},{7,4},{8,9},{9,10},{10,1... | collective-permute-start | bytes 2752520 | tf_op jit(solution)/shard_map/ppermute | solution.py:43
  110.6 22.3 %collective-permute-start.35 = (bf16[7,512,128]{2,1,0:T(8,128)(2,1)S(1)}, bf16[7,512,128]{2,1,0:T(8,128)(2,1)S(1)}, u32[]{:S(2)}, u32[]{:S(2)}) collective-permute-start(bf16[7,512,128]{2,1,0:T(8,128)(2,1)S(1)} %get-tuple-element.73), channel_id=1, source_target_pairs={{0,3},{1,0},{2,1},{3,2},{4,7},{5,4},{6,5},{7,6},{8,11},{9,8},{10,9... | collective-permute-start | bytes 2752520 | tf_op jit(solution)/shard_map/ppermute | solution.py:43
  112.6 20.3 %collective-permute-start.36 = (bf16[6,512,128]{2,1,0:T(8,128)(2,1)S(1)}, bf16[6,512,128]{2,1,0:T(8,128)(2,1)S(1)}, u32[]{:S(2)}, u32[]{:S(2)}) collective-permute-start(bf16[6,512,128]{2,1,0:T(8,128)(2,1)S(1)} %pad_maximum_fusion.8.token_ref), channel_id=1, source_target_pairs={{0,2},{1,3},{2,0},{3,1},{4,6},{5,7},{6,4},{7,5},{8,10},{9,11},{10,... | collective-permute-start | bytes 2359304 | tf_op jit(solution)/shard_map/ppermute | solution.py:43
  113.4 8.7 %collective-permute-start.31 = (bf16[2,512,128]{2,1,0:T(8,128)(2,1)S(1)}, bf16[2,512,128]{2,1,0:T(8,128)(2,1)S(1)}, u32[]{:S(2)}, u32[]{:S(2)}) collective-permute-start(bf16[2,512,128]{2,1,0:T(8,128)(2,1)S(1)} %get-tuple-element.51.refs_0_), channel_id=1, source_target_pairs={{0,32},{1,33},{2,34},{3,35},{4,36},{5,37},{6,38},{7,39},{8,40},{9,... | collective-permute-start | bytes 786440 | tf_op jit(solution)/shard_map/ppermute | solution.py:43
  115.0 11.6 %collective-permute-start.32 = (bf16[2,512,128]{2,1,0:T(8,128)(2,1)S(1)}, bf16[2,512,128]{2,1,0:T(8,128)(2,1)S(1)}, u32[]{:S(2)}, u32[]{:S(2)}) collective-permute-start(bf16[2,512,128]{2,1,0:T(8,128)(2,1)S(1)} %get-tuple-element.51.refs_0_), channel_id=1, source_target_pairs={{0,96},{1,97},{2,98},{3,99},{4,100},{5,101},{6,102},{7,103},{8,104... | collective-permute-start | bytes 786440 | tf_op jit(solution)/shard_map/ppermute | solution.py:43
  122.1 7.0 %collective-permute-start.33 = (bf16[2,512,128]{2,1,0:T(8,128)(2,1)S(1)}, bf16[2,512,128]{2,1,0:T(8,128)(2,1)S(1)}, u32[]{:S(2)}, u32[]{:S(2)}) collective-permute-start(bf16[2,512,128]{2,1,0:T(8,128)(2,1)S(1)} %get-tuple-element.51.refs_0_), channel_id=1, source_target_pairs={{0,64},{1,65},{2,66},{3,67},{4,68},{5,69},{6,70},{7,71},{8,72},{9,... | collective-permute-start | bytes 786440 | tf_op jit(solution)/shard_map/ppermute | solution.py:43
  136.6 9.4 %collective-permute-start.37 = (bf16[2,512,128]{2,1,0:T(8,128)(2,1)S(1)}, bf16[2,512,128]{2,1,0:T(8,128)(2,1)S(1)}, u32[]{:S(2)}, u32[]{:S(2)}) collective-permute-start(bf16[2,512,128]{2,1,0:T(8,128)(2,1)S(1)} %get-tuple-element.56.refs_0_), channel_id=1, source_target_pairs={{0,4},{1,5},{2,6},{3,7},{4,8},{5,9},{6,10},{7,11},{8,12},{9,13},{1... | collective-permute-start | bytes 786440 | tf_op jit(solution)/shard_map/ppermute | solution.py:43
  137.5 8.5 %collective-permute-start.38 = (bf16[2,512,128]{2,1,0:T(8,128)(2,1)S(1)}, bf16[2,512,128]{2,1,0:T(8,128)(2,1)S(1)}, u32[]{:S(2)}, u32[]{:S(2)}) collective-permute-start(bf16[2,512,128]{2,1,0:T(8,128)(2,1)S(1)} %get-tuple-element.56.refs_0_), channel_id=1, source_target_pairs={{0,12},{1,13},{2,14},{3,15},{4,0},{5,1},{6,2},{7,3},{8,4},{9,5},{1... | collective-permute-start | bytes 786440 | tf_op jit(solution)/shard_map/ppermute | solution.py:43
  139.4 7.4 %collective-permute-start.39 = (bf16[2,512,128]{2,1,0:T(8,128)(2,1)S(1)}, bf16[2,512,128]{2,1,0:T(8,128)(2,1)S(1)}, u32[]{:S(2)}, u32[]{:S(2)}) collective-permute-start(bf16[2,512,128]{2,1,0:T(8,128)(2,1)S(1)} %get-tuple-element.56.refs_0_), channel_id=1, source_target_pairs={{0,8},{1,9},{2,10},{3,11},{4,12},{5,13},{6,14},{7,15},{8,0},{9,1},... | collective-permute-start | bytes 786440 | tf_op jit(solution)/shard_map/ppermute | solution.py:43
  139.9 3.4 %collective-permute-start.40 = (bf16[512,128]{1,0:T(8,128)(2,1)S(1)}, bf16[512,128]{1,0:T(8,128)(2,1)S(1)}, u32[]{:S(2)}, u32[]{:S(2)}) collective-permute-start(bf16[512,128]{1,0:T(8,128)(2,1)S(1)} %get-tuple-element.54), channel_id=1, source_target_pairs={{0,16},{1,17},{2,18},{3,19},{4,20},{5,21},{6,22},{7,23},{8,24},{9,... | collective-permute-start | bytes 393224 | tf_op jit(solution)/shard_map/ppermute | solution.py:43
  143.3 8.5 %collective-permute-start.41 = (bf16[2,512,128]{2,1,0:T(8,128)(2,1)S(1)}, bf16[2,512,128]{2,1,0:T(8,128)(2,1)S(1)}, u32[]{:S(2)}, u32[]{:S(2)}) collective-permute-start(bf16[2,512,128]{2,1,0:T(8,128)(2,1)S(1)} %get-tuple-element.56.refs_0_), channel_id=1, source_target_pairs={{0,1},{1,2},{2,3},{3,0},{4,5},{5,6},{6,7},{7,4},{8,9},{9,10},{10,1... | collective-permute-start | bytes 786440 | tf_op jit(solution)/shard_map/ppermute | solution.py:43
  143.4 8.4 %collective-permute-start.42 = (bf16[2,512,128]{2,1,0:T(8,128)(2,1)S(1)}, bf16[2,512,128]{2,1,0:T(8,128)(2,1)S(1)}, u32[]{:S(2)}, u32[]{:S(2)}) collective-permute-start(bf16[2,512,128]{2,1,0:T(8,128)(2,1)S(1)} %get-tuple-element.56.refs_0_), channel_id=1, source_target_pairs={{0,3},{1,0},{2,1},{3,2},{4,7},{5,4},{6,5},{7,6},{8,11},{9,8},{10,9... | collective-permute-start | bytes 786440 | tf_op jit(solution)/shard_map/ppermute | solution.py:43
  152.0 23.0 %collective-permute-start.46 = (bf16[7,512,128]{2,1,0:T(8,128)(2,1)S(1)}, bf16[7,512,128]{2,1,0:T(8,128)(2,1)S(1)}, u32[]{:S(2)}, u32[]{:S(2)}) collective-permute-start(bf16[7,512,128]{2,1,0:T(8,128)(2,1)S(1)} %get-tuple-element.72), channel_id=1, source_target_pairs={{0,1},{1,2},{2,3},{3,0},{4,5},{5,6},{6,7},{7,4},{8,9},{9,10},{10,1... | collective-permute-start | bytes 2752520 | tf_op jit(solution)/shard_map/ppermute | solution.py:43
  152.1 22.9 %collective-permute-start.47 = (bf16[7,512,128]{2,1,0:T(8,128)(2,1)S(1)}, bf16[7,512,128]{2,1,0:T(8,128)(2,1)S(1)}, u32[]{:S(2)}, u32[]{:S(2)}) collective-permute-start(bf16[7,512,128]{2,1,0:T(8,128)(2,1)S(1)} %get-tuple-element.71), channel_id=1, source_target_pairs={{0,3},{1,0},{2,1},{3,2},{4,7},{5,4},{6,5},{7,6},{8,11},{9,8},{10,9... | collective-permute-start | bytes 2752520 | tf_op jit(solution)/shard_map/ppermute | solution.py:43
  154.8 20.2 %collective-permute-start.48 = (bf16[6,512,128]{2,1,0:T(8,128)(2,1)S(1)}, bf16[6,512,128]{2,1,0:T(8,128)(2,1)S(1)}, u32[]{:S(2)}, u32[]{:S(2)}) collective-permute-start(bf16[6,512,128]{2,1,0:T(8,128)(2,1)S(1)} %pad_maximum_fusion.9.token_ref), channel_id=1, source_target_pairs={{0,2},{1,3},{2,0},{3,1},{4,6},{5,7},{6,4},{7,5},{8,10},{9,11},{10,... | collective-permute-start | bytes 2359304 | tf_op jit(solution)/shard_map/ppermute | solution.py:43
  155.5 9.8 %collective-permute-start.43 = (bf16[2,512,128]{2,1,0:T(8,128)(2,1)S(1)}, bf16[2,512,128]{2,1,0:T(8,128)(2,1)S(1)}, u32[]{:S(2)}, u32[]{:S(2)}) collective-permute-start(bf16[2,512,128]{2,1,0:T(8,128)(2,1)S(1)} %get-tuple-element.56.refs_0_), channel_id=1, source_target_pairs={{0,32},{1,33},{2,34},{3,35},{4,36},{5,37},{6,38},{7,39},{8,40},{9,... | collective-permute-start | bytes 786440 | tf_op jit(solution)/shard_map/ppermute | solution.py:43
  157.2 12.6 %collective-permute-start.44 = (bf16[2,512,128]{2,1,0:T(8,128)(2,1)S(1)}, bf16[2,512,128]{2,1,0:T(8,128)(2,1)S(1)}, u32[]{:S(2)}, u32[]{:S(2)}) collective-permute-start(bf16[2,512,128]{2,1,0:T(8,128)(2,1)S(1)} %get-tuple-element.56.refs_0_), channel_id=1, source_target_pairs={{0,96},{1,97},{2,98},{3,99},{4,100},{5,101},{6,102},{7,103},{8,104... | collective-permute-start | bytes 786440 | tf_op jit(solution)/shard_map/ppermute | solution.py:43
  165.3 8.1 %collective-permute-start.45 = (bf16[2,512,128]{2,1,0:T(8,128)(2,1)S(1)}, bf16[2,512,128]{2,1,0:T(8,128)(2,1)S(1)}, u32[]{:S(2)}, u32[]{:S(2)}) collective-permute-start(bf16[2,512,128]{2,1,0:T(8,128)(2,1)S(1)} %get-tuple-element.56.refs_0_), channel_id=1, source_target_pairs={{0,64},{1,65},{2,66},{3,67},{4,68},{5,69},{6,70},{7,71},{8,72},{9,... | collective-permute-start | bytes 786440 | tf_op jit(solution)/shard_map/ppermute | solution.py:43
  (8 other events, 54.7 us)

commit v4 on v3

--- a/solution.py
+++ b/solution.py
@@ -159,7 +159,7 @@
         scratch_shapes=[pltpu.VMEM((2, 8, rows, columns), jnp.bfloat16)],
         compiler_params=pltpu.CompilerParams(vmem_limit_bytes=24 * 1024 * 1024),
         cost_estimate=pl.CostEstimate(
-            flops=2 * 16 * rows * rows * columns, bytes_accessed=16 * rows * columns * 2, transcendentals=0
+            flops=8 * 16 * rows * rows * columns, bytes_accessed=16 * rows * columns * 2, transcendentals=0
         ),
     )(where, *sources, mine, theirs, factor)
 
@@ -240,10 +240,14 @@
         draws, give = level_call(level, where, sources, own_terms, other_terms, factor)
         kept.append(draws[0])
         given.append(give)
-    got.append(send(given[-1], OTHER))
-    left = jnp.stack(kept)
-    right = jnp.stack(got)
-    whole = jnp.where(low, jnp.concatenate([left, right], axis=-1), jnp.concatenate([right, left], axis=-1))
+    def joined(left, right):
+        return jnp.where(low, jnp.concatenate([left, right], axis=-1), jnp.concatenate([right, left], axis=-1))
+
+    levels = len(kept)
+    whole = joined(jnp.stack(kept[:-1]), jnp.stack(got))
+    whole = jnp.concatenate([whole, jnp.zeros_like(whole[:1])])
+    last = joined(kept[-1], send(given[-1], OTHER))
+    whole = lax.dynamic_update_slice(whole, last[None], (levels - 1, 0, 0))
     return whole[:, None, None]
 
 

time: 182 us -> 182 us (level)
  transfers between devices with their start and end apart: 50 -> 50, of which waited for: 23 -> 23; matrix products, arithmetic and copies ran while one was open for 1% -> 2% of each run, Pallas kernels for 10% -> 10%
where the time goes in v4:
time: 182 us
  waiting for transfers between devices  71.6 us (39%)
  starting transfers between devices  69.2 us (38%)
  Pallas kernels  33.1 us (18%)
  local copies, waits for them, and re-layouts  4.16 us (2%)
  other arithmetic  3.39 us (2%)
    ppermute x50, waiting for transfers between devices, send(): return lax.ppermute(value, AXES, route)  71.6 us
    ppermute x50, starting transfers between devices, send(): return lax.ppermute(value, AXES, route)  69.2 us
    pallas_call x4, Pallas kernels, level_call(): pl.pallas_call(functools.partial(level_kernel, level, len(sources)), out_...  15 us
    pallas_call x4, Pallas kernels, stage_call(): pl.pallas_call(functools.partial(stage_kernel, level), out_shape=jax.Shap...  13.9 us
    pallas_call x1, Pallas kernels, noise_call(): pl.pallas_call(noise_kernel, out_shape=(shape, shape), in_specs=[SMEM, HB...  4.23 us
  transfers between devices with their start and end apart: 50, of which 23 were waited for; matrix products, arithmetic and copies ran while one was open for 2% of the time, Pallas kernels for 10%

profile of v4, /device:TPU:1, one launch (start us, length us, event | category | flops | bytes accessed | tf_op | source)
XLA Modules:
  0.0 182.0 jit_solution(2447359907126487455)
XLA Ops:
  2.6 4.2 %shard_map.64 = (f32[4,512,128]{2,1,0:T(8,128)}, f32[4,512,128]{2,1,0:T(8,128)}) custom-call(s32[1]{0:T(128)} %bitcast.3.core_ref, bf16[4,512,512]{2,1,0:T(8,128)(2,1)} %bitcast.26, bf16[4,512,256]{2,1,0:T(8,128)(2,1)} %bitcast.27), custom_call_target="tpu_custom_call" | custom-call | flops 536870912 | bytes 4194304 | tf_op jit(solution)/shard_map/pallas_call | solution.py:72
  8.7 2.3 %collective-permute-done.11.refs_13_ = f32[4,512,128]{2,1,0:T(8,128)S(1)} collective-permute-done((f32[4,512,128]{2,1,0:T(8,128)S(1)}, f32[4,512,128]{2,1,0:T(8,128)S(1)}, u32[]{:S(2)}, u32[]{:S(2)}) %collective-permute-start.11) | collective-permute-done | bytes 1048608 | tf_op jit(solution)/shard_map/ppermute | solution.py:43
  14.1 1.6 collective-permute-start.4
  15.8 2.4 %collective-permute-done.2.refs_1_ = bf16[2,512,128]{2,1,0:T(8,128)(2,1)S(1)} collective-permute-done((bf16[2,512,128]{2,1,0:T(8,128)(2,1)S(1)}, bf16[2,512,128]{2,1,0:T(8,128)(2,1)S(1)}, u32[]{:S(2)}, u32[]{:S(2)}) %collective-permute-start.2) | collective-permute-done | bytes 262176 | tf_op jit(solution)/shard_map/ppermute | solution.py:43
  18.2 4.0 %collective-permute-done.4.refs_3_ = bf16[2,512,128]{2,1,0:T(8,128)(2,1)S(1)} collective-permute-done((bf16[2,512,128]{2,1,0:T(8,128)(2,1)S(1)}, bf16[2,512,128]{2,1,0:T(8,128)(2,1)S(1)}, u32[]{:S(2)}, u32[]{:S(2)}) %collective-permute-start.4) | collective-permute-done | bytes 262176 | tf_op jit(solution)/shard_map/ppermute | solution.py:43
  22.4 2.5 %collective-permute-start.10 = (bf16[8,512,128]{2,1,0:T(8,128)(2,1)S(1)}, bf16[8,512,128]{2,1,0:T(8,128)(2,1)S(1)}, u32[]{:S(2)}, u32[]{:S(2)}) collective-permute-start(bf16[8,512,128]{2,1,0:T(8,128)(2,1)S(1)} %constant_dynamic-update-slice_fusion), channel_id=1, source_target_pairs={{0,2},{1,3},{2,0},{3,1},{4,6},{5,7},{6,4},{7,5},{8,10},{9,11},{10,... | collective-permute-start | bytes 3145736 | tf_op jit(solution)/shard_map/ppermute | solution.py:43
  25.2 2.4 %collective-permute-start.9 = (bf16[8,512,128]{2,1,0:T(8,128)(2,1)S(1)}, bf16[8,512,128]{2,1,0:T(8,128)(2,1)S(1)}, u32[]{:S(2)}, u32[]{:S(2)}) collective-permute-start(bf16[8,512,128]{2,1,0:T(8,128)(2,1)S(1)} %constant_dynamic-update-slice_fusion), channel_id=1, source_target_pairs={{0,3},{1,0},{2,1},{3,2},{4,7},{5,4},{6,5},{7,6},{8,11},{9,8},{10,9... | collective-permute-start | bytes 3145736 | tf_op jit(solution)/shard_map/ppermute | solution.py:43
  27.6 1.6 collective-permute-start.5
  29.2 6.7 %collective-permute-done.5.refs_6_ = bf16[2,512,128]{2,1,0:T(8,128)(2,1)S(1)} collective-permute-done((bf16[2,512,128]{2,1,0:T(8,128)(2,1)S(1)}, bf16[2,512,128]{2,1,0:T(8,128)(2,1)S(1)}, u32[]{:S(2)}, u32[]{:S(2)}) %collective-permute-start.5) | collective-permute-done | bytes 262176 | tf_op jit(solution)/shard_map/ppermute | solution.py:43
  37.1 2.9 %collective-permute-start.7 = (bf16[2,512,128]{2,1,0:T(8,128)(2,1)S(1)}, bf16[2,512,128]{2,1,0:T(8,128)(2,1)S(1)}, u32[]{:S(2)}, u32[]{:S(2)}) collective-permute-start(bf16[2,512,128]{2,1,0:T(8,128)(2,1)S(1)} %pad_maximum_fusion.10.refs_0_.refs_4_.refs_5_), channel_id=1, source_target_pairs={{0,64},{1,65},{2,66},{3,67},{4,68},{5,69},{6,70},{7,71},{8,72},{9,... | collective-permute-start | bytes 786440 | tf_op jit(solution)/shard_map/ppermute | solution.py:43
  40.0 2.9 %copy-done.3 = bf16[4,8,512,512]{3,2,1,0:T(8,128)(2,1)} copy-done((bf16[4,8,512,512]{3,2,1,0:T(8,128)(2,1)}, bf16[4,8,512,512]{3,2,1,0:T(8,128)(2,1)S(1)}, u32[]{:S(2)}) %copy-start.3) | copy-done | bytes 16777240
  42.9 3.5 %shard_map.65.refs_14_ = bf16[2,8,512,512]{3,2,1,0:T(8,128)(2,1)S(1)} custom-call(bf16[6,512,128]{2,1,0:T(8,128)(2,1)S(1)} %pad_maximum_fusion.6.token_ref, bf16[4,8,512,512]{3,2,1,0:T(8,128)(2,1)} %bitcast.22, bf16[4,8,512,512]{3,2,1,0:T(8,128)(2,1)} %copy-done.3), custom_call_target="tpu_custom_call" | custom-call | bytes 8388608 | tf_op jit(solution)/shard_map/pallas_call | solution.py:118
  46.4 2.7 %collective-permute-done.8.refs_9_ = bf16[8,512,128]{2,1,0:T(8,128)(2,1)S(1)} collective-permute-done((bf16[8,512,128]{2,1,0:T(8,128)(2,1)S(1)}, bf16[8,512,128]{2,1,0:T(8,128)(2,1)S(1)}, u32[]{:S(2)}, u32[]{:S(2)}) %collective-permute-start.8) | collective-permute-done | bytes 1048608 | tf_op jit(solution)/shard_map/ppermute | solution.py:43
  49.2 3.7 %shard_map.66 = (bf16[2,512,128]{2,1,0:T(8,128)(2,1)S(1)}, bf16[512,128]{1,0:T(8,128)(2,1)S(1)}) custom-call(s32[4,2,8]{2,1,0:T(2,128)S(1)} %compare_select_fusion.23.where_ref, bf16[2,512,128]{2,1,0:T(8,128)(2,1)S(1)} %pad_maximum_fusion.10.refs_0_.refs_4_.refs_5_, bf16[2,512,128]{2,1,0:T(8,128)(2,1)S(1)} %collective-permute-done.2.refs_1_, ...), custom_call_target="tpu_custom_call" | custom-call | flops 4294967296 | bytes 2097152 | tf_op jit(solution)/shard_map/pallas_call | solution.py:151
  53.9 1.7 collective-permute-start.14
  55.8 2.8 %collective-permute-start.16 = (bf16[512,128]{1,0:T(8,128)(2,1)S(1)}, bf16[512,128]{1,0:T(8,128)(2,1)S(1)}, u32[]{:S(2)}, u32[]{:S(2)}) collective-permute-start(bf16[512,128]{1,0:T(8,128)(2,1)S(1)} %get-tuple-element.44), channel_id=1, source_target_pairs={{0,16},{1,17},{2,18},{3,19},{4,20},{5,21},{6,22},{7,23},{8,24},{9,... | collective-permute-start | bytes 393224 | tf_op jit(solution)/shard_map/ppermute | solution.py:43
  62.4 5.7 %collective-permute-done.17.refs_4_ = bf16[2,512,128]{2,1,0:T(8,128)(2,1)S(1)} collective-permute-done((bf16[2,512,128]{2,1,0:T(8,128)(2,1)S(1)}, bf16[2,512,128]{2,1,0:T(8,128)(2,1)S(1)}, u32[]{:S(2)}, u32[]{:S(2)}) %collective-permute-start.17) | collective-permute-done | bytes 262176 | tf_op jit(solution)/shard_map/ppermute | solution.py:43
  69.3 1.8 collective-permute-start.23
  71.8 1.6 collective-permute-start.19
  73.4 2.1 %collective-permute-start.20 = (bf16[2,512,128]{2,1,0:T(8,128)(2,1)S(1)}, bf16[2,512,128]{2,1,0:T(8,128)(2,1)S(1)}, u32[]{:S(2)}, u32[]{:S(2)}) collective-permute-start(bf16[2,512,128]{2,1,0:T(8,128)(2,1)S(1)} %get-tuple-element.46.refs_0_), channel_id=1, source_target_pairs={{0,96},{1,97},{2,98},{3,99},{4,100},{5,101},{6,102},{7,103},{8,104... | collective-permute-start | bytes 786440 | tf_op jit(solution)/shard_map/ppermute | solution.py:43
  75.6 5.8 %collective-permute-done.19.refs_6_ = bf16[2,512,128]{2,1,0:T(8,128)(2,1)S(1)} collective-permute-done((bf16[2,512,128]{2,1,0:T(8,128)(2,1)S(1)}, bf16[2,512,128]{2,1,0:T(8,128)(2,1)S(1)}, u32[]{:S(2)}, u32[]{:S(2)}) %collective-permute-start.19) | collective-permute-done | bytes 262176 | tf_op jit(solution)/shard_map/ppermute | solution.py:43
  82.3 3.5 %shard_map.67.refs_14_ = bf16[2,8,512,512]{3,2,1,0:T(8,128)(2,1)S(1)} custom-call(bf16[6,512,128]{2,1,0:T(8,128)(2,1)S(1)} %pad_maximum_fusion.7.token_ref, bf16[4,8,512,512]{3,2,1,0:T(8,128)(2,1)} %bitcast.23, bf16[4,8,512,512]{3,2,1,0:T(8,128)(2,1)} %copy-done.3), custom_call_target="tpu_custom_call" | custom-call | bytes 8388608 | tf_op jit(solution)/shard_map/pallas_call | solution.py:118
  85.8 3.4 %collective-permute-done.21.refs_8_ = bf16[2,512,128]{2,1,0:T(8,128)(2,1)S(1)} collective-permute-done((bf16[2,512,128]{2,1,0:T(8,128)(2,1)S(1)}, bf16[2,512,128]{2,1,0:T(8,128)(2,1)S(1)}, u32[]{:S(2)}, u32[]{:S(2)}) %collective-permute-start.21) | collective-permute-done | bytes 262176 | tf_op jit(solution)/shard_map/ppermute | solution.py:43
  89.2 2.1 %collective-permute-done.24.refs_11_ = bf16[6,512,128]{2,1,0:T(8,128)(2,1)S(1)} collective-permute-done((bf16[6,512,128]{2,1,0:T(8,128)(2,1)S(1)}, bf16[6,512,128]{2,1,0:T(8,128)(2,1)S(1)}, u32[]{:S(2)}, u32[]{:S(2)}) %collective-permute-start.24) | collective-permute-done | bytes 786464 | tf_op jit(solution)/shard_map/ppermute | solution.py:43
  91.3 3.7 %shard_map.68 = (bf16[2,512,128]{2,1,0:T(8,128)(2,1)S(1)}, bf16[512,128]{1,0:T(8,128)(2,1)S(1)}) custom-call(s32[4,2,8]{2,1,0:T(2,128)S(1)} %compare_select_fusion.23.where_ref, bf16[2,512,128]{2,1,0:T(8,128)(2,1)S(1)} %get-tuple-element.46.refs_0_, bf16[2,512,128]{2,1,0:T(8,128)(2,1)S(1)} %collective-permute-done.13.refs_1_, ...), custom_call_target="tpu_custom_call" | custom-call | flops 4294967296 | bytes 2097152 | tf_op jit(solution)/shard_map/pallas_call | solution.py:151
  98.8 2.4 %collective-permute-start.28 = (bf16[512,128]{1,0:T(8,128)(2,1)S(1)}, bf16[512,128]{1,0:T(8,128)(2,1)S(1)}, u32[]{:S(2)}, u32[]{:S(2)}) collective-permute-start(bf16[512,128]{1,0:T(8,128)(2,1)S(1)} %get-tuple-element.49), channel_id=1, source_target_pairs={{0,16},{1,17},{2,18},{3,19},{4,20},{5,21},{6,22},{7,23},{8,24},{9,... | collective-permute-start | bytes 393224 | tf_op jit(solution)/shard_map/ppermute | solution.py:43
  102.2 2.7 %collective-permute-start.30 = (bf16[2,512,128]{2,1,0:T(8,128)(2,1)S(1)}, bf16[2,512,128]{2,1,0:T(8,128)(2,1)S(1)}, u32[]{:S(2)}, u32[]{:S(2)}) collective-permute-start(bf16[2,512,128]{2,1,0:T(8,128)(2,1)S(1)} %get-tuple-element.51.refs_0_), channel_id=1, source_target_pairs={{0,3},{1,0},{2,1},{3,2},{4,7},{5,4},{6,5},{7,6},{8,11},{9,8},{10,9... | collective-permute-start | bytes 786440 | tf_op jit(solution)/shard_map/ppermute | solution.py:43
  105.7 4.0 %collective-permute-done.29.refs_4_ = bf16[2,512,128]{2,1,0:T(8,128)(2,1)S(1)} collective-permute-done((bf16[2,512,128]{2,1,0:T(8,128)(2,1)S(1)}, bf16[2,512,128]{2,1,0:T(8,128)(2,1)S(1)}, u32[]{:S(2)}, u32[]{:S(2)}) %collective-permute-start.29) | collective-permute-done | bytes 262176 | tf_op jit(solution)/shard_map/ppermute | solution.py:43
  110.6 2.0 %collective-permute-start.35 = (bf16[7,512,128]{2,1,0:T(8,128)(2,1)S(1)}, bf16[7,512,128]{2,1,0:T(8,128)(2,1)S(1)}, u32[]{:S(2)}, u32[]{:S(2)}) collective-permute-start(bf16[7,512,128]{2,1,0:T(8,128)(2,1)S(1)} %get-tuple-element.73), channel_id=1, source_target_pairs={{0,3},{1,0},{2,1},{3,2},{4,7},{5,4},{6,5},{7,6},{8,11},{9,8},{10,9... | collective-permute-start | bytes 2752520 | tf_op jit(solution)/shard_map/ppermute | solution.py:43
  113.4 1.7 collective-permute-start.31
  115.0 2.1 %collective-permute-start.32 = (bf16[2,512,128]{2,1,0:T(8,128)(2,1)S(1)}, bf16[2,512,128]{2,1,0:T(8,128)(2,1)S(1)}, u32[]{:S(2)}, u32[]{:S(2)}) collective-permute-start(bf16[2,512,128]{2,1,0:T(8,128)(2,1)S(1)} %get-tuple-element.51.refs_0_), channel_id=1, source_target_pairs={{0,96},{1,97},{2,98},{3,99},{4,100},{5,101},{6,102},{7,103},{8,104... | collective-permute-start | bytes 786440 | tf_op jit(solution)/shard_map/ppermute | solution.py:43
  117.2 5.0 %collective-permute-done.31.refs_6_ = bf16[2,512,128]{2,1,0:T(8,128)(2,1)S(1)} collective-permute-done((bf16[2,512,128]{2,1,0:T(8,128)(2,1)S(1)}, bf16[2,512,128]{2,1,0:T(8,128)(2,1)S(1)}, u32[]{:S(2)}, u32[]{:S(2)}) %collective-permute-start.31) | collective-permute-done | bytes 262176 | tf_op jit(solution)/shard_map/ppermute | solution.py:43
  123.1 3.5 %shard_map.69.refs_14_ = bf16[2,8,512,512]{3,2,1,0:T(8,128)(2,1)S(1)} custom-call(bf16[6,512,128]{2,1,0:T(8,128)(2,1)S(1)} %pad_maximum_fusion.8.token_ref, bf16[4,8,512,512]{3,2,1,0:T(8,128)(2,1)} %bitcast.24, bf16[4,8,512,512]{3,2,1,0:T(8,128)(2,1)} %copy-done.3), custom_call_target="tpu_custom_call" | custom-call | bytes 8388608 | tf_op jit(solution)/shard_map/pallas_call | solution.py:118
  126.6 2.5 %collective-permute-done.33.refs_8_ = bf16[2,512,128]{2,1,0:T(8,128)(2,1)S(1)} collective-permute-done((bf16[2,512,128]{2,1,0:T(8,128)(2,1)S(1)}, bf16[2,512,128]{2,1,0:T(8,128)(2,1)S(1)}, u32[]{:S(2)}, u32[]{:S(2)}) %collective-permute-start.33) | collective-permute-done | bytes 262176 | tf_op jit(solution)/shard_map/ppermute | solution.py:43
  129.2 3.7 %collective-permute-done.36.refs_11_ = bf16[6,512,128]{2,1,0:T(8,128)(2,1)S(1)} collective-permute-done((bf16[6,512,128]{2,1,0:T(8,128)(2,1)S(1)}, bf16[6,512,128]{2,1,0:T(8,128)(2,1)S(1)}, u32[]{:S(2)}, u32[]{:S(2)}) %collective-permute-start.36) | collective-permute-done | bytes 786464 | tf_op jit(solution)/shard_map/ppermute | solution.py:43
  132.9 3.7 %shard_map.70 = (bf16[2,512,128]{2,1,0:T(8,128)(2,1)S(1)}, bf16[512,128]{1,0:T(8,128)(2,1)S(1)}) custom-call(s32[4,2,8]{2,1,0:T(2,128)S(1)} %compare_select_fusion.23.where_ref, bf16[2,512,128]{2,1,0:T(8,128)(2,1)S(1)} %get-tuple-element.51.refs_0_, bf16[2,512,128]{2,1,0:T(8,128)(2,1)S(1)} %collective-permute-done.25.refs_1_, ...), custom_call_target="tpu_custom_call" | custom-call | flops 4294967296 | bytes 2097152 | tf_op jit(solution)/shard_map/pallas_call | solution.py:151
  137.6 1.8 collective-permute-start.39
  139.9 2.5 %collective-permute-start.37 = (bf16[512,128]{1,0:T(8,128)(2,1)S(1)}, bf16[512,128]{1,0:T(8,128)(2,1)S(1)}, u32[]{:S(2)}, u32[]{:S(2)}) collective-permute-start(bf16[512,128]{1,0:T(8,128)(2,1)S(1)} %get-tuple-element.56), channel_id=1, source_target_pairs={{0,16},{1,17},{2,18},{3,19},{4,20},{5,21},{6,22},{7,23},{8,24},{9,... | collective-permute-start | bytes 393224 | tf_op jit(solution)/shard_map/ppermute | solution.py:43
  143.4 2.6 %collective-permute-start.42 = (bf16[2,512,128]{2,1,0:T(8,128)(2,1)S(1)}, bf16[2,512,128]{2,1,0:T(8,128)(2,1)S(1)}, u32[]{:S(2)}, u32[]{:S(2)}) collective-permute-start(bf16[2,512,128]{2,1,0:T(8,128)(2,1)S(1)} %get-tuple-element.59.refs_0_), channel_id=1, source_target_pairs={{0,3},{1,0},{2,1},{3,2},{4,7},{5,4},{6,5},{7,6},{8,11},{9,8},{10,9... | collective-permute-start | bytes 786440 | tf_op jit(solution)/shard_map/ppermute | solution.py:43
  146.8 5.1 %collective-permute-done.41.refs_4_ = bf16[2,512,128]{2,1,0:T(8,128)(2,1)S(1)} collective-permute-done((bf16[2,512,128]{2,1,0:T(8,128)(2,1)S(1)}, bf16[2,512,128]{2,1,0:T(8,128)(2,1)S(1)}, u32[]{:S(2)}, u32[]{:S(2)}) %collective-permute-start.41) | collective-permute-done | bytes 262176 | tf_op jit(solution)/shard_map/ppermute | solution.py:43
  152.1 2.7 %collective-permute-start.47 = (bf16[7,512,128]{2,1,0:T(8,128)(2,1)S(1)}, bf16[7,512,128]{2,1,0:T(8,128)(2,1)S(1)}, u32[]{:S(2)}, u32[]{:S(2)}) collective-permute-start(bf16[7,512,128]{2,1,0:T(8,128)(2,1)S(1)} %get-tuple-element.71), channel_id=1, source_target_pairs={{0,3},{1,0},{2,1},{3,2},{4,7},{5,4},{6,5},{7,6},{8,11},{9,8},{10,9... | collective-permute-start | bytes 2752520 | tf_op jit(solution)/shard_map/ppermute | solution.py:43
  155.5 1.7 collective-permute-start.43
  157.2 2.1 %collective-permute-start.44 = (bf16[2,512,128]{2,1,0:T(8,128)(2,1)S(1)}, bf16[2,512,128]{2,1,0:T(8,128)(2,1)S(1)}, u32[]{:S(2)}, u32[]{:S(2)}) collective-permute-start(bf16[2,512,128]{2,1,0:T(8,128)(2,1)S(1)} %get-tuple-element.59.refs_0_), channel_id=1, source_target_pairs={{0,96},{1,97},{2,98},{3,99},{4,100},{5,101},{6,102},{7,103},{8,104... | collective-permute-start | bytes 786440 | tf_op jit(solution)/shard_map/ppermute | solution.py:43
  159.3 5.9 %collective-permute-done.43.refs_6_ = bf16[2,512,128]{2,1,0:T(8,128)(2,1)S(1)} collective-permute-done((bf16[2,512,128]{2,1,0:T(8,128)(2,1)S(1)}, bf16[2,512,128]{2,1,0:T(8,128)(2,1)S(1)}, u32[]{:S(2)}, u32[]{:S(2)}) %collective-permute-start.43) | collective-permute-done | bytes 262176 | tf_op jit(solution)/shard_map/ppermute | solution.py:43
  166.3 3.5 %shard_map.71.refs_14_ = bf16[2,8,512,512]{3,2,1,0:T(8,128)(2,1)S(1)} custom-call(bf16[6,512,128]{2,1,0:T(8,128)(2,1)S(1)} %pad_maximum_fusion.9.token_ref, bf16[4,8,512,512]{3,2,1,0:T(8,128)(2,1)} %bitcast.25, bf16[4,8,512,512]{3,2,1,0:T(8,128)(2,1)} %copy-done.3), custom_call_target="tpu_custom_call" | custom-call | bytes 8388608 | tf_op jit(solution)/shard_map/pallas_call | solution.py:118
  169.8 3.4 %collective-permute-done.45.refs_8_ = bf16[2,512,128]{2,1,0:T(8,128)(2,1)S(1)} collective-permute-done((bf16[2,512,128]{2,1,0:T(8,128)(2,1)S(1)}, bf16[2,512,128]{2,1,0:T(8,128)(2,1)S(1)}, u32[]{:S(2)}, u32[]{:S(2)}) %collective-permute-start.45) | collective-permute-done | bytes 262176 | tf_op jit(solution)/shard_map/ppermute | solution.py:43
  173.2 1.8 collective-permute-done.48.refs_11_
  175.0 3.8 %shard_map.72 = (bf16[2,512,128]{2,1,0:T(8,128)(2,1)S(1)}, bf16[512,128]{1,0:T(8,128)(2,1)S(1)}) custom-call(s32[4,2,8]{2,1,0:T(2,128)S(1)} %compare_select_fusion.23.where_ref, bf16[2,512,128]{2,1,0:T(8,128)(2,1)S(1)} %get-tuple-element.59.refs_0_, bf16[2,512,128]{2,1,0:T(8,128)(2,1)S(1)} %collective-permute-done.38.refs_1_, ...), custom_call_target="tpu_custom_call" | custom-call | flops 4294967296 | bytes 2097152 | tf_op jit(solution)/shard_map/pallas_call | solution.py:151
  (111 shorter events, 33.7 us)
Async XLA Ops:
  0.0 6.8 %collective-permute-start.1 = (s32[4,8]{1,0:T(4,128)}, s32[4,8]{1,0:T(4,128)S(1)}, u32[]{:S(2)}, u32[]{:S(2)}) collective-permute-start(s32[4,8]{1,0:T(4,128)} %bitcast.34), channel_id=1, source_target_pairs={{0,16},{1,17},{2,18},{3,19},{4,20},{5,21},{6,22},{7,23},{8,24},{9,... | collective-permute-start | bytes 392 | tf_op jit(solution)/shard_map/ppermute | solution.py:43
  2.4 5.7 %collective-permute-start = (bf16[512,128]{1,0:T(8,128)(2,1)S(1)}, bf16[512,128]{1,0:T(8,128)(2,1)S(1)}, u32[]{:S(2)}, u32[]{:S(2)}) collective-permute-start(bf16[512,128]{1,0:T(8,128)(2,1)S(1)} %get-tuple-element.78), channel_id=1, source_target_pairs={{0,16},{1,17},{2,18},{3,19},{4,20},{5,21},{6,22},{7,23},{8,24},{9,... | collective-permute-start | bytes 393224 | tf_op jit(solution)/shard_map/ppermute | solution.py:43
  10.9 26.2 %collective-permute-start.12 = (bf16[4,8,512,512]{3,2,1,0:T(8,128)(2,1)}, bf16[4,8,512,512]{3,2,1,0:T(8,128)(2,1)S(1)}, u32[]{:S(2)}, u32[]{:S(2)}) collective-permute-start(bf16[4,8,512,512]{3,2,1,0:T(8,128)(2,1)} %bitcast.21), channel_id=1, source_target_pairs={{0,16},{1,17},{2,18},{3,19},{4,20},{5,21},{6,22},{7,23},{8,24},{9,... | collective-permute-start | bytes 50331656 | tf_op jit(solution)/shard_map/ppermute | solution.py:43
  11.3 6.9 %collective-permute-start.2 = (bf16[2,512,128]{2,1,0:T(8,128)(2,1)S(1)}, bf16[2,512,128]{2,1,0:T(8,128)(2,1)S(1)}, u32[]{:S(2)}, u32[]{:S(2)}) collective-permute-start(bf16[2,512,128]{2,1,0:T(8,128)(2,1)S(1)} %pad_maximum_fusion.10.refs_0_.refs_4_.refs_5_), channel_id=1, source_target_pairs={{0,4},{1,5},{2,6},{3,7},{4,8},{5,9},{6,10},{7,11},{8,12},{9,13},{1... | collective-permute-start | bytes 786440 | tf_op jit(solution)/shard_map/ppermute | solution.py:43
  12.7 5.5 %collective-permute-start.3 = (bf16[2,512,128]{2,1,0:T(8,128)(2,1)S(1)}, bf16[2,512,128]{2,1,0:T(8,128)(2,1)S(1)}, u32[]{:S(2)}, u32[]{:S(2)}) collective-permute-start(bf16[2,512,128]{2,1,0:T(8,128)(2,1)S(1)} %pad_maximum_fusion.10.refs_0_.refs_4_.refs_5_), channel_id=1, source_target_pairs={{0,12},{1,13},{2,14},{3,15},{4,0},{5,1},{6,2},{7,3},{8,4},{9,5},{1... | collective-permute-start | bytes 786440 | tf_op jit(solution)/shard_map/ppermute | solution.py:43
  14.1 8.0 %collective-permute-start.4 = (bf16[2,512,128]{2,1,0:T(8,128)(2,1)S(1)}, bf16[2,512,128]{2,1,0:T(8,128)(2,1)S(1)}, u32[]{:S(2)}, u32[]{:S(2)}) collective-permute-start(bf16[2,512,128]{2,1,0:T(8,128)(2,1)S(1)} %pad_maximum_fusion.10.refs_0_.refs_4_.refs_5_), channel_id=1, source_target_pairs={{0,8},{1,9},{2,10},{3,11},{4,12},{5,13},{6,14},{7,15},{8,0},{9,1},... | collective-permute-start | bytes 786440 | tf_op jit(solution)/shard_map/ppermute | solution.py:43
  22.4 24.0 %collective-permute-start.10 = (bf16[8,512,128]{2,1,0:T(8,128)(2,1)S(1)}, bf16[8,512,128]{2,1,0:T(8,128)(2,1)S(1)}, u32[]{:S(2)}, u32[]{:S(2)}) collective-permute-start(bf16[8,512,128]{2,1,0:T(8,128)(2,1)S(1)} %constant_dynamic-update-slice_fusion), channel_id=1, source_target_pairs={{0,2},{1,3},{2,0},{3,1},{4,6},{5,7},{6,4},{7,5},{8,10},{9,11},{10,... | collective-permute-start | bytes 3145736 | tf_op jit(solution)/shard_map/ppermute | solution.py:43
  24.9 24.2 %collective-permute-start.8 = (bf16[8,512,128]{2,1,0:T(8,128)(2,1)S(1)}, bf16[8,512,128]{2,1,0:T(8,128)(2,1)S(1)}, u32[]{:S(2)}, u32[]{:S(2)}) collective-permute-start(bf16[8,512,128]{2,1,0:T(8,128)(2,1)S(1)} %constant_dynamic-update-slice_fusion), channel_id=1, source_target_pairs={{0,1},{1,2},{2,3},{3,0},{4,5},{5,6},{6,7},{7,4},{8,9},{9,10},{10,1... | collective-permute-start | bytes 3145736 | tf_op jit(solution)/shard_map/ppermute | solution.py:43
  25.2 23.9 %collective-permute-start.9 = (bf16[8,512,128]{2,1,0:T(8,128)(2,1)S(1)}, bf16[8,512,128]{2,1,0:T(8,128)(2,1)S(1)}, u32[]{:S(2)}, u32[]{:S(2)}) collective-permute-start(bf16[8,512,128]{2,1,0:T(8,128)(2,1)S(1)} %constant_dynamic-update-slice_fusion), channel_id=1, source_target_pairs={{0,3},{1,0},{2,1},{3,2},{4,7},{5,4},{6,5},{7,6},{8,11},{9,8},{10,9... | collective-permute-start | bytes 3145736 | tf_op jit(solution)/shard_map/ppermute | solution.py:43
  27.6 8.3 %collective-permute-start.5 = (bf16[2,512,128]{2,1,0:T(8,128)(2,1)S(1)}, bf16[2,512,128]{2,1,0:T(8,128)(2,1)S(1)}, u32[]{:S(2)}, u32[]{:S(2)}) collective-permute-start(bf16[2,512,128]{2,1,0:T(8,128)(2,1)S(1)} %pad_maximum_fusion.10.refs_0_.refs_4_.refs_5_), channel_id=1, source_target_pairs={{0,32},{1,33},{2,34},{3,35},{4,36},{5,37},{6,38},{7,39},{8,40},{9,... | collective-permute-start | bytes 786440 | tf_op jit(solution)/shard_map/ppermute | solution.py:43
  35.9 10.5 %collective-permute-start.6 = (bf16[2,512,128]{2,1,0:T(8,128)(2,1)S(1)}, bf16[2,512,128]{2,1,0:T(8,128)(2,1)S(1)}, u32[]{:S(2)}, u32[]{:S(2)}) collective-permute-start(bf16[2,512,128]{2,1,0:T(8,128)(2,1)S(1)} %pad_maximum_fusion.10.refs_0_.refs_4_.refs_5_), channel_id=1, source_target_pairs={{0,96},{1,97},{2,98},{3,99},{4,100},{5,101},{6,102},{7,103},{8,104... | collective-permute-start | bytes 786440 | tf_op jit(solution)/shard_map/ppermute | solution.py:43
  37.1 9.3 %collective-permute-start.7 = (bf16[2,512,128]{2,1,0:T(8,128)(2,1)S(1)}, bf16[2,512,128]{2,1,0:T(8,128)(2,1)S(1)}, u32[]{:S(2)}, u32[]{:S(2)}) collective-permute-start(bf16[2,512,128]{2,1,0:T(8,128)(2,1)S(1)} %pad_maximum_fusion.10.refs_0_.refs_4_.refs_5_), channel_id=1, source_target_pairs={{0,64},{1,65},{2,66},{3,67},{4,68},{5,69},{6,70},{7,71},{8,72},{9,... | collective-permute-start | bytes 786440 | tf_op jit(solution)/shard_map/ppermute | solution.py:43
  52.9 9.5 %collective-permute-start.13 = (bf16[2,512,128]{2,1,0:T(8,128)(2,1)S(1)}, bf16[2,512,128]{2,1,0:T(8,128)(2,1)S(1)}, u32[]{:S(2)}, u32[]{:S(2)}) collective-permute-start(bf16[2,512,128]{2,1,0:T(8,128)(2,1)S(1)} %get-tuple-element.46.refs_0_), channel_id=1, source_target_pairs={{0,4},{1,5},{2,6},{3,7},{4,8},{5,9},{6,10},{7,11},{8,12},{9,13},{1... | collective-permute-start | bytes 786440 | tf_op jit(solution)/shard_map/ppermute | solution.py:43
  53.9 8.4 %collective-permute-start.14 = (bf16[2,512,128]{2,1,0:T(8,128)(2,1)S(1)}, bf16[2,512,128]{2,1,0:T(8,128)(2,1)S(1)}, u32[]{:S(2)}, u32[]{:S(2)}) collective-permute-start(bf16[2,512,128]{2,1,0:T(8,128)(2,1)S(1)} %get-tuple-element.46.refs_0_), channel_id=1, source_target_pairs={{0,12},{1,13},{2,14},{3,15},{4,0},{5,1},{6,2},{7,3},{8,4},{9,5},{1... | collective-permute-start | bytes 786440 | tf_op jit(solution)/shard_map/ppermute | solution.py:43
  55.6 6.7 %collective-permute-start.15 = (bf16[2,512,128]{2,1,0:T(8,128)(2,1)S(1)}, bf16[2,512,128]{2,1,0:T(8,128)(2,1)S(1)}, u32[]{:S(2)}, u32[]{:S(2)}) collective-permute-start(bf16[2,512,128]{2,1,0:T(8,128)(2,1)S(1)} %get-tuple-element.46.refs_0_), channel_id=1, source_target_pairs={{0,8},{1,9},{2,10},{3,11},{4,12},{5,13},{6,14},{7,15},{8,0},{9,1},... | collective-permute-start | bytes 786440 | tf_op jit(solution)/shard_map/ppermute | solution.py:43
  55.8 3.8 %collective-permute-start.16 = (bf16[512,128]{1,0:T(8,128)(2,1)S(1)}, bf16[512,128]{1,0:T(8,128)(2,1)S(1)}, u32[]{:S(2)}, u32[]{:S(2)}) collective-permute-start(bf16[512,128]{1,0:T(8,128)(2,1)S(1)} %get-tuple-element.44), channel_id=1, source_target_pairs={{0,16},{1,17},{2,18},{3,19},{4,20},{5,21},{6,22},{7,23},{8,24},{9,... | collective-permute-start | bytes 393224 | tf_op jit(solution)/shard_map/ppermute | solution.py:43
  59.6 8.5 %collective-permute-start.17 = (bf16[2,512,128]{2,1,0:T(8,128)(2,1)S(1)}, bf16[2,512,128]{2,1,0:T(8,128)(2,1)S(1)}, u32[]{:S(2)}, u32[]{:S(2)}) collective-permute-start(bf16[2,512,128]{2,1,0:T(8,128)(2,1)S(1)} %get-tuple-element.46.refs_0_), channel_id=1, source_target_pairs={{0,1},{1,2},{2,3},{3,0},{4,5},{5,6},{6,7},{7,4},{8,9},{9,10},{10,1... | collective-permute-start | bytes 786440 | tf_op jit(solution)/shard_map/ppermute | solution.py:43
  60.8 7.4 %collective-permute-start.18 = (bf16[2,512,128]{2,1,0:T(8,128)(2,1)S(1)}, bf16[2,512,128]{2,1,0:T(8,128)(2,1)S(1)}, u32[]{:S(2)}, u32[]{:S(2)}) collective-permute-start(bf16[2,512,128]{2,1,0:T(8,128)(2,1)S(1)} %get-tuple-element.46.refs_0_), channel_id=1, source_target_pairs={{0,3},{1,0},{2,1},{3,2},{4,7},{5,4},{6,5},{7,6},{8,11},{9,8},{10,9... | collective-permute-start | bytes 786440 | tf_op jit(solution)/shard_map/ppermute | solution.py:43
  68.3 23.0 %collective-permute-start.22 = (bf16[7,512,128]{2,1,0:T(8,128)(2,1)S(1)}, bf16[7,512,128]{2,1,0:T(8,128)(2,1)S(1)}, u32[]{:S(2)}, u32[]{:S(2)}) collective-permute-start(bf16[7,512,128]{2,1,0:T(8,128)(2,1)S(1)} %get-tuple-element.76), channel_id=1, source_target_pairs={{0,1},{1,2},{2,3},{3,0},{4,5},{5,6},{6,7},{7,4},{8,9},{9,10},{10,1... | collective-permute-start | bytes 2752520 | tf_op jit(solution)/shard_map/ppermute | solution.py:43
  69.3 22.0 %collective-permute-start.23 = (bf16[7,512,128]{2,1,0:T(8,128)(2,1)S(1)}, bf16[7,512,128]{2,1,0:T(8,128)(2,1)S(1)}, u32[]{:S(2)}, u32[]{:S(2)}) collective-permute-start(bf16[7,512,128]{2,1,0:T(8,128)(2,1)S(1)} %get-tuple-element.75), channel_id=1, source_target_pairs={{0,3},{1,0},{2,1},{3,2},{4,7},{5,4},{6,5},{7,6},{8,11},{9,8},{10,9... | collective-permute-start | bytes 2752520 | tf_op jit(solution)/shard_map/ppermute | solution.py:43
  71.1 20.2 %collective-permute-start.24 = (bf16[6,512,128]{2,1,0:T(8,128)(2,1)S(1)}, bf16[6,512,128]{2,1,0:T(8,128)(2,1)S(1)}, u32[]{:S(2)}, u32[]{:S(2)}) collective-permute-start(bf16[6,512,128]{2,1,0:T(8,128)(2,1)S(1)} %pad_maximum_fusion.7.token_ref), channel_id=1, source_target_pairs={{0,2},{1,3},{2,0},{3,1},{4,6},{5,7},{6,4},{7,5},{8,10},{9,11},{10,... | collective-permute-start | bytes 2359304 | tf_op jit(solution)/shard_map/ppermute | solution.py:43
  71.8 9.6 %collective-permute-start.19 = (bf16[2,512,128]{2,1,0:T(8,128)(2,1)S(1)}, bf16[2,512,128]{2,1,0:T(8,128)(2,1)S(1)}, u32[]{:S(2)}, u32[]{:S(2)}) collective-permute-start(bf16[2,512,128]{2,1,0:T(8,128)(2,1)S(1)} %get-tuple-element.46.refs_0_), channel_id=1, source_target_pairs={{0,32},{1,33},{2,34},{3,35},{4,36},{5,37},{6,38},{7,39},{8,40},{9,... | collective-permute-start | bytes 786440 | tf_op jit(solution)/shard_map/ppermute | solution.py:43
  73.4 12.4 %collective-permute-start.20 = (bf16[2,512,128]{2,1,0:T(8,128)(2,1)S(1)}, bf16[2,512,128]{2,1,0:T(8,128)(2,1)S(1)}, u32[]{:S(2)}, u32[]{:S(2)}) collective-permute-start(bf16[2,512,128]{2,1,0:T(8,128)(2,1)S(1)} %get-tuple-element.46.refs_0_), channel_id=1, source_target_pairs={{0,96},{1,97},{2,98},{3,99},{4,100},{5,101},{6,102},{7,103},{8,104... | collective-permute-start | bytes 786440 | tf_op jit(solution)/shard_map/ppermute | solution.py:43
  81.3 7.8 %collective-permute-start.21 = (bf16[2,512,128]{2,1,0:T(8,128)(2,1)S(1)}, bf16[2,512,128]{2,1,0:T(8,128)(2,1)S(1)}, u32[]{:S(2)}, u32[]{:S(2)}) collective-permute-start(bf16[2,512,128]{2,1,0:T(8,128)(2,1)S(1)} %get-tuple-element.46.refs_0_), channel_id=1, source_target_pairs={{0,64},{1,65},{2,66},{3,67},{4,68},{5,69},{6,70},{7,71},{8,72},{9,... | collective-permute-start | bytes 786440 | tf_op jit(solution)/shard_map/ppermute | solution.py:43
  95.0 9.8 %collective-permute-start.25 = (bf16[2,512,128]{2,1,0:T(8,128)(2,1)S(1)}, bf16[2,512,128]{2,1,0:T(8,128)(2,1)S(1)}, u32[]{:S(2)}, u32[]{:S(2)}) collective-permute-start(bf16[2,512,128]{2,1,0:T(8,128)(2,1)S(1)} %get-tuple-element.51.refs_0_), channel_id=1, source_target_pairs={{0,4},{1,5},{2,6},{3,7},{4,8},{5,9},{6,10},{7,11},{8,12},{9,13},{1... | collective-permute-start | bytes 786440 | tf_op jit(solution)/shard_map/ppermute | solution.py:43
  96.2 8.7 %collective-permute-start.26 = (bf16[2,512,128]{2,1,0:T(8,128)(2,1)S(1)}, bf16[2,512,128]{2,1,0:T(8,128)(2,1)S(1)}, u32[]{:S(2)}, u32[]{:S(2)}) collective-permute-start(bf16[2,512,128]{2,1,0:T(8,128)(2,1)S(1)} %get-tuple-element.51.refs_0_), channel_id=1, source_target_pairs={{0,12},{1,13},{2,14},{3,15},{4,0},{5,1},{6,2},{7,3},{8,4},{9,5},{1... | collective-permute-start | bytes 786440 | tf_op jit(solution)/shard_map/ppermute | solution.py:43
  97.8 7.8 %collective-permute-start.27 = (bf16[2,512,128]{2,1,0:T(8,128)(2,1)S(1)}, bf16[2,512,128]{2,1,0:T(8,128)(2,1)S(1)}, u32[]{:S(2)}, u32[]{:S(2)}) collective-permute-start(bf16[2,512,128]{2,1,0:T(8,128)(2,1)S(1)} %get-tuple-element.51.refs_0_), channel_id=1, source_target_pairs={{0,8},{1,9},{2,10},{3,11},{4,12},{5,13},{6,14},{7,15},{8,0},{9,1},... | collective-permute-start | bytes 786440 | tf_op jit(solution)/shard_map/ppermute | solution.py:43
  98.8 3.4 %collective-permute-start.28 = (bf16[512,128]{1,0:T(8,128)(2,1)S(1)}, bf16[512,128]{1,0:T(8,128)(2,1)S(1)}, u32[]{:S(2)}, u32[]{:S(2)}) collective-permute-start(bf16[512,128]{1,0:T(8,128)(2,1)S(1)} %get-tuple-element.49), channel_id=1, source_target_pairs={{0,16},{1,17},{2,18},{3,19},{4,20},{5,21},{6,22},{7,23},{8,24},{9,... | collective-permute-start | bytes 393224 | tf_op jit(solution)/shard_map/ppermute | solution.py:43
  102.2 7.5 %collective-permute-start.29 = (bf16[2,512,128]{2,1,0:T(8,128)(2,1)S(1)}, bf16[2,512,128]{2,1,0:T(8,128)(2,1)S(1)}, u32[]{:S(2)}, u32[]{:S(2)}) collective-permute-start(bf16[2,512,128]{2,1,0:T(8,128)(2,1)S(1)} %get-tuple-element.51.refs_0_), channel_id=1, source_target_pairs={{0,1},{1,2},{2,3},{3,0},{4,5},{5,6},{6,7},{7,4},{8,9},{9,10},{10,1... | collective-permute-start | bytes 786440 | tf_op jit(solution)/shard_map/ppermute | solution.py:43
  102.2 7.6 %collective-permute-start.30 = (bf16[2,512,128]{2,1,0:T(8,128)(2,1)S(1)}, bf16[2,512,128]{2,1,0:T(8,128)(2,1)S(1)}, u32[]{:S(2)}, u32[]{:S(2)}) collective-permute-start(bf16[2,512,128]{2,1,0:T(8,128)(2,1)S(1)} %get-tuple-element.51.refs_0_), channel_id=1, source_target_pairs={{0,3},{1,0},{2,1},{3,2},{4,7},{5,4},{6,5},{7,6},{8,11},{9,8},{10,9... | collective-permute-start | bytes 786440 | tf_op jit(solution)/shard_map/ppermute | solution.py:43
  109.9 23.0 %collective-permute-start.34 = (bf16[7,512,128]{2,1,0:T(8,128)(2,1)S(1)}, bf16[7,512,128]{2,1,0:T(8,128)(2,1)S(1)}, u32[]{:S(2)}, u32[]{:S(2)}) collective-permute-start(bf16[7,512,128]{2,1,0:T(8,128)(2,1)S(1)} %get-tuple-element.74), channel_id=1, source_target_pairs={{0,1},{1,2},{2,3},{3,0},{4,5},{5,6},{6,7},{7,4},{8,9},{9,10},{10,1... | collective-permute-start | bytes 2752520 | tf_op jit(solution)/shard_map/ppermute | solution.py:43
  110.6 22.3 %collective-permute-start.35 = (bf16[7,512,128]{2,1,0:T(8,128)(2,1)S(1)}, bf16[7,512,128]{2,1,0:T(8,128)(2,1)S(1)}, u32[]{:S(2)}, u32[]{:S(2)}) collective-permute-start(bf16[7,512,128]{2,1,0:T(8,128)(2,1)S(1)} %get-tuple-element.73), channel_id=1, source_target_pairs={{0,3},{1,0},{2,1},{3,2},{4,7},{5,4},{6,5},{7,6},{8,11},{9,8},{10,9... | collective-permute-start | bytes 2752520 | tf_op jit(solution)/shard_map/ppermute | solution.py:43
  112.6 20.2 %collective-permute-start.36 = (bf16[6,512,128]{2,1,0:T(8,128)(2,1)S(1)}, bf16[6,512,128]{2,1,0:T(8,128)(2,1)S(1)}, u32[]{:S(2)}, u32[]{:S(2)}) collective-permute-start(bf16[6,512,128]{2,1,0:T(8,128)(2,1)S(1)} %pad_maximum_fusion.8.token_ref), channel_id=1, source_target_pairs={{0,2},{1,3},{2,0},{3,1},{4,6},{5,7},{6,4},{7,5},{8,10},{9,11},{10,... | collective-permute-start | bytes 2359304 | tf_op jit(solution)/shard_map/ppermute | solution.py:43
  113.4 8.8 %collective-permute-start.31 = (bf16[2,512,128]{2,1,0:T(8,128)(2,1)S(1)}, bf16[2,512,128]{2,1,0:T(8,128)(2,1)S(1)}, u32[]{:S(2)}, u32[]{:S(2)}) collective-permute-start(bf16[2,512,128]{2,1,0:T(8,128)(2,1)S(1)} %get-tuple-element.51.refs_0_), channel_id=1, source_target_pairs={{0,32},{1,33},{2,34},{3,35},{4,36},{5,37},{6,38},{7,39},{8,40},{9,... | collective-permute-start | bytes 786440 | tf_op jit(solution)/shard_map/ppermute | solution.py:43
  115.0 11.6 %collective-permute-start.32 = (bf16[2,512,128]{2,1,0:T(8,128)(2,1)S(1)}, bf16[2,512,128]{2,1,0:T(8,128)(2,1)S(1)}, u32[]{:S(2)}, u32[]{:S(2)}) collective-permute-start(bf16[2,512,128]{2,1,0:T(8,128)(2,1)S(1)} %get-tuple-element.51.refs_0_), channel_id=1, source_target_pairs={{0,96},{1,97},{2,98},{3,99},{4,100},{5,101},{6,102},{7,103},{8,104... | collective-permute-start | bytes 786440 | tf_op jit(solution)/shard_map/ppermute | solution.py:43
  122.1 7.0 %collective-permute-start.33 = (bf16[2,512,128]{2,1,0:T(8,128)(2,1)S(1)}, bf16[2,512,128]{2,1,0:T(8,128)(2,1)S(1)}, u32[]{:S(2)}, u32[]{:S(2)}) collective-permute-start(bf16[2,512,128]{2,1,0:T(8,128)(2,1)S(1)} %get-tuple-element.51.refs_0_), channel_id=1, source_target_pairs={{0,64},{1,65},{2,66},{3,67},{4,68},{5,69},{6,70},{7,71},{8,72},{9,... | collective-permute-start | bytes 786440 | tf_op jit(solution)/shard_map/ppermute | solution.py:43
  136.6 9.4 %collective-permute-start.38 = (bf16[2,512,128]{2,1,0:T(8,128)(2,1)S(1)}, bf16[2,512,128]{2,1,0:T(8,128)(2,1)S(1)}, u32[]{:S(2)}, u32[]{:S(2)}) collective-permute-start(bf16[2,512,128]{2,1,0:T(8,128)(2,1)S(1)} %get-tuple-element.59.refs_0_), channel_id=1, source_target_pairs={{0,4},{1,5},{2,6},{3,7},{4,8},{5,9},{6,10},{7,11},{8,12},{9,13},{1... | collective-permute-start | bytes 786440 | tf_op jit(solution)/shard_map/ppermute | solution.py:43
  137.6 8.5 %collective-permute-start.39 = (bf16[2,512,128]{2,1,0:T(8,128)(2,1)S(1)}, bf16[2,512,128]{2,1,0:T(8,128)(2,1)S(1)}, u32[]{:S(2)}, u32[]{:S(2)}) collective-permute-start(bf16[2,512,128]{2,1,0:T(8,128)(2,1)S(1)} %get-tuple-element.59.refs_0_), channel_id=1, source_target_pairs={{0,12},{1,13},{2,14},{3,15},{4,0},{5,1},{6,2},{7,3},{8,4},{9,5},{1... | collective-permute-start | bytes 786440 | tf_op jit(solution)/shard_map/ppermute | solution.py:43
  139.4 7.4 %collective-permute-start.40 = (bf16[2,512,128]{2,1,0:T(8,128)(2,1)S(1)}, bf16[2,512,128]{2,1,0:T(8,128)(2,1)S(1)}, u32[]{:S(2)}, u32[]{:S(2)}) collective-permute-start(bf16[2,512,128]{2,1,0:T(8,128)(2,1)S(1)} %get-tuple-element.59.refs_0_), channel_id=1, source_target_pairs={{0,8},{1,9},{2,10},{3,11},{4,12},{5,13},{6,14},{7,15},{8,0},{9,1},... | collective-permute-start | bytes 786440 | tf_op jit(solution)/shard_map/ppermute | solution.py:43
  139.9 3.5 %collective-permute-start.37 = (bf16[512,128]{1,0:T(8,128)(2,1)S(1)}, bf16[512,128]{1,0:T(8,128)(2,1)S(1)}, u32[]{:S(2)}, u32[]{:S(2)}) collective-permute-start(bf16[512,128]{1,0:T(8,128)(2,1)S(1)} %get-tuple-element.56), channel_id=1, source_target_pairs={{0,16},{1,17},{2,18},{3,19},{4,20},{5,21},{6,22},{7,23},{8,24},{9,... | collective-permute-start | bytes 393224 | tf_op jit(solution)/shard_map/ppermute | solution.py:43
  143.4 8.5 %collective-permute-start.41 = (bf16[2,512,128]{2,1,0:T(8,128)(2,1)S(1)}, bf16[2,512,128]{2,1,0:T(8,128)(2,1)S(1)}, u32[]{:S(2)}, u32[]{:S(2)}) collective-permute-start(bf16[2,512,128]{2,1,0:T(8,128)(2,1)S(1)} %get-tuple-element.59.refs_0_), channel_id=1, source_target_pairs={{0,1},{1,2},{2,3},{3,0},{4,5},{5,6},{6,7},{7,4},{8,9},{9,10},{10,1... | collective-permute-start | bytes 786440 | tf_op jit(solution)/shard_map/ppermute | solution.py:43
  143.4 8.4 %collective-permute-start.42 = (bf16[2,512,128]{2,1,0:T(8,128)(2,1)S(1)}, bf16[2,512,128]{2,1,0:T(8,128)(2,1)S(1)}, u32[]{:S(2)}, u32[]{:S(2)}) collective-permute-start(bf16[2,512,128]{2,1,0:T(8,128)(2,1)S(1)} %get-tuple-element.59.refs_0_), channel_id=1, source_target_pairs={{0,3},{1,0},{2,1},{3,2},{4,7},{5,4},{6,5},{7,6},{8,11},{9,8},{10,9... | collective-permute-start | bytes 786440 | tf_op jit(solution)/shard_map/ppermute | solution.py:43
  152.0 23.0 %collective-permute-start.46 = (bf16[7,512,128]{2,1,0:T(8,128)(2,1)S(1)}, bf16[7,512,128]{2,1,0:T(8,128)(2,1)S(1)}, u32[]{:S(2)}, u32[]{:S(2)}) collective-permute-start(bf16[7,512,128]{2,1,0:T(8,128)(2,1)S(1)} %get-tuple-element.72), channel_id=1, source_target_pairs={{0,1},{1,2},{2,3},{3,0},{4,5},{5,6},{6,7},{7,4},{8,9},{9,10},{10,1... | collective-permute-start | bytes 2752520 | tf_op jit(solution)/shard_map/ppermute | solution.py:43
  152.1 22.9 %collective-permute-start.47 = (bf16[7,512,128]{2,1,0:T(8,128)(2,1)S(1)}, bf16[7,512,128]{2,1,0:T(8,128)(2,1)S(1)}, u32[]{:S(2)}, u32[]{:S(2)}) collective-permute-start(bf16[7,512,128]{2,1,0:T(8,128)(2,1)S(1)} %get-tuple-element.71), channel_id=1, source_target_pairs={{0,3},{1,0},{2,1},{3,2},{4,7},{5,4},{6,5},{7,6},{8,11},{9,8},{10,9... | collective-permute-start | bytes 2752520 | tf_op jit(solution)/shard_map/ppermute | solution.py:43
  154.8 20.2 %collective-permute-start.48 = (bf16[6,512,128]{2,1,0:T(8,128)(2,1)S(1)}, bf16[6,512,128]{2,1,0:T(8,128)(2,1)S(1)}, u32[]{:S(2)}, u32[]{:S(2)}) collective-permute-start(bf16[6,512,128]{2,1,0:T(8,128)(2,1)S(1)} %pad_maximum_fusion.9.token_ref), channel_id=1, source_target_pairs={{0,2},{1,3},{2,0},{3,1},{4,6},{5,7},{6,4},{7,5},{8,10},{9,11},{10,... | collective-permute-start | bytes 2359304 | tf_op jit(solution)/shard_map/ppermute | solution.py:43
  155.5 9.7 %collective-permute-start.43 = (bf16[2,512,128]{2,1,0:T(8,128)(2,1)S(1)}, bf16[2,512,128]{2,1,0:T(8,128)(2,1)S(1)}, u32[]{:S(2)}, u32[]{:S(2)}) collective-permute-start(bf16[2,512,128]{2,1,0:T(8,128)(2,1)S(1)} %get-tuple-element.59.refs_0_), channel_id=1, source_target_pairs={{0,32},{1,33},{2,34},{3,35},{4,36},{5,37},{6,38},{7,39},{8,40},{9,... | collective-permute-start | bytes 786440 | tf_op jit(solution)/shard_map/ppermute | solution.py:43
  157.2 12.7 %collective-permute-start.44 = (bf16[2,512,128]{2,1,0:T(8,128)(2,1)S(1)}, bf16[2,512,128]{2,1,0:T(8,128)(2,1)S(1)}, u32[]{:S(2)}, u32[]{:S(2)}) collective-permute-start(bf16[2,512,128]{2,1,0:T(8,128)(2,1)S(1)} %get-tuple-element.59.refs_0_), channel_id=1, source_target_pairs={{0,96},{1,97},{2,98},{3,99},{4,100},{5,101},{6,102},{7,103},{8,104... | collective-permute-start | bytes 786440 | tf_op jit(solution)/shard_map/ppermute | solution.py:43
  165.2 8.0 %collective-permute-start.45 = (bf16[2,512,128]{2,1,0:T(8,128)(2,1)S(1)}, bf16[2,512,128]{2,1,0:T(8,128)(2,1)S(1)}, u32[]{:S(2)}, u32[]{:S(2)}) collective-permute-start(bf16[2,512,128]{2,1,0:T(8,128)(2,1)S(1)} %get-tuple-element.59.refs_0_), channel_id=1, source_target_pairs={{0,64},{1,65},{2,66},{3,67},{4,68},{5,69},{6,70},{7,71},{8,72},{9,... | collective-permute-start | bytes 786440 | tf_op jit(solution)/shard_map/ppermute | solution.py:43
  (8 other events, 52.0 us)
